TPU v7x, 32 devices: a whole 2x2x4 slice. The times are simulated.
32 devices in a mesh: fsdp: 8 (over z, y), grp: 4 (over x, core).
Axes of the slice: x: 2, y: 2, z: 4, core: 2. Of those that a mesh axis runs over, the one named last changes fastest.
Arguments:
- grads: bfloat16 [4, 8, 128, 8192], P('grp', 'fsdp'), may hold values from -6 to 6
- master: float32 [128, 8192], P('fsdp', 'grp'), may hold values from -0.0625 to 0.0625
- moment_one: float32 [128, 8192], P('fsdp', 'grp'), may hold values from -0.2 to 0.2
- moment_two: float32 [128, 8192], P('fsdp', 'grp'), may hold values from 0.0001 to 0.004
Outputs:
- new_master: float32 [128, 8192], P('fsdp', 'grp')
- new_first: float32 [128, 8192], P('fsdp', 'grp')
- new_second: float32 [128, 8192], P('fsdp', 'grp')
- weights: bfloat16 [128, 8192], P('fsdp')
- copy_master: float32 [128, 8192], P('fsdp', 'grp')
- copy_first: float32 [128, 8192], P('fsdp', 'grp')
- copy_second: float32 [128, 8192], P('fsdp', 'grp')
All inputs are finite; a program needn't handle non-finite values.
Results may differ from a plain program's by a relative error of at most 0.009.
Values may be sent and summed in bfloat16 or wider, within the bound.
No kernel may reach another device: no remote copies, remote signals or barrier semaphores. Data moves between devices by JAX's collectives and lax.ppermute only.
A program may use at most 64 MiB of HBM per device.

v0:
```python
import jax
import jax.numpy as jnp
from jax import lax
from jax.sharding import PartitionSpec as P

beta_one = 0.9
beta_two = 0.95
learn_rate = 0.01
decay_rate = 0.1
epsilon = 1e-08
step_count = 100


def passed_along(shard, axis, by):
    length = lax.axis_size(axis)
    return lax.ppermute(shard, axis, [(i, (i + by) % length) for i in range(length)])


def shards(grads, master, moment_one, moment_two):
    summand = grads[0, 0].astype(jnp.float32)
    column_share = lax.psum_scatter(
        summand.astype(jnp.bfloat16), "grp", scatter_dimension=1, tiled=True
    ).astype(jnp.float32)
    owned_grad = lax.psum_scatter(column_share, "fsdp", scatter_dimension=0, tiled=True)
    gradient = owned_grad / (lax.axis_size("fsdp") * lax.axis_size("grp"))
    new_first = beta_one * moment_one + (1.0 - beta_one) * gradient
    new_second = beta_two * moment_two + (1.0 - beta_two) * gradient * gradient
    first_hat = new_first / (1.0 - beta_one**step_count)
    second_hat = new_second / (1.0 - beta_two**step_count)
    new_master = master - learn_rate * (
        first_hat / (jnp.sqrt(second_hat) + epsilon) + decay_rate * master
    )
    snapshot = passed_along((new_master, new_first, new_second), "grp", 1)
    weights = lax.all_gather(new_master.astype(jnp.bfloat16), "grp", axis=1, tiled=True)
    return (new_master, new_first, new_second, weights, snapshot[0], snapshot[1], snapshot[2])


def solution(mesh):
    return jax.shard_map(
        shards,
        mesh=mesh,
        in_specs=(
            P("grp", "fsdp", None, None),
            P("fsdp", "grp"),
            P("fsdp", "grp"),
            P("fsdp", "grp"),
        ),
        out_specs=(
            P("fsdp", "grp"),
            P("fsdp", "grp"),
            P("fsdp", "grp"),
            P("fsdp", None),
            P("fsdp", "grp"),
            P("fsdp", "grp"),
            P("fsdp", "grp"),
        ),
        check_vma=False,
    )
```

profile of v0, /device:TPU:0, one launch (start us, length us, event | category | flops | bytes accessed | tf_op | source)
XLA Modules:
  0.0 131.8 jit_solution(14323098608287559717)
XLA Ops:
  7.2 0.0 reduce-scatter.3.cloned.1.call-start
  7.2 0.0 copy-start
  7.2 0.0 copy-start.1
  7.2 0.0 copy-start.2
  7.2 0.7 reduce-scatter.3.cloned.1.call-update
  7.9 0.0 reduce-scatter.5.cloned.1.call-start
  7.9 36.7 %reduce-scatter.3.cloned.1.call-done = bf16[128,2048]{1,0:T(8,128)(2,1)} async-done(((bf16[128,8192]{1,0:T(8,128)(2,1)}), bf16[128,2048]{1,0:T(8,128)(2,1)}) %reduce-scatter.3.cloned.1.call-update) | async-done | bytes 524304 | tf_op jit(solution)/shard_map/reduce_scatter | solution.py:21
  44.7 2.1 %convert_element_type.8 = f32[128,2048]{1,0:T(8,128)} convert(bf16[128,2048]{1,0:T(8,128)(2,1)} %reduce-scatter.3.cloned.1.call-done) | non-fusion elementwise | flops 262144 | bytes 1572864 | tf_op jit(solution)/shard_map/convert_element_type | solution.py:23
  46.8 0.0 reduce-scatter.5.cloned.1.call-update
  46.8 65.2 %reduce-scatter.5.cloned.1.call-done = f32[16,2048]{1,0:T(8,128)} async-done(((f32[128,2048]{1,0:T(8,128)}), f32[16,2048]{1,0:T(8,128)}) %reduce-scatter.5.cloned.1.call-update) | async-done | bytes 131088 | tf_op jit(solution)/shard_map/reduce_scatter | solution.py:24
  112.0 0.0 copy-done
  112.0 0.0 copy-done.1
  112.0 0.0 copy-done.2
  112.0 1.0 fusion
  113.1 0.0 copy-start.3
  113.1 0.0 copy-start.4
  113.1 0.0 copy-start.5
  113.1 0.1 collective-permute-start
  113.2 1.6 %collective-permute-start.1 = (f32[16,2048]{1,0:T(8,128)S(1)}, f32[16,2048]{1,0:T(8,128)S(1)}, u32[]{:S(2)}, u32[]{:S(2)}) collective-permute-start(f32[16,2048]{1,0:T(8,128)S(1)} %get-tuple-element.19), channel_id=1, source_target_pairs={{0,1},{1,2},{2,3},{3,0},{4,5},{5,6},{6,7},{7,4},{8,9},{9,10},{10,1... | collective-permute-start | bytes 393224 | tf_op jit(solution)/shard_map/ppermute | solution.py:16
  114.7 0.1 collective-permute-start.2
  114.8 7.4 %all_gather.3 = bf16[16,8192]{1,0:T(8,128)(2,1)S(1)} all-gather(bf16[16,2048]{1,0:T(8,128)(2,1)S(1)} %get-tuple-element.7), channel_id=1, replica_groups=mesh['fsdp'=8,'grp'=4] {'grp'}, dimensions={1}, use_global_device_ids=true | all-gather | bytes 327680 | tf_op jit(solution)/shard_map/all_gather | solution.py:34
  122.2 0.0 collective-permute-done
  122.3 0.0 collective-permute-done.1
  122.3 0.0 collective-permute-done.2
  122.3 0.7 copy.15
  123.0 0.7 copy.16
  123.6 0.7 copy.17
  124.3 0.7 copy.18
  124.9 0.0 copy-done.3
  124.9 0.0 copy-done.4
  124.9 0.0 copy-done.5
Async XLA Ops:
  7.2 37.5 %reduce-scatter.3.cloned.1.call-start = ((), (), s32[]{:S(2)}) async-start(), calls=%async_computation.2 | async-start | bytes 2621440 | tf_op jit(solution)/shard_map/reduce_scatter | solution.py:21
  7.2 104.8 %copy-start = (f32[16,2048]{1,0:T(8,128)S(1)}, f32[16,2048]{1,0:T(8,128)}, u32[]{:S(2)}) copy-start(f32[16,2048]{1,0:T(8,128)} %param.5) | copy-start | bytes 393220
  7.2 104.8 %copy-start.1 = (f32[16,2048]{1,0:T(8,128)S(1)}, f32[16,2048]{1,0:T(8,128)}, u32[]{:S(2)}) copy-start(f32[16,2048]{1,0:T(8,128)} %param.6) | copy-start | bytes 393220
  7.2 104.8 %copy-start.2 = (f32[16,2048]{1,0:T(8,128)S(1)}, f32[16,2048]{1,0:T(8,128)}, u32[]{:S(2)}) copy-start(f32[16,2048]{1,0:T(8,128)} %param.7) | copy-start | bytes 393220
  7.9 104.1 %reduce-scatter.5.cloned.1.call-start = ((), (), s32[]{:S(2)}) async-start(), calls=%async_computation.3 | async-start | bytes 1179648 | tf_op jit(solution)/shard_map/reduce_scatter | solution.py:24
  113.1 11.9 %copy-start.3 = (f32[16,2048]{1,0:T(8,128)}, f32[16,2048]{1,0:T(8,128)S(1)}, u32[]{:S(2)}) copy-start(f32[16,2048]{1,0:T(8,128)S(1)} %get-tuple-element.18) | copy-start | bytes 393220
  113.1 11.9 %copy-start.4 = (f32[16,2048]{1,0:T(8,128)}, f32[16,2048]{1,0:T(8,128)S(1)}, u32[]{:S(2)}) copy-start(f32[16,2048]{1,0:T(8,128)S(1)} %get-tuple-element.19) | copy-start | bytes 393220
  113.1 11.9 %copy-start.5 = (f32[16,2048]{1,0:T(8,128)}, f32[16,2048]{1,0:T(8,128)S(1)}, u32[]{:S(2)}) copy-start(f32[16,2048]{1,0:T(8,128)S(1)} %get-tuple-element.20) | copy-start | bytes 393220
  113.1 9.2 %collective-permute-start = (f32[16,2048]{1,0:T(8,128)S(1)}, f32[16,2048]{1,0:T(8,128)S(1)}, u32[]{:S(2)}, u32[]{:S(2)}) collective-permute-start(f32[16,2048]{1,0:T(8,128)S(1)} %get-tuple-element.18), channel_id=1, source_target_pairs={{0,1},{1,2},{2,3},{3,0},{4,5},{5,6},{6,7},{7,4},{8,9},{9,10},{10,1... | collective-permute-start | bytes 393224 | tf_op jit(solution)/shard_map/ppermute | solution.py:16
  113.2 9.1 %collective-permute-start.1 = (f32[16,2048]{1,0:T(8,128)S(1)}, f32[16,2048]{1,0:T(8,128)S(1)}, u32[]{:S(2)}, u32[]{:S(2)}) collective-permute-start(f32[16,2048]{1,0:T(8,128)S(1)} %get-tuple-element.19), channel_id=1, source_target_pairs={{0,1},{1,2},{2,3},{3,0},{4,5},{5,6},{6,7},{7,4},{8,9},{9,10},{10,1... | collective-permute-start | bytes 393224 | tf_op jit(solution)/shard_map/ppermute | solution.py:16
  114.7 7.5 %collective-permute-start.2 = (f32[16,2048]{1,0:T(8,128)S(1)}, f32[16,2048]{1,0:T(8,128)S(1)}, u32[]{:S(2)}, u32[]{:S(2)}) collective-permute-start(f32[16,2048]{1,0:T(8,128)S(1)} %get-tuple-element.20), channel_id=1, source_target_pairs={{0,1},{1,2},{2,3},{3,0},{4,5},{5,6},{6,7},{7,4},{8,9},{9,10},{10,1... | collective-permute-start | bytes 393224 | tf_op jit(solution)/shard_map/ppermute | solution.py:16
Sparse Core Ops, SparseCore 0:
  10.5 34.1 reduce-scatter.2
  48.5 63.4 reduce-scatter.4
where the time goes:
time: 132 us
  waiting for transfers between devices  103 us (78%)
  between operations  14.1 us (11%)
  blocking collectives  7.44 us (6%)
  other arithmetic  3.15 us (2%)
  local copies, waits for them, and re-layouts  2.7 us (2%)
  starting transfers between devices  1.78 us (1%)
    reduce_scatter x1, waiting for transfers between devices, shards(): lax.psum_scatter(column_share, 'fsdp', scatter_dimension=0, tiled=True)  65.2 us
    reduce_scatter x1, waiting for transfers between devices, shards(): lax.psum_scatter(summand.astype(jnp.bfloat16), 'grp', scatter_dimension=1...  36.7 us
    all_gather x1, blocking collectives, shards(): lax.all_gather(new_master.astype(jnp.bfloat16), 'grp', axis=1, tiled=True)  7.44 us
    unnamed x16, local copies, waits for them, and re-layouts  2.7 us
  transfers between devices with their start and end apart: 5, of which 2 were waited for; matrix products, arithmetic and copies ran while one was open for 0% of the time, Pallas kernels for 0%

commit v1 on v0

v1 whole, which is shorter than its diff:
```python
import jax
import jax.numpy as jnp
from jax import lax
from jax.sharding import PartitionSpec as P

beta_one = 0.9
beta_two = 0.95
learn_rate = 0.01
decay_rate = 0.1
epsilon = 1e-08
step_count = 100
F32 = jnp.float32
BF16 = jnp.bfloat16


def swap(x, axis, mask):
    n = lax.axis_size(axis)
    return lax.ppermute(x, axis, [(i, i ^ mask) for i in range(n)])


def pick(t, index, dim):
    return lax.dynamic_index_in_dim(t, index, dim, keepdims=False)


def halve(t, dims, step):
    axis, bit = step
    mine = (lax.axis_index(axis) >> bit) & 1
    dim = dims.index(step)
    got = swap(pick(t, 1 - mine, dim).astype(BF16), axis, 1 << bit)
    kept = pick(t, mine, dim).astype(F32) + got.astype(F32)
    return kept, dims[:dim] + dims[dim + 1 :]


def shards(grads, master, moment_one, moment_two):
    g = grads[0, 0]
    ng, nf = lax.axis_size("grp"), lax.axis_size("fsdp")
    me_g, me_f = lax.axis_index("grp"), lax.axis_index("fsdp")
    rows, cols = g.shape[0] // nf, g.shape[1] // ng
    g_steps = [("grp", b) for b in range(1, ng.bit_length() - 1)]
    f_steps = [("fsdp", b) for b in range(nf.bit_length() - 1)]
    dims0 = g_steps[::-1] + f_steps[::-1]
    core = me_g & 1
    g_core = g
    portions = []
    start = 0
    cuts = [('gf', 8), ('fg', 8)]
    for order, share in cuts:
        width = cols * share // 16
        sides = []
        for side in (1 - core, core):
            part = [lax.dynamic_slice(g, (0, (2 * k + side) * cols + start), (g.shape[0], width)) for k in range(ng // 2)]
            sides.append(jnp.stack(part).reshape((2,) * len(dims0) + (rows, width)))
        start += width
        portions.append([sides[0], sides[1], order, dims0])
    for p in portions:
        p[0] = swap(p[0], "grp", 1)
    state = []
    for got, own, order, dims in portions:
        t = own.astype(F32) + got.astype(F32)
        steps = {"gf": g_steps + f_steps, "fg": f_steps + g_steps, "yxz": f_steps[:1] + g_steps + f_steps[1:], "zxy": f_steps[1:] + g_steps + f_steps[:1], "zyx": f_steps[1:] + f_steps[:1] + g_steps}[order]
        state.append((t, dims, steps))
    for k in range(len(dims0)):
        state = [halve(t, dims, steps[k]) + (steps,) for t, dims, steps in state]
    gradient = jnp.concatenate([t for t, _, _ in state], 1) / (ng * nf)
    new_first = beta_one * moment_one + (1.0 - beta_one) * gradient
    new_second = beta_two * moment_two + (1.0 - beta_two) * gradient * gradient
    first_hat = new_first / (1.0 - beta_one**step_count)
    second_hat = new_second / (1.0 - beta_two**step_count)
    new_master = master - learn_rate * (
        first_hat / (jnp.sqrt(second_hat) + epsilon) + decay_rate * master
    )
    w = new_master.astype(BF16)

    pack = jnp.stack([w, new_first.astype(BF16), new_second.astype(BF16)])
    weights = jnp.zeros((rows, cols * ng), BF16)
    weights = lax.dynamic_update_slice(weights, w, (0, me_g * cols))
    got = {}
    for k in range(1, ng):
        got[k] = lax.ppermute(pack if k == 1 else w, "grp", [(i, (i + k) % ng) for i in range(ng)])
    copy_master, copy_first, copy_second = got[1].astype(F32)
    for k in range(1, ng):
        weights = lax.dynamic_update_slice(weights, got[k][0] if k == 1 else got[k], (0, ((me_g + ng - k) % ng) * cols))

    return (new_master, new_first, new_second, weights, copy_master, copy_first, copy_second)


def solution(mesh):
    return jax.shard_map(
        shards,
        mesh=mesh,
        in_specs=(P("grp", "fsdp", None, None), P("fsdp", "grp"), P("fsdp", "grp"), P("fsdp", "grp")),
        out_specs=(P("fsdp", "grp"), P("fsdp", "grp"), P("fsdp", "grp"), P("fsdp", None), P("fsdp", "grp"), P("fsdp", "grp"), P("fsdp", "grp")),
        check_vma=False,
    )
```

time: 132 us -> 40.7 us (0.31)
  waiting for transfers between devices: 103 us -> 14.3 us
  starting transfers between devices: 1.78 us -> 20.2 us
  between operations: 14.1 us -> 0.99 us
  blocking collectives: 7.44 us -> 0 us
  other arithmetic: 3.15 us -> 1.52 us
    reduce_scatter x2 -> x0, waiting for transfers between devices: 102 us -> none  [the longest x1 65.2 us: shards(): lax.psum_scatter(column_share, 'fsdp', scatter_dimension=0, tiled=True)]
    ppermute x3 -> x13, starting transfers between devices: 1.7 us -> 20.2 us  [the longest x10 17.1 us: swap(): return lax.ppermute(x, axis, [(i, i ^ mask) for i in range(n)])]
    ppermute x3 -> x13, waiting for transfers between devices: 0.01 us -> 14.3 us  [the longest x10 10.9 us: swap(): return lax.ppermute(x, axis, [(i, i ^ mask) for i in range(n)])]
    all_gather x1 -> x0, blocking collectives: 7.44 us -> none  [shards(): lax.all_gather(new_master.astype(jnp.bfloat16), 'grp', axis=1, tiled=True)]
    convert_element_type x2 -> x1, other arithmetic: 3.15 us -> 0.03 us  [shards(): copy_master, copy_first, copy_second = got[1].astype(F32)]
    unnamed x16 -> x12, local copies, waits for them, and re-layouts: 2.7 us -> 0.71 us
    dynamic_slice x0 -> x1, local copies, waits for them, and re-layouts: none -> 1.75 us  [shards(): lax.dynamic_slice(g, (0, (2 * k + side) * cols + start), (g.shape[0], wid...]
  transfers between devices with their start and end apart: 5 -> 13, of which waited for: 2 -> 8; matrix products, arithmetic and copies ran while one was open for 0% -> 4% of each run, Pallas kernels for 0% -> 0%
where the time goes in v1:
time: 40.7 us; the launch traced here: 40.5 us
  starting transfers between devices  20.2 us (50%)
  waiting for transfers between devices  14.3 us (35%)
  local copies, waits for them, and re-layouts  3.5 us (9%)
  other arithmetic  1.52 us (4%)
  between operations  0.99 us (2%)
    ppermute x10, starting transfers between devices, swap(): return lax.ppermute(x, axis, [(i, i ^ mask) for i in range(n)])  17.1 us
    ppermute x10, waiting for transfers between devices, swap(): return lax.ppermute(x, axis, [(i, i ^ mask) for i in range(n)])  10.9 us
    ppermute x3, waiting for transfers between devices, shards(): lax.ppermute(pack if k == 1 else w, 'grp', [(i, (i + k) % ng) for i in ra...  3.33 us
    ppermute x3, starting transfers between devices, shards(): lax.ppermute(pack if k == 1 else w, 'grp', [(i, (i + k) % ng) for i in ra...  3.18 us
    dynamic_slice x1, local copies, waits for them, and re-layouts, shards(): lax.dynamic_slice(g, (0, (2 * k + side) * cols + start), (g.shape[0], wid...  1.75 us
  transfers between devices with their start and end apart: 13, of which 8 were waited for; matrix products, arithmetic and copies ran while one was open for 4% of the time, Pallas kernels for 0%

profile of v1, /device:TPU:0, one launch (start us, length us, event | category | flops | bytes accessed | tf_op | source)
XLA Modules:
  0.0 40.5 jit_solution(2084906246498942143)
XLA Ops:
  0.6 1.8 %constant_dynamic-slice_fusion.7 = (bf16[1,1,128,1024]{3,2,1,0:T(8,128)(2,1)S(1)}, bf16[1,1,128,1024]{3,2,1,0:T(8,128)(2,1)S(1)}, bf16[1,1,128,1024]{3,2,1,0:T(8...) fusion(bf16[1,1,128,8192]{3,2,1,0:T(8,128)(2,1)} %param.4, ...), kind=kLoop, calls=%fused_computation.51 | loop fusion | bytes 4194336 | tf_op jit(solution)/shard_map/dynamic_slice | solution.py:51
  2.4 0.1 pad_maximum_fusion
  2.5 0.5 %collective-permute-start = (bf16[2,2,2,2,16,1024]{5,4,3,2,1,0:T(8,128)(2,1)S(1)}, bf16[2,2,2,2,16,1024]{5,4,3,2,1,0:T(8,128)(2,1)S(1)}, u32[]{:S(2)}, u32[]{:S(2)}) collective-permute-start(bf16[2,2,2,2,16,1024]{5,4,3,2,1,0:T(8,128)(2,1)S(1)} %pad_maximum_fusion), channel_id=1, source_target_pairs={{0,1},{1,0},{2,3},{3,2},{4,5},{5,4},{6,7},{7,6},{8,9},{9,8},{10,11... | collective-permute-start | bytes 1572872 | tf_op jit(solution)/shard_map/ppermute | solution.py:18
  3.0 0.1 pad_maximum_fusion.2
  3.1 0.1 collective-permute-start.5
  3.2 1.3 %collective-permute-done = bf16[2,2,2,2,16,1024]{5,4,3,2,1,0:T(8,128)(2,1)S(1)} collective-permute-done((bf16[2,2,2,2,16,1024]{5,4,3,2,1,0:T(8,128)(2,1)S(1)}, bf16[2,2,2,2,16,1024]{5,4,3,2,1,0:T(8,128)(2,1)S(1)}, u32[]{:S(2)}, u32[]{:S(2)}) %collective-permute-start) | collective-permute-done | bytes 524320 | tf_op jit(solution)/shard_map/ppermute | solution.py:18
  4.5 0.2 convert_add_fusion.1
  4.7 2.9 %collective-permute-start.1 = (bf16[2,2,2,16,1024]{4,3,2,1,0:T(8,128)(2,1)S(1)}, bf16[2,2,2,16,1024]{4,3,2,1,0:T(8,128)(2,1)S(1)}, u32[]{:S(2)}, u32[]{:S(2)}) collective-permute-start(bf16[2,2,2,16,1024]{4,3,2,1,0:T(8,128)(2,1)S(1)} %fusion), channel_id=1, source_target_pairs={{0,2},{1,3},{2,0},{3,1},{4,6},{5,7},{6,4},{7,5},{8,10},{9,11},{10,... | collective-permute-start | bytes 786440 | tf_op jit(solution)/shard_map/ppermute | solution.py:18
  7.7 0.0 collective-permute-done.5
  7.7 0.2 convert_add_fusion
  7.9 1.6 %collective-permute-start.6 = (bf16[2,2,2,16,1024]{4,3,0,1,2:T(8,128)(2,1)S(1)}, bf16[2,2,2,16,1024]{4,3,0,1,2:T(8,128)(2,1)S(1)}, u32[]{:S(2)}, u32[]{:S(2)}) collective-permute-start(bf16[2,2,2,16,1024]{4,3,0,1,2:T(8,128)(2,1)S(1)} %fusion.1), channel_id=1, source_target_pairs={{0,4},{4,0},{8,12},{12,8},{16,20},{20,16},{24,28},{28,24},{1,5},{5... | collective-permute-start | bytes 786440 | tf_op jit(solution)/shard_map/ppermute | solution.py:18
  9.5 4.8 %collective-permute-done.1 = bf16[2,2,2,16,1024]{4,3,2,1,0:T(8,128)(2,1)S(1)} collective-permute-done((bf16[2,2,2,16,1024]{4,3,2,1,0:T(8,128)(2,1)S(1)}, bf16[2,2,2,16,1024]{4,3,2,1,0:T(8,128)(2,1)S(1)}, u32[]{:S(2)}, u32[]{:S(2)}) %collective-permute-start.1) | collective-permute-done | bytes 262176 | tf_op jit(solution)/shard_map/ppermute | solution.py:18
  14.3 0.1 bitcast_add_fusion.1
  14.4 0.0 copy-start.3
  14.4 0.0 copy-start.4
  14.4 1.8 %collective-permute-start.2 = (bf16[2,2,16,1024]{3,2,1,0:T(8,128)(2,1)S(1)}, bf16[2,2,16,1024]{3,2,1,0:T(8,128)(2,1)S(1)}, u32[]{:S(2)}, u32[]{:S(2)}) collective-permute-start(bf16[2,2,16,1024]{3,2,1,0:T(8,128)(2,1)S(1)} %fusion.2), channel_id=1, source_target_pairs={{0,4},{4,0},{8,12},{12,8},{16,20},{20,16},{24,28},{28,24},{1,5},{5... | collective-permute-start | bytes 393224 | tf_op jit(solution)/shard_map/ppermute | solution.py:18
  16.2 0.0 collective-permute-done.6
  16.2 0.1 bitcast_add_fusion
  16.3 0.0 copy-start.5
  16.3 1.6 %collective-permute-start.7 = (bf16[2,2,16,1024]{3,2,0,1:T(8,128)(2,1)S(1)}, bf16[2,2,16,1024]{3,2,0,1:T(8,128)(2,1)S(1)}, u32[]{:S(2)}, u32[]{:S(2)}) collective-permute-start(bf16[2,2,16,1024]{3,2,0,1:T(8,128)(2,1)S(1)} %fusion.3), channel_id=1, source_target_pairs={{0,8},{4,12},{8,0},{12,4},{16,24},{20,28},{24,16},{28,20},{1,9},{5... | collective-permute-start | bytes 393224 | tf_op jit(solution)/shard_map/ppermute | solution.py:18
  18.0 1.5 %collective-permute-done.2 = bf16[2,2,16,1024]{3,2,1,0:T(8,128)(2,1)S(1)} collective-permute-done((bf16[2,2,16,1024]{3,2,1,0:T(8,128)(2,1)S(1)}, bf16[2,2,16,1024]{3,2,1,0:T(8,128)(2,1)S(1)}, u32[]{:S(2)}, u32[]{:S(2)}) %collective-permute-start.2) | collective-permute-done | bytes 131104 | tf_op jit(solution)/shard_map/ppermute | solution.py:18
  19.5 1.8 %collective-permute-start.3 = (bf16[2,16,1024]{2,1,0:T(8,128)(2,1)S(1)}, bf16[2,16,1024]{2,1,0:T(8,128)(2,1)S(1)}, u32[]{:S(2)}, u32[]{:S(2)}) collective-permute-start(bf16[2,16,1024]{2,1,0:T(8,128)(2,1)S(1)} %fusion.4), channel_id=1, source_target_pairs={{0,8},{4,12},{8,0},{12,4},{16,24},{20,28},{24,16},{28,20},{1,9},{5... | collective-permute-start | bytes 196616 | tf_op jit(solution)/shard_map/ppermute | solution.py:18
  21.4 0.4 %collective-permute-done.7 = bf16[2,2,16,1024]{3,2,0,1:T(8,128)(2,1)S(1)} collective-permute-done((bf16[2,2,16,1024]{3,2,0,1:T(8,128)(2,1)S(1)}, bf16[2,2,16,1024]{3,2,0,1:T(8,128)(2,1)S(1)}, u32[]{:S(2)}, u32[]{:S(2)}) %collective-permute-start.7) | collective-permute-done | bytes 131104 | tf_op jit(solution)/shard_map/ppermute | solution.py:18
  21.9 2.9 %collective-permute-start.8 = (bf16[2,16,1024]{2,1,0:T(8,128)(2,1)S(1)}, bf16[2,16,1024]{2,1,0:T(8,128)(2,1)S(1)}, u32[]{:S(2)}, u32[]{:S(2)}) collective-permute-start(bf16[2,16,1024]{2,1,0:T(8,128)(2,1)S(1)} %fusion.5), channel_id=1, source_target_pairs={{0,16},{4,20},{8,24},{12,28},{16,0},{20,4},{24,8},{28,12},{1,17},{... | collective-permute-start | bytes 196616 | tf_op jit(solution)/shard_map/ppermute | solution.py:18
  24.8 0.0 collective-permute-done.3
  24.8 1.9 %collective-permute-start.4 = (bf16[16,1024]{1,0:T(8,128)(2,1)S(1)}, bf16[16,1024]{1,0:T(8,128)(2,1)S(1)}, u32[]{:S(2)}, u32[]{:S(2)}) collective-permute-start(bf16[16,1024]{1,0:T(8,128)(2,1)S(1)} %fusion.7), channel_id=1, source_target_pairs={{0,16},{4,20},{8,24},{12,28},{16,0},{20,4},{24,8},{28,12},{1,17},{... | collective-permute-start | bytes 98312 | tf_op jit(solution)/shard_map/ppermute | solution.py:18
  26.8 0.7 %collective-permute-done.8 = bf16[2,16,1024]{2,1,0:T(8,128)(2,1)S(1)} collective-permute-done((bf16[2,16,1024]{2,1,0:T(8,128)(2,1)S(1)}, bf16[2,16,1024]{2,1,0:T(8,128)(2,1)S(1)}, u32[]{:S(2)}, u32[]{:S(2)}) %collective-permute-start.8) | collective-permute-done | bytes 65568 | tf_op jit(solution)/shard_map/ppermute | solution.py:18
  27.5 1.8 %collective-permute-start.9 = (bf16[16,1024]{1,0:T(8,128)(2,1)S(1)}, bf16[16,1024]{1,0:T(8,128)(2,1)S(1)}, u32[]{:S(2)}, u32[]{:S(2)}) collective-permute-start(bf16[16,1024]{1,0:T(8,128)(2,1)S(1)} %fusion.8), channel_id=1, source_target_pairs={{0,2},{1,3},{2,0},{3,1},{4,6},{5,7},{6,4},{7,5},{8,10},{9,11},{10,... | collective-permute-start | bytes 98312 | tf_op jit(solution)/shard_map/ppermute | solution.py:18
  29.3 0.4 %collective-permute-done.4 = bf16[16,1024]{1,0:T(8,128)(2,1)S(1)} collective-permute-done((bf16[16,1024]{1,0:T(8,128)(2,1)S(1)}, bf16[16,1024]{1,0:T(8,128)(2,1)S(1)}, u32[]{:S(2)}, u32[]{:S(2)}) %collective-permute-start.4) | collective-permute-done | bytes 32800 | tf_op jit(solution)/shard_map/ppermute | solution.py:18
  29.7 1.8 %collective-permute-done.9 = bf16[16,1024]{1,0:T(8,128)(2,1)S(1)} collective-permute-done((bf16[16,1024]{1,0:T(8,128)(2,1)S(1)}, bf16[16,1024]{1,0:T(8,128)(2,1)S(1)}, u32[]{:S(2)}, u32[]{:S(2)}) %collective-permute-start.9) | collective-permute-done | bytes 32800 | tf_op jit(solution)/shard_map/ppermute | solution.py:18
  31.5 0.0 copy-done.3
  31.5 0.0 copy-done.4
  31.6 0.0 copy-start
  31.6 0.0 copy-start.1
  31.6 0.0 copy-done.5
  31.6 0.7 %constant_dynamic-update-slice_fusion.2 = (bf16[16,8192]{1,0:T(8,128)(2,1)S(1)}, bf16[16,2048]{1,0:T(8,128)(2,1)S(1)}, f32[16,2048]{1,0:T(8,128)}) fusion(bf16[16,8192]{1,0:T(8,128)(2,1)S(1)} %broadcast_in_dim.3, s32[]{:T(128)S(6)} %select_n.104, f32[16,2048]{1,0:T(8,128)S(1)} %copy-done.5, f32[16,2048]{1,0:T(8,128)S(1)} %get-tuple-element.26, ...), kind=kLoop, calls=%fused_computation.43 | loop fusion | flops 294912 | bytes 655364 | tf_op jit(solution)/shard_map/dynamic_update_slice | solution.py:76
  32.4 0.1 collective-permute-start.10
  32.5 1.8 %collective-permute-start.11 = (bf16[16,2048]{1,0:T(8,128)(2,1)S(1)}, bf16[16,2048]{1,0:T(8,128)(2,1)S(1)}, u32[]{:S(2)}, u32[]{:S(2)}) collective-permute-start(bf16[16,2048]{1,0:T(8,128)(2,1)S(1)} %get-tuple-element.12), channel_id=1, source_target_pairs={{0,2},{1,3},{2,0},{3,1},{4,6},{5,7},{6,4},{7,5},{8,10},{9,11},{10,... | collective-permute-start | bytes 196616 | tf_op jit(solution)/shard_map/ppermute | solution.py:79
  34.3 1.3 %collective-permute-start.12 = (bf16[16,2048]{1,0:T(8,128)(2,1)S(1)}, bf16[16,2048]{1,0:T(8,128)(2,1)S(1)}, u32[]{:S(2)}, u32[]{:S(2)}) collective-permute-start(bf16[16,2048]{1,0:T(8,128)(2,1)S(1)} %get-tuple-element.12), channel_id=1, source_target_pairs={{0,3},{1,0},{2,1},{3,2},{4,7},{5,4},{6,5},{7,6},{8,11},{9,8},{10,9... | collective-permute-start | bytes 196616 | tf_op jit(solution)/shard_map/ppermute | solution.py:79
  35.6 3.3 %collective-permute-done.10 = bf16[3,16,2048]{2,1,0:T(8,128)(2,1)S(1)} collective-permute-done((bf16[3,16,2048]{2,1,0:T(8,128)(2,1)S(1)}, bf16[3,16,2048]{2,1,0:T(8,128)(2,1)S(1)}, u32[]{:S(2)}, u32[]{:S(2)}) %collective-permute-start.10) | collective-permute-done | bytes 196640 | tf_op jit(solution)/shard_map/ppermute | solution.py:79
  39.0 0.8 %slice_bitcast_fusion = (f32[16,2048]{1,0:T(8,128)}, f32[16,2048]{1,0:T(8,128)}, f32[16,2048]{1,0:T(8,128)}) fusion(f32[3,16,2048]{2,1,0:T(8,128)S(1)} %convert_element_type.127), kind=kLoop, calls=%fused_computation.18 | loop fusion | bytes 786432 | tf_op jit(solution)/shard_map/unstack | solution.py:80
  39.8 0.0 collective-permute-done.11
  39.8 0.0 collective-permute-done.12
  39.8 0.0 copy-start.2
  39.8 0.0 copy-done
  39.8 0.0 copy-done.1
  39.8 0.7 %copy-done.2 = bf16[16,8192]{1,0:T(8,128)(2,1)} copy-done((bf16[16,8192]{1,0:T(8,128)(2,1)}, bf16[16,8192]{1,0:T(8,128)(2,1)S(1)}, u32[]{:S(2)}) %copy-start.2) | copy-done | bytes 262168
  (22 shorter events, 0.5 us)
Async XLA Ops:
  2.5 2.1 %collective-permute-start = (bf16[2,2,2,2,16,1024]{5,4,3,2,1,0:T(8,128)(2,1)S(1)}, bf16[2,2,2,2,16,1024]{5,4,3,2,1,0:T(8,128)(2,1)S(1)}, u32[]{:S(2)}, u32[]{:S(2)}) collective-permute-start(bf16[2,2,2,2,16,1024]{5,4,3,2,1,0:T(8,128)(2,1)S(1)} %pad_maximum_fusion), channel_id=1, source_target_pairs={{0,1},{1,0},{2,3},{3,2},{4,5},{5,4},{6,7},{7,6},{8,9},{9,8},{10,11... | collective-permute-start | bytes 1572872 | tf_op jit(solution)/shard_map/ppermute | solution.py:18
  3.1 4.6 %collective-permute-start.5 = (bf16[2,2,2,2,16,1024]{5,4,0,1,2,3:T(8,128)(2,1)S(1)}, bf16[2,2,2,2,16,1024]{5,4,0,1,2,3:T(8,128)(2,1)S(1)}, u32[]{:S(2)}, u32[]{:S(2)}) collective-permute-start(bf16[2,2,2,2,16,1024]{5,4,0,1,2,3:T(8,128)(2,1)S(1)} %copy.16), channel_id=1, source_target_pairs={{0,1},{1,0},{2,3},{3,2},{4,5},{5,4},{6,7},{7,6},{8,9},{9,8},{10,11... | collective-permute-start | bytes 1572872 | tf_op jit(solution)/shard_map/ppermute | solution.py:18
  4.7 9.5 %collective-permute-start.1 = (bf16[2,2,2,16,1024]{4,3,2,1,0:T(8,128)(2,1)S(1)}, bf16[2,2,2,16,1024]{4,3,2,1,0:T(8,128)(2,1)S(1)}, u32[]{:S(2)}, u32[]{:S(2)}) collective-permute-start(bf16[2,2,2,16,1024]{4,3,2,1,0:T(8,128)(2,1)S(1)} %fusion), channel_id=1, source_target_pairs={{0,2},{1,3},{2,0},{3,1},{4,6},{5,7},{6,4},{7,5},{8,10},{9,11},{10,... | collective-permute-start | bytes 786440 | tf_op jit(solution)/shard_map/ppermute | solution.py:18
  7.9 8.3 %collective-permute-start.6 = (bf16[2,2,2,16,1024]{4,3,0,1,2:T(8,128)(2,1)S(1)}, bf16[2,2,2,16,1024]{4,3,0,1,2:T(8,128)(2,1)S(1)}, u32[]{:S(2)}, u32[]{:S(2)}) collective-permute-start(bf16[2,2,2,16,1024]{4,3,0,1,2:T(8,128)(2,1)S(1)} %fusion.1), channel_id=1, source_target_pairs={{0,4},{4,0},{8,12},{12,8},{16,20},{20,16},{24,28},{28,24},{1,5},{5... | collective-permute-start | bytes 786440 | tf_op jit(solution)/shard_map/ppermute | solution.py:18
  14.4 17.1 %copy-start.3 = (f32[16,2048]{1,0:T(8,128)S(1)}, f32[16,2048]{1,0:T(8,128)}, u32[]{:S(2)}) copy-start(f32[16,2048]{1,0:T(8,128)} %param.6) | copy-start | bytes 393220
  14.4 17.1 %copy-start.4 = (f32[16,2048]{1,0:T(8,128)S(1)}, f32[16,2048]{1,0:T(8,128)}, u32[]{:S(2)}) copy-start(f32[16,2048]{1,0:T(8,128)} %param.7) | copy-start | bytes 393220
  14.4 5.1 %collective-permute-start.2 = (bf16[2,2,16,1024]{3,2,1,0:T(8,128)(2,1)S(1)}, bf16[2,2,16,1024]{3,2,1,0:T(8,128)(2,1)S(1)}, u32[]{:S(2)}, u32[]{:S(2)}) collective-permute-start(bf16[2,2,16,1024]{3,2,1,0:T(8,128)(2,1)S(1)} %fusion.2), channel_id=1, source_target_pairs={{0,4},{4,0},{8,12},{12,8},{16,20},{20,16},{24,28},{28,24},{1,5},{5... | collective-permute-start | bytes 393224 | tf_op jit(solution)/shard_map/ppermute | solution.py:18
  16.3 15.3 %copy-start.5 = (f32[16,2048]{1,0:T(8,128)S(1)}, f32[16,2048]{1,0:T(8,128)}, u32[]{:S(2)}) copy-start(f32[16,2048]{1,0:T(8,128)} %param.5) | copy-start | bytes 393220
  16.3 5.5 %collective-permute-start.7 = (bf16[2,2,16,1024]{3,2,0,1:T(8,128)(2,1)S(1)}, bf16[2,2,16,1024]{3,2,0,1:T(8,128)(2,1)S(1)}, u32[]{:S(2)}, u32[]{:S(2)}) collective-permute-start(bf16[2,2,16,1024]{3,2,0,1:T(8,128)(2,1)S(1)} %fusion.3), channel_id=1, source_target_pairs={{0,8},{4,12},{8,0},{12,4},{16,24},{20,28},{24,16},{28,20},{1,9},{5... | collective-permute-start | bytes 393224 | tf_op jit(solution)/shard_map/ppermute | solution.py:18
  19.5 5.2 %collective-permute-start.3 = (bf16[2,16,1024]{2,1,0:T(8,128)(2,1)S(1)}, bf16[2,16,1024]{2,1,0:T(8,128)(2,1)S(1)}, u32[]{:S(2)}, u32[]{:S(2)}) collective-permute-start(bf16[2,16,1024]{2,1,0:T(8,128)(2,1)S(1)} %fusion.4), channel_id=1, source_target_pairs={{0,8},{4,12},{8,0},{12,4},{16,24},{20,28},{24,16},{28,20},{1,9},{5... | collective-permute-start | bytes 196616 | tf_op jit(solution)/shard_map/ppermute | solution.py:18
  21.9 5.6 %collective-permute-start.8 = (bf16[2,16,1024]{2,1,0:T(8,128)(2,1)S(1)}, bf16[2,16,1024]{2,1,0:T(8,128)(2,1)S(1)}, u32[]{:S(2)}, u32[]{:S(2)}) collective-permute-start(bf16[2,16,1024]{2,1,0:T(8,128)(2,1)S(1)} %fusion.5), channel_id=1, source_target_pairs={{0,16},{4,20},{8,24},{12,28},{16,0},{20,4},{24,8},{28,12},{1,17},{... | collective-permute-start | bytes 196616 | tf_op jit(solution)/shard_map/ppermute | solution.py:18
  24.8 4.9 %collective-permute-start.4 = (bf16[16,1024]{1,0:T(8,128)(2,1)S(1)}, bf16[16,1024]{1,0:T(8,128)(2,1)S(1)}, u32[]{:S(2)}, u32[]{:S(2)}) collective-permute-start(bf16[16,1024]{1,0:T(8,128)(2,1)S(1)} %fusion.7), channel_id=1, source_target_pairs={{0,16},{4,20},{8,24},{12,28},{16,0},{20,4},{24,8},{28,12},{1,17},{... | collective-permute-start | bytes 98312 | tf_op jit(solution)/shard_map/ppermute | solution.py:18
  27.5 4.0 %collective-permute-start.9 = (bf16[16,1024]{1,0:T(8,128)(2,1)S(1)}, bf16[16,1024]{1,0:T(8,128)(2,1)S(1)}, u32[]{:S(2)}, u32[]{:S(2)}) collective-permute-start(bf16[16,1024]{1,0:T(8,128)(2,1)S(1)} %fusion.8), channel_id=1, source_target_pairs={{0,2},{1,3},{2,0},{3,1},{4,6},{5,7},{6,4},{7,5},{8,10},{9,11},{10,... | collective-permute-start | bytes 98312 | tf_op jit(solution)/shard_map/ppermute | solution.py:18
  31.6 8.3 %copy-start = (f32[16,2048]{1,0:T(8,128)}, f32[16,2048]{1,0:T(8,128)S(1)}, u32[]{:S(2)}) copy-start(f32[16,2048]{1,0:T(8,128)S(1)} %get-tuple-element.8) | copy-start | bytes 393220
  31.6 8.3 %copy-start.1 = (f32[16,2048]{1,0:T(8,128)}, f32[16,2048]{1,0:T(8,128)S(1)}, u32[]{:S(2)}) copy-start(f32[16,2048]{1,0:T(8,128)S(1)} %get-tuple-element.26) | copy-start | bytes 393220
  32.4 6.6 %collective-permute-start.10 = (bf16[3,16,2048]{2,1,0:T(8,128)(2,1)S(1)}, bf16[3,16,2048]{2,1,0:T(8,128)(2,1)S(1)}, u32[]{:S(2)}, u32[]{:S(2)}) collective-permute-start(bf16[3,16,2048]{2,1,0:T(8,128)(2,1)S(1)} %pad_maximum_fusion.3), channel_id=1, source_target_pairs={{0,1},{1,2},{2,3},{3,0},{4,5},{5,6},{6,7},{7,4},{8,9},{9,10},{10,1... | collective-permute-start | bytes 589832 | tf_op jit(solution)/shard_map/ppermute | solution.py:79
  32.5 7.2 %collective-permute-start.11 = (bf16[16,2048]{1,0:T(8,128)(2,1)S(1)}, bf16[16,2048]{1,0:T(8,128)(2,1)S(1)}, u32[]{:S(2)}, u32[]{:S(2)}) collective-permute-start(bf16[16,2048]{1,0:T(8,128)(2,1)S(1)} %get-tuple-element.12), channel_id=1, source_target_pairs={{0,2},{1,3},{2,0},{3,1},{4,6},{5,7},{6,4},{7,5},{8,10},{9,11},{10,... | collective-permute-start | bytes 196616 | tf_op jit(solution)/shard_map/ppermute | solution.py:79
  34.3 5.5 %collective-permute-start.12 = (bf16[16,2048]{1,0:T(8,128)(2,1)S(1)}, bf16[16,2048]{1,0:T(8,128)(2,1)S(1)}, u32[]{:S(2)}, u32[]{:S(2)}) collective-permute-start(bf16[16,2048]{1,0:T(8,128)(2,1)S(1)} %get-tuple-element.12), channel_id=1, source_target_pairs={{0,3},{1,0},{2,1},{3,2},{4,7},{5,4},{6,5},{7,6},{8,11},{9,8},{10,9... | collective-permute-start | bytes 196616 | tf_op jit(solution)/shard_map/ppermute | solution.py:79
  39.8 0.7 %copy-start.2 = (bf16[16,8192]{1,0:T(8,128)(2,1)}, bf16[16,8192]{1,0:T(8,128)(2,1)S(1)}, u32[]{:S(2)}) copy-start(bf16[16,8192]{1,0:T(8,128)(2,1)S(1)} %constant_dynamic-update-slice_fusion) | copy-start | bytes 786436

commit v2 on v0

v2 whole, which is shorter than its diff:
```python
import jax
import jax.numpy as jnp
from jax import lax
from jax.experimental import pallas as pl
from jax.experimental.pallas import tpu as pltpu
from jax.sharding import PartitionSpec as P

beta_one = 0.9
beta_two = 0.95
learn_rate = 0.01
decay_rate = 0.1
epsilon = 1e-08
step_count = 100
F32 = jnp.float32
BF16 = jnp.bfloat16
BOTH = ("fsdp", "grp")
LIMIT = 4 * 2**20
SPLITS = [2]
VMEM = pl.BlockSpec(memory_space=pltpu.VMEM)
ANY = pl.BlockSpec(memory_space=pl.ANY)


def device_bit(bit, n_grp):
    flat = lax.axis_index("fsdp") * n_grp + lax.axis_index("grp")
    return (flat >> bit) & 1


def swap(x, masks):
    n = lax.axis_size("fsdp") * lax.axis_size("grp")
    return lax.ppermute(x, BOTH, [(i, i ^ masks[i & 1]) for i in range(n)])


def pick(t, index, dim):
    return lax.dynamic_index_in_dim(t, index, dim, keepdims=False)


def updated(gradient, master, moment_one, moment_two):
    new_first = beta_one * moment_one + (1.0 - beta_one) * gradient
    new_second = beta_two * moment_two + (1.0 - beta_two) * gradient * gradient
    first_hat = new_first / (1.0 - beta_one**step_count)
    second_hat = new_second / (1.0 - beta_two**step_count)
    new_master = master - learn_rate * (
        first_hat / (jnp.sqrt(second_hat) + epsilon) + decay_rate * master
    )
    return new_master, new_first, new_second


def widths(cols, parts):
    cuts = [cols * k // parts // 128 * 128 for k in range(parts)] + [cols]
    return [b - a for a, b in zip(cuts, cuts[1:])]


def shards(grads, master, moment_one, moment_two):
    ng, nf = lax.axis_size("grp"), lax.axis_size("fsdp")
    g_bits, f_bits = ng.bit_length() - 1, nf.bit_length() - 1
    me_g = lax.axis_index("grp")
    g = grads[0, 0]
    rows, cols = g.shape[0] // nf, g.shape[1] // ng
    bit = [device_bit(k, ng) for k in range(g_bits + f_bits)]
    core, over = bit[0], ng // 4

    def place(core, j, away):
        return jnp.where(core == 0, bit[1] ^ away, j), jnp.where(core == 0, j, bit[g_bits] ^ away)

    def pieces(core, away, start, width):
        rolled = g.reshape((2,) * f_bits + (rows, g.shape[1]))
        halves = []
        for j in range(2):
            x, y = place(core, j, away)
            half = pick(rolled, y, f_bits - 1)
            sides = [lax.dynamic_slice_in_dim(half, (4 * k + 2 * x + core) * cols + start, width, f_bits) for k in range(over)]
            halves.append(jnp.stack(sides))
        return jnp.stack(halves).reshape((2,) * (g_bits - 2 + f_bits) + (rows, width))

    cut = widths(cols, SPLITS[0])
    near = [1, 1]

    starts = [sum(cut[:k]) for k in range(len(cut))]
    if over == 1 and rows % 16 == 0 and min(cut) % 128 == 0:
        away_out, = gathered(g, [(1, 1)], cut, rows, nf)
        kept_out, away_own, kept_own = gathered(g, [(1, 0), (0, 1), (0, 0)], cut, rows, nf)
        shape = (2,) * (g_bits - 2 + f_bits) + (rows,)
        away_out, kept_out, away_own, kept_own = [[t.reshape(shape + t.shape[-1:]) for t in ts] for ts in (away_out, kept_out, away_own, kept_own)]
    else:
        away_out, kept_out, away_own, kept_own = [
            [pieces(c, away, a, w) for a, w in zip(starts, cut)] for c, away in ((1 - core, 1), (1 - core, 0), (core, 1), (core, 0))
        ]
    got_away = [swap(t, near) for t in away_out]
    got_kept = [swap(t, near) for t in kept_out]
    sent = [(t.astype(F32) + x.astype(F32)).astype(BF16) for t, x in zip(away_own, got_away)]
    kept = [t.astype(F32) + x.astype(F32) for t, x in zip(kept_own, got_kept)]

    dims = list(range(g_bits - 1, 1, -1)) + list(range(g_bits + f_bits - 1, g_bits, -1))
    pair = (1, g_bits)
    left = list(range(2, g_bits)) + list(range(g_bits + 1, g_bits + f_bits))
    step = 0
    while True:
        p, q = pair
        got = [swap(s, [1 << p, 1 << q]) for s in sent]
        ts = [k + x.astype(F32) for k, x in zip(kept, got)]
        step += 1
        ts = recut(ts, cols, SPLITS[min(step, len(SPLITS) - 1)])
        if p != q:
            mine = jnp.where(core == 0, bit[q], bit[p])
            got = [swap(pick(t, 1 - mine, 0).astype(BF16), [1 << q, 1 << p]) for t in ts]
            ts = [pick(t, mine, 0) + x.astype(F32) for t, x in zip(ts, got)]
            step += 1
            ts = recut(ts, cols, SPLITS[min(step, len(SPLITS) - 1)])
        if not left:
            break
        pair = (left[0], left[1]) if len(left) > 1 else (left[0], left[0])
        left = left[2:]
        p, q = pair
        at_p, at_q = dims.index(p), dims.index(q)

        def choose(t, j, away):
            i_p = jnp.where(core == 0, bit[p] ^ away, j)
            i_q = jnp.where(core == 0, j, bit[q] ^ away)
            first, last = ((i_p, at_p), (i_q, at_q)) if at_p > at_q else ((i_q, at_q), (i_p, at_p))
            return pick(pick(t, *first), *last)

        if p == q:
            sent = [pick(t, 1 - bit[p], at_p).astype(BF16) for t in ts]
            kept = [pick(t, bit[p], at_p) for t in ts]
        else:
            sent = [jnp.stack([choose(t, j, 1) for j in range(2)]).astype(BF16) for t in ts]
            kept = [jnp.stack([choose(t, j, 0) for j in range(2)]) for t in ts]
        dims = [d for d in dims if d not in pair]
    gradient = recut(ts, cols, 1)[0] / (ng * nf)

    early = updated(gradient, master, moment_one, moment_two)
    pack = lax.optimization_barrier(jnp.stack([e.astype(BF16) for e in early]))
    w = pack[0]
    new_master, new_first, new_second = updated(*lax.optimization_barrier((gradient, master, moment_one, moment_two)))
    got = [pack]
    for k in range(1, ng):
        got.append(lax.ppermute(pack if k == 1 else w, "grp", [(i, (i + k) % ng) for i in range(ng)]))
    if rows % 16 == 0 and cols % 128 == 0:
        weights, copy_master, copy_first, copy_second = spread(got)
    else:
        weights = jnp.zeros((rows, cols * ng), BF16)
        for k in range(ng):
            weights = lax.dynamic_update_slice(weights, got[k][0] if k < 2 else got[k], (0, ((me_g + ng - k) % ng) * cols))
        copy_master, copy_first, copy_second = got[1].astype(F32)

    return (new_master, new_first, new_second, weights, copy_master, copy_first, copy_second)


def recut(ts, cols, parts):
    if len(ts) == parts:
        return ts
    whole = jnp.concatenate(ts, -1) if len(ts) > 1 else ts[0]
    starts = [sum(widths(cols, parts)[:k]) for k in range(parts + 1)]
    return [lax.slice_in_dim(whole, a, b, axis=whole.ndim - 1) for a, b in zip(starts, starts[1:])] if parts > 1 else [whole]


def gathered(g, wanted, cut, rows, nf):
    cols = sum(cut)
    starts = [sum(cut[:k]) for k in range(len(cut))]

    def kernel(g_ref, *refs):
        outs, sem = refs[:-1], refs[-1]
        me_f, me_g = lax.axis_index("fsdp"), lax.axis_index("grp")
        copies = []
        for n, (sibling, away) in enumerate(wanted):
            core = (me_g & 1) ^ sibling
            for j in range(2):
                x = jnp.where(core == 0, (me_g >> 1) ^ away, j)
                y = jnp.where(core == 0, j, (me_f & 1) ^ away)
                base = (2 * x + core) * cols
                for k, (a, w) in enumerate(zip(starts, cut)):
                    column = pl.multiple_of(base + a, 128)
                    copies.append(pltpu.make_async_copy(g_ref.at[:, y, :, pl.ds(column, w)], outs[n * len(cut) + k].at[j], sem.at[len(copies)]))
        for c in copies:
            c.start()
        for c in copies:
            c.wait()

    size = g.size * 2 // nf // 4 // 2
    flat = pl.pallas_call(
        kernel,
        out_shape=[jax.ShapeDtypeStruct((2, nf // 2, rows, w), g.dtype) for _ in wanted for w in cut],
        in_specs=[ANY],
        out_specs=[VMEM] * (len(wanted) * len(cut)),
        scratch_shapes=[pltpu.SemaphoreType.DMA((2 * len(wanted) * len(cut),))],
        compiler_params=pltpu.CompilerParams(vmem_limit_bytes=LIMIT),
        cost_estimate=pl.CostEstimate(flops=0, bytes_accessed=g.size * len(wanted), transcendentals=0),
    )(g.reshape(nf // 2, 2, rows, g.shape[1]))
    return [flat[n * len(cut) : (n + 1) * len(cut)] for n in range(len(wanted))]


def spread(got):
    ng, (rows, cols) = len(got), got[2].shape

    def kernel(*refs):
        me = lax.axis_index("grp")
        blocks, weights, copies, wide, sem = refs[:ng], refs[ng], refs[ng + 1 : ng + 4], refs[ng + 4], refs[ng + 5]
        moves = []
        for k in range(ng):
            owner = lax.rem(me + ng - k, ng)
            source = blocks[k].at[0] if k < 2 else blocks[k]
            moves.append(pltpu.make_async_copy(source, weights.at[:, pl.ds(pl.multiple_of(owner * cols, 128), cols)], sem.at[k]))
            moves[-1].start()
        for k in range(3):
            wide[k] = blocks[1][k].astype(F32)
            moves.append(pltpu.make_async_copy(wide.at[k], copies[k], sem.at[ng + k]))
            moves[-1].start()
        for m in moves:
            m.wait()

    return pl.pallas_call(
        kernel,
        out_shape=[jax.ShapeDtypeStruct((rows, cols * ng), BF16)] + [jax.ShapeDtypeStruct((rows, cols), F32)] * 3,
        in_specs=[VMEM] * ng,
        out_specs=[ANY] * 4,
        scratch_shapes=[pltpu.VMEM((3, rows, cols), F32), pltpu.SemaphoreType.DMA((ng + 3,))],
        compiler_params=pltpu.CompilerParams(vmem_limit_bytes=LIMIT),
    )(*got)


def solution(mesh):
    return jax.shard_map(
        shards,
        mesh=mesh,
        in_specs=(P("grp", "fsdp", None, None), P("fsdp", "grp"), P("fsdp", "grp"), P("fsdp", "grp")),
        out_specs=(P("fsdp", "grp"), P("fsdp", "grp"), P("fsdp", "grp"), P("fsdp", None), P("fsdp", "grp"), P("fsdp", "grp"), P("fsdp", "grp")),
        check_vma=False,
    )
```

time: 132 us -> 38.6 us (0.29)
  waiting for transfers between devices: 103 us -> 12.1 us
  starting transfers between devices: 1.78 us -> 20.8 us
  between operations: 14.1 us -> 0.88 us
  blocking collectives: 7.44 us -> 0 us
  other arithmetic: 3.15 us -> 1.41 us
  Pallas kernels: 0 us -> 1.46 us
    reduce_scatter x2 -> x0, waiting for transfers between devices: 102 us -> none  [the longest x1 65.2 us: shards(): lax.psum_scatter(column_share, 'fsdp', scatter_dimension=0, tiled=True)]
    ppermute x3 -> x15, starting transfers between devices: 1.7 us -> 20.8 us  [the longest x12 19 us: swap(): return lax.ppermute(x, BOTH, [(i, i ^ masks[i & 1]) for i in range(n)])]
    ppermute x3 -> x15, waiting for transfers between devices: 0.01 us -> 12.1 us  [the longest x12 7.42 us: swap(): return lax.ppermute(x, BOTH, [(i, i ^ masks[i & 1]) for i in range(n)])]
    all_gather x1 -> x0, blocking collectives: 7.44 us -> none  [shards(): lax.all_gather(new_master.astype(jnp.bfloat16), 'grp', axis=1, tiled=True)]
    convert_element_type x2, other arithmetic: 3.15 us -> 0.13 us  [shards(): (t.astype(F32) + x.astype(F32)).astype(BF16)]
    pallas_call x0 -> x3, Pallas kernels: none -> 1.46 us  [the longest x1 0.9 us: spread(): pl.pallas_call(kernel, out_shape=[jax.ShapeDtypeStruct((rows, cols * ng),...]
    unnamed x16 -> x8, local copies, waits for them, and re-layouts: 2.7 us -> 1.6 us
  transfers between devices with their start and end apart: 5 -> 15, of which waited for: 2 -> 7; matrix products, arithmetic and copies ran while one was open for 0% -> 4% of each run, Pallas kernels for 0% -> 1%
where the time goes in v2:
time: 38.6 us; the launch traced here: 38.4 us
  starting transfers between devices  20.8 us (54%)
  waiting for transfers between devices  12.1 us (31%)
  local copies, waits for them, and re-layouts  1.76 us (5%)
  Pallas kernels  1.46 us (4%)
  other arithmetic  1.41 us (4%)
  between operations  0.88 us (2%)
    ppermute x12, starting transfers between devices, swap(): return lax.ppermute(x, BOTH, [(i, i ^ masks[i & 1]) for i in range(n)])  19 us
    ppermute x12, waiting for transfers between devices, swap(): return lax.ppermute(x, BOTH, [(i, i ^ masks[i & 1]) for i in range(n)])  7.42 us
    ppermute x3, waiting for transfers between devices, shards(): lax.ppermute(pack if k == 1 else w, 'grp', [(i, (i + k) % ng) for i in ra...  4.71 us
    ppermute x3, starting transfers between devices, shards(): lax.ppermute(pack if k == 1 else w, 'grp', [(i, (i + k) % ng) for i in ra...  1.78 us
    unnamed x8, local copies, waits for them, and re-layouts  1.6 us
    pallas_call x1, Pallas kernels, spread(): pl.pallas_call(kernel, out_shape=[jax.ShapeDtypeStruct((rows, cols * ng),...  0.9 us
    sub x1, other arithmetic, updated(): master - learn_rate * (first_hat / (jnp.sqrt(second_hat) + epsilon) + dec...  0.8 us
  transfers between devices with their start and end apart: 15, of which 7 were waited for; matrix products, arithmetic and copies ran while one was open for 4% of the time, Pallas kernels for 1%

profile of v2, /device:TPU:0, one launch (start us, length us, event | category | flops | bytes accessed | tf_op | source)
XLA Modules:
  0.0 38.4 jit_solution(16880651916902101598)
XLA Ops:
  0.6 0.0 copy-start
  0.6 1.6 %copy-done = bf16[1,1,128,8192]{3,2,1,0:T(8,128)(2,1)S(1)} copy-done((bf16[1,1,128,8192]{3,2,1,0:T(8,128)(2,1)S(1)}, bf16[1,1,128,8192]{3,2,1,0:T(8,128)(2,1)}, u32[]{:S(2)}) %copy-start) | copy-done | bytes 2097176
  2.2 0.1 shard_map.100
  2.4 0.5 %collective-permute-start.1 = (bf16[2,2,2,16,1024]{4,3,2,1,0:T(8,128)(2,1)S(1)}, bf16[2,2,2,16,1024]{4,3,2,1,0:T(8,128)(2,1)S(1)}, u32[]{:S(2)}, u32[]{:S(2)}) collective-permute-start(bf16[2,2,2,16,1024]{4,3,2,1,0:T(8,128)(2,1)S(1)} %bitcast.62), channel_id=1, source_target_pairs={{0,1},{1,0},{2,3},{3,2},{4,5},{5,4},{6,7},{7,6},{8,9},{9,8},{10,11... | collective-permute-start | bytes 786440 | tf_op jit(solution)/shard_map/ppermute | solution.py:30
  2.9 0.1 collective-permute-start.7
  3.0 0.4 %shard_map.99 = (bf16[2,4,16,1024]{3,2,1,0:T(8,128)(2,1)S(1)}, bf16[2,4,16,1024]{3,2,1,0:T(8,128)(2,1)S(1)}, bf16[2,4,16,1024]{3,2,1,0:T(8,128)(2,1)S(1)}, bf16[...) custom-call(bf16[4,2,16,8192]{3,2,1,0:T(8,128)(2,1)S(1)} %bitcast.54), custom_call_target="tpu_custom_call" | custom-call | bytes 3145728 | tf_op jit(solution)/shard_map/pallas_call | solution.py:180
  3.4 0.5 %collective-permute-start = (bf16[2,2,2,16,1024]{4,3,2,1,0:T(8,128)(2,1)S(1)}, bf16[2,2,2,16,1024]{4,3,2,1,0:T(8,128)(2,1)S(1)}, u32[]{:S(2)}, u32[]{:S(2)}) collective-permute-start(bf16[2,2,2,16,1024]{4,3,2,1,0:T(8,128)(2,1)S(1)} %bitcast.61), channel_id=1, source_target_pairs={{0,1},{1,0},{2,3},{3,2},{4,5},{5,4},{6,7},{7,6},{8,9},{9,8},{10,11... | collective-permute-start | bytes 786440 | tf_op jit(solution)/shard_map/ppermute | solution.py:30
  3.9 0.1 collective-permute-done.1
  4.0 0.1 fusion.2
  4.1 2.9 %collective-permute-start.2 = (bf16[2,2,2,16,1024]{4,3,2,1,0:T(8,128)(2,1)S(1)}, bf16[2,2,2,16,1024]{4,3,2,1,0:T(8,128)(2,1)S(1)}, u32[]{:S(2)}, u32[]{:S(2)}) collective-permute-start(bf16[2,2,2,16,1024]{4,3,2,1,0:T(8,128)(2,1)S(1)} %fusion.2), channel_id=1, source_target_pairs={{0,2},{1,5},{2,0},{3,7},{4,6},{5,1},{6,4},{7,3},{8,10},{9,13},{10,... | collective-permute-start | bytes 786440 | tf_op jit(solution)/shard_map/ppermute | solution.py:30
  7.0 0.0 collective-permute-start.6
  7.0 0.0 collective-permute-done.7
  7.0 0.1 fusion
  7.1 1.4 %collective-permute-start.8 = (bf16[2,2,2,16,1024]{4,3,2,1,0:T(8,128)(2,1)S(1)}, bf16[2,2,2,16,1024]{4,3,2,1,0:T(8,128)(2,1)S(1)}, u32[]{:S(2)}, u32[]{:S(2)}) collective-permute-start(bf16[2,2,2,16,1024]{4,3,2,1,0:T(8,128)(2,1)S(1)} %fusion), channel_id=1, source_target_pairs={{0,2},{1,5},{2,0},{3,7},{4,6},{5,1},{6,4},{7,3},{8,10},{9,13},{10,... | collective-permute-start | bytes 786440 | tf_op jit(solution)/shard_map/ppermute | solution.py:30
  8.6 0.0 collective-permute-done
  8.6 2.8 %collective-permute-done.2 = bf16[2,2,2,16,1024]{4,3,2,1,0:T(8,128)(2,1)S(1)} collective-permute-done((bf16[2,2,2,16,1024]{4,3,2,1,0:T(8,128)(2,1)S(1)}, bf16[2,2,2,16,1024]{4,3,2,1,0:T(8,128)(2,1)S(1)}, u32[]{:S(2)}, u32[]{:S(2)}) %collective-permute-start.2) | collective-permute-done | bytes 262176 | tf_op jit(solution)/shard_map/ppermute | solution.py:30
  11.4 0.1 fusion.3
  11.5 2.1 %collective-permute-start.3 = (bf16[2,2,16,1024]{3,2,1,0:T(8,128)(2,1)S(1)}, bf16[2,2,16,1024]{3,2,1,0:T(8,128)(2,1)S(1)}, u32[]{:S(2)}, u32[]{:S(2)}) collective-permute-start(bf16[2,2,16,1024]{3,2,1,0:T(8,128)(2,1)S(1)} %fusion.5), channel_id=1, source_target_pairs={{0,4},{1,3},{2,6},{3,1},{4,0},{5,7},{6,2},{7,5},{8,12},{9,11},{10,... | collective-permute-start | bytes 393224 | tf_op jit(solution)/shard_map/ppermute | solution.py:30
  13.6 0.0 collective-permute-done.6
  13.7 0.9 %collective-permute-done.8 = bf16[2,2,2,16,1024]{4,3,2,1,0:T(8,128)(2,1)S(1)} collective-permute-done((bf16[2,2,2,16,1024]{4,3,2,1,0:T(8,128)(2,1)S(1)}, bf16[2,2,2,16,1024]{4,3,2,1,0:T(8,128)(2,1)S(1)}, u32[]{:S(2)}, u32[]{:S(2)}) %collective-permute-start.8) | collective-permute-done | bytes 262176 | tf_op jit(solution)/shard_map/ppermute | solution.py:30
  14.5 0.1 fusion.1
  14.7 0.0 copy-start.1
  14.7 0.0 copy-start.2
  14.7 0.0 copy-start.3
  14.7 2.4 %collective-permute-start.9 = (bf16[2,2,16,1024]{3,2,1,0:T(8,128)(2,1)S(1)}, bf16[2,2,16,1024]{3,2,1,0:T(8,128)(2,1)S(1)}, u32[]{:S(2)}, u32[]{:S(2)}) collective-permute-start(bf16[2,2,16,1024]{3,2,1,0:T(8,128)(2,1)S(1)} %fusion.6), channel_id=1, source_target_pairs={{0,4},{1,3},{2,6},{3,1},{4,0},{5,7},{6,2},{7,5},{8,12},{9,11},{10,... | collective-permute-start | bytes 393224 | tf_op jit(solution)/shard_map/ppermute | solution.py:30
  17.2 0.0 collective-permute-done.3
  17.2 1.6 %collective-permute-start.4 = (bf16[2,16,1024]{2,1,0:T(8,128)(2,1)S(1)}, bf16[2,16,1024]{2,1,0:T(8,128)(2,1)S(1)}, u32[]{:S(2)}, u32[]{:S(2)}) collective-permute-start(bf16[2,16,1024]{2,1,0:T(8,128)(2,1)S(1)} %pad_maximum_fusion.2), channel_id=1, source_target_pairs={{0,8},{1,17},{2,10},{3,19},{4,12},{5,21},{6,14},{7,23},{8,0},{9,25... | collective-permute-start | bytes 196616 | tf_op jit(solution)/shard_map/ppermute | solution.py:30
  18.9 1.2 %collective-permute-done.9 = bf16[2,2,16,1024]{3,2,1,0:T(8,128)(2,1)S(1)} collective-permute-done((bf16[2,2,16,1024]{3,2,1,0:T(8,128)(2,1)S(1)}, bf16[2,2,16,1024]{3,2,1,0:T(8,128)(2,1)S(1)}, u32[]{:S(2)}, u32[]{:S(2)}) %collective-permute-start.9) | collective-permute-done | bytes 131104 | tf_op jit(solution)/shard_map/ppermute | solution.py:30
  20.2 2.1 %collective-permute-start.10 = (bf16[2,16,1024]{2,1,0:T(8,128)(2,1)S(1)}, bf16[2,16,1024]{2,1,0:T(8,128)(2,1)S(1)}, u32[]{:S(2)}, u32[]{:S(2)}) collective-permute-start(bf16[2,16,1024]{2,1,0:T(8,128)(2,1)S(1)} %pad_maximum_fusion.3), channel_id=1, source_target_pairs={{0,8},{1,17},{2,10},{3,19},{4,12},{5,21},{6,14},{7,23},{8,0},{9,25... | collective-permute-start | bytes 196616 | tf_op jit(solution)/shard_map/ppermute | solution.py:30
  22.4 0.0 collective-permute-done.4
  22.4 2.7 %collective-permute-start.5 = (bf16[16,1024]{1,0:T(8,128)(2,1)S(1)}, bf16[16,1024]{1,0:T(8,128)(2,1)S(1)}, u32[]{:S(2)}, u32[]{:S(2)}) collective-permute-start(bf16[16,1024]{1,0:T(8,128)(2,1)S(1)} %fusion.11), channel_id=1, source_target_pairs={{0,16},{1,9},{2,18},{3,11},{4,20},{5,13},{6,22},{7,15},{8,24},{9,1... | collective-permute-start | bytes 98312 | tf_op jit(solution)/shard_map/ppermute | solution.py:30
  25.1 0.0 collective-permute-done.10
  25.1 2.6 %collective-permute-start.11 = (bf16[16,1024]{1,0:T(8,128)(2,1)S(1)}, bf16[16,1024]{1,0:T(8,128)(2,1)S(1)}, u32[]{:S(2)}, u32[]{:S(2)}) collective-permute-start(bf16[16,1024]{1,0:T(8,128)(2,1)S(1)} %fusion.14), channel_id=1, source_target_pairs={{0,16},{1,9},{2,18},{3,11},{4,20},{5,13},{6,22},{7,15},{8,24},{9,1... | collective-permute-start | bytes 98312 | tf_op jit(solution)/shard_map/ppermute | solution.py:30
  27.7 0.0 collective-permute-done.5
  27.7 2.3 %collective-permute-done.11 = bf16[16,1024]{1,0:T(8,128)(2,1)S(1)} collective-permute-done((bf16[16,1024]{1,0:T(8,128)(2,1)S(1)}, bf16[16,1024]{1,0:T(8,128)(2,1)S(1)}, u32[]{:S(2)}, u32[]{:S(2)}) %collective-permute-start.11) | collective-permute-done | bytes 32800 | tf_op jit(solution)/shard_map/ppermute | solution.py:30
  30.0 0.0 copy-done.1
  30.0 0.0 copy-done.2
  30.1 0.0 copy-done.3
  30.1 0.1 fusion.8
  30.2 0.1 collective-permute-start.14
  30.3 1.6 %collective-permute-start.13 = (bf16[16,2048]{1,0:T(8,128)(2,1)S(1)}, bf16[16,2048]{1,0:T(8,128)(2,1)S(1)}, u32[]{:S(2)}, u32[]{:S(2)}) collective-permute-start(bf16[16,2048]{1,0:T(8,128)(2,1)S(1)} %slice_bitcast_fusion), channel_id=1, source_target_pairs={{0,2},{1,3},{2,0},{3,1},{4,6},{5,7},{6,4},{7,5},{8,10},{9,11},{10,... | collective-permute-start | bytes 196616 | tf_op jit(solution)/shard_map/ppermute | solution.py:137
  31.9 0.2 collective-permute-start.12
  32.0 0.8 %multiply_subtract_fusion = (f32[16,2048]{1,0:T(8,128)}, f32[16,2048]{1,0:T(8,128)}, f32[16,2048]{1,0:T(8,128)}) fusion(f32[16,2048]{1,0:T(8,128)S(1)} %copy-done.1, f32[16,2048]{1,0:T(8,128)S(1)} %get-tuple-element.33, f32[16,2048]{1,0:T(8,128)S(1)} %copy-done.2, f32[16,2048]{1,0:T(8,128)S(1)} %copy-done.3), kind=kLoop, calls=%fused_computation.23 | loop fusion | flops 491520 | bytes 917504 | tf_op jit(solution)/shard_map/sub | solution.py:42
  32.8 0.0 collective-permute-done.14.refs_3_
  32.8 3.1 %collective-permute-done.13.refs_2_ = bf16[16,2048]{1,0:T(8,128)(2,1)S(1)} collective-permute-done((bf16[16,2048]{1,0:T(8,128)(2,1)S(1)}, bf16[16,2048]{1,0:T(8,128)(2,1)S(1)}, u32[]{:S(2)}, u32[]{:S(2)}) %collective-permute-start.13) | collective-permute-done | bytes 65568 | tf_op jit(solution)/shard_map/ppermute | solution.py:137
  36.0 1.6 %collective-permute-done.12.refs_1_ = bf16[3,16,2048]{2,1,0:T(8,128)(2,1)S(1)} collective-permute-done((bf16[3,16,2048]{2,1,0:T(8,128)(2,1)S(1)}, bf16[3,16,2048]{2,1,0:T(8,128)(2,1)S(1)}, u32[]{:S(2)}, u32[]{:S(2)}) %collective-permute-start.12) | collective-permute-done | bytes 196640 | tf_op jit(solution)/shard_map/ppermute | solution.py:137
  37.5 0.9 %shard_map.101 = (bf16[16,8192]{1,0:T(8,128)(2,1)}, f32[16,2048]{1,0:T(8,128)}, f32[16,2048]{1,0:T(8,128)}, f32[16,2048]{1,0:T(8,128)}) custom-call(bf16[3,16,2048]{2,1,0:T(8,128)(2,1)S(1)} %pad_maximum_fusion.refs_0_, bf16[3,16,2048]{2,1,0:T(8,128)(2,1)S(1)} %collective-permute-done.12.refs_1_, bf16[16,2048]{1,0:T(8,128)(2,1)S(1)} %collective-permute-done.13.refs_2_, ...), custom_call_target="tpu_custom_call" | custom-call | tf_op jit(solution)/shard_map/pallas_call | solution.py:211
  (18 shorter events, 0.3 us)
Async XLA Ops:
  0.6 1.6 %copy-start = (bf16[1,1,128,8192]{3,2,1,0:T(8,128)(2,1)S(1)}, bf16[1,1,128,8192]{3,2,1,0:T(8,128)(2,1)}, u32[]{:S(2)}) copy-start(bf16[1,1,128,8192]{3,2,1,0:T(8,128)(2,1)} %param.4) | copy-start | bytes 6291460
  2.4 1.7 %collective-permute-start.1 = (bf16[2,2,2,16,1024]{4,3,2,1,0:T(8,128)(2,1)S(1)}, bf16[2,2,2,16,1024]{4,3,2,1,0:T(8,128)(2,1)S(1)}, u32[]{:S(2)}, u32[]{:S(2)}) collective-permute-start(bf16[2,2,2,16,1024]{4,3,2,1,0:T(8,128)(2,1)S(1)} %bitcast.62), channel_id=1, source_target_pairs={{0,1},{1,0},{2,3},{3,2},{4,5},{5,4},{6,7},{7,6},{8,9},{9,8},{10,11... | collective-permute-start | bytes 786440 | tf_op jit(solution)/shard_map/ppermute | solution.py:30
  2.9 4.2 %collective-permute-start.7 = (bf16[2,2,2,16,1024]{4,3,2,1,0:T(8,128)(2,1)S(1)}, bf16[2,2,2,16,1024]{4,3,2,1,0:T(8,128)(2,1)S(1)}, u32[]{:S(2)}, u32[]{:S(2)}) collective-permute-start(bf16[2,2,2,16,1024]{4,3,2,1,0:T(8,128)(2,1)S(1)} %bitcast.60), channel_id=1, source_target_pairs={{0,1},{1,0},{2,3},{3,2},{4,5},{5,4},{6,7},{7,6},{8,9},{9,8},{10,11... | collective-permute-start | bytes 786440 | tf_op jit(solution)/shard_map/ppermute | solution.py:30
  3.4 5.2 %collective-permute-start = (bf16[2,2,2,16,1024]{4,3,2,1,0:T(8,128)(2,1)S(1)}, bf16[2,2,2,16,1024]{4,3,2,1,0:T(8,128)(2,1)S(1)}, u32[]{:S(2)}, u32[]{:S(2)}) collective-permute-start(bf16[2,2,2,16,1024]{4,3,2,1,0:T(8,128)(2,1)S(1)} %bitcast.61), channel_id=1, source_target_pairs={{0,1},{1,0},{2,3},{3,2},{4,5},{5,4},{6,7},{7,6},{8,9},{9,8},{10,11... | collective-permute-start | bytes 786440 | tf_op jit(solution)/shard_map/ppermute | solution.py:30
  4.1 7.3 %collective-permute-start.2 = (bf16[2,2,2,16,1024]{4,3,2,1,0:T(8,128)(2,1)S(1)}, bf16[2,2,2,16,1024]{4,3,2,1,0:T(8,128)(2,1)S(1)}, u32[]{:S(2)}, u32[]{:S(2)}) collective-permute-start(bf16[2,2,2,16,1024]{4,3,2,1,0:T(8,128)(2,1)S(1)} %fusion.2), channel_id=1, source_target_pairs={{0,2},{1,5},{2,0},{3,7},{4,6},{5,1},{6,4},{7,3},{8,10},{9,13},{10,... | collective-permute-start | bytes 786440 | tf_op jit(solution)/shard_map/ppermute | solution.py:30
  7.0 6.6 %collective-permute-start.6 = (bf16[2,2,2,16,1024]{4,3,2,1,0:T(8,128)(2,1)S(1)}, bf16[2,2,2,16,1024]{4,3,2,1,0:T(8,128)(2,1)S(1)}, u32[]{:S(2)}, u32[]{:S(2)}) collective-permute-start(bf16[2,2,2,16,1024]{4,3,2,1,0:T(8,128)(2,1)S(1)} %bitcast.59), channel_id=1, source_target_pairs={{0,1},{1,0},{2,3},{3,2},{4,5},{5,4},{6,7},{7,6},{8,9},{9,8},{10,11... | collective-permute-start | bytes 786440 | tf_op jit(solution)/shard_map/ppermute | solution.py:30
  7.1 7.4 %collective-permute-start.8 = (bf16[2,2,2,16,1024]{4,3,2,1,0:T(8,128)(2,1)S(1)}, bf16[2,2,2,16,1024]{4,3,2,1,0:T(8,128)(2,1)S(1)}, u32[]{:S(2)}, u32[]{:S(2)}) collective-permute-start(bf16[2,2,2,16,1024]{4,3,2,1,0:T(8,128)(2,1)S(1)} %fusion), channel_id=1, source_target_pairs={{0,2},{1,5},{2,0},{3,7},{4,6},{5,1},{6,4},{7,3},{8,10},{9,13},{10,... | collective-permute-start | bytes 786440 | tf_op jit(solution)/shard_map/ppermute | solution.py:30
  11.5 5.6 %collective-permute-start.3 = (bf16[2,2,16,1024]{3,2,1,0:T(8,128)(2,1)S(1)}, bf16[2,2,16,1024]{3,2,1,0:T(8,128)(2,1)S(1)}, u32[]{:S(2)}, u32[]{:S(2)}) collective-permute-start(bf16[2,2,16,1024]{3,2,1,0:T(8,128)(2,1)S(1)} %fusion.5), channel_id=1, source_target_pairs={{0,4},{1,3},{2,6},{3,1},{4,0},{5,7},{6,2},{7,5},{8,12},{9,11},{10,... | collective-permute-start | bytes 393224 | tf_op jit(solution)/shard_map/ppermute | solution.py:30
  14.7 15.4 %copy-start.1 = (f32[16,2048]{1,0:T(8,128)S(1)}, f32[16,2048]{1,0:T(8,128)}, u32[]{:S(2)}) copy-start(f32[16,2048]{1,0:T(8,128)} %param.5) | copy-start | bytes 393220
  14.7 15.4 %copy-start.2 = (f32[16,2048]{1,0:T(8,128)S(1)}, f32[16,2048]{1,0:T(8,128)}, u32[]{:S(2)}) copy-start(f32[16,2048]{1,0:T(8,128)} %param.6) | copy-start | bytes 393220
  14.7 15.4 %copy-start.3 = (f32[16,2048]{1,0:T(8,128)S(1)}, f32[16,2048]{1,0:T(8,128)}, u32[]{:S(2)}) copy-start(f32[16,2048]{1,0:T(8,128)} %param.7) | copy-start | bytes 393220
  14.7 5.4 %collective-permute-start.9 = (bf16[2,2,16,1024]{3,2,1,0:T(8,128)(2,1)S(1)}, bf16[2,2,16,1024]{3,2,1,0:T(8,128)(2,1)S(1)}, u32[]{:S(2)}, u32[]{:S(2)}) collective-permute-start(bf16[2,2,16,1024]{3,2,1,0:T(8,128)(2,1)S(1)} %fusion.6), channel_id=1, source_target_pairs={{0,4},{1,3},{2,6},{3,1},{4,0},{5,7},{6,2},{7,5},{8,12},{9,11},{10,... | collective-permute-start | bytes 393224 | tf_op jit(solution)/shard_map/ppermute | solution.py:30
  17.2 5.1 %collective-permute-start.4 = (bf16[2,16,1024]{2,1,0:T(8,128)(2,1)S(1)}, bf16[2,16,1024]{2,1,0:T(8,128)(2,1)S(1)}, u32[]{:S(2)}, u32[]{:S(2)}) collective-permute-start(bf16[2,16,1024]{2,1,0:T(8,128)(2,1)S(1)} %pad_maximum_fusion.2), channel_id=1, source_target_pairs={{0,8},{1,17},{2,10},{3,19},{4,12},{5,21},{6,14},{7,23},{8,0},{9,25... | collective-permute-start | bytes 196616 | tf_op jit(solution)/shard_map/ppermute | solution.py:30
  20.2 4.9 %collective-permute-start.10 = (bf16[2,16,1024]{2,1,0:T(8,128)(2,1)S(1)}, bf16[2,16,1024]{2,1,0:T(8,128)(2,1)S(1)}, u32[]{:S(2)}, u32[]{:S(2)}) collective-permute-start(bf16[2,16,1024]{2,1,0:T(8,128)(2,1)S(1)} %pad_maximum_fusion.3), channel_id=1, source_target_pairs={{0,8},{1,17},{2,10},{3,19},{4,12},{5,21},{6,14},{7,23},{8,0},{9,25... | collective-permute-start | bytes 196616 | tf_op jit(solution)/shard_map/ppermute | solution.py:30
  22.4 5.3 %collective-permute-start.5 = (bf16[16,1024]{1,0:T(8,128)(2,1)S(1)}, bf16[16,1024]{1,0:T(8,128)(2,1)S(1)}, u32[]{:S(2)}, u32[]{:S(2)}) collective-permute-start(bf16[16,1024]{1,0:T(8,128)(2,1)S(1)} %fusion.11), channel_id=1, source_target_pairs={{0,16},{1,9},{2,18},{3,11},{4,20},{5,13},{6,22},{7,15},{8,24},{9,1... | collective-permute-start | bytes 98312 | tf_op jit(solution)/shard_map/ppermute | solution.py:30
  25.1 4.9 %collective-permute-start.11 = (bf16[16,1024]{1,0:T(8,128)(2,1)S(1)}, bf16[16,1024]{1,0:T(8,128)(2,1)S(1)}, u32[]{:S(2)}, u32[]{:S(2)}) collective-permute-start(bf16[16,1024]{1,0:T(8,128)(2,1)S(1)} %fusion.14), channel_id=1, source_target_pairs={{0,16},{1,9},{2,18},{3,11},{4,20},{5,13},{6,22},{7,15},{8,24},{9,1... | collective-permute-start | bytes 98312 | tf_op jit(solution)/shard_map/ppermute | solution.py:30
  30.2 2.6 %collective-permute-start.14 = (bf16[16,2048]{1,0:T(8,128)(2,1)S(1)}, bf16[16,2048]{1,0:T(8,128)(2,1)S(1)}, u32[]{:S(2)}, u32[]{:S(2)}) collective-permute-start(bf16[16,2048]{1,0:T(8,128)(2,1)S(1)} %slice_bitcast_fusion), channel_id=1, source_target_pairs={{0,3},{1,0},{2,1},{3,2},{4,7},{5,4},{6,5},{7,6},{8,11},{9,8},{10,9... | collective-permute-start | bytes 196616 | tf_op jit(solution)/shard_map/ppermute | solution.py:137
  30.3 5.6 %collective-permute-start.13 = (bf16[16,2048]{1,0:T(8,128)(2,1)S(1)}, bf16[16,2048]{1,0:T(8,128)(2,1)S(1)}, u32[]{:S(2)}, u32[]{:S(2)}) collective-permute-start(bf16[16,2048]{1,0:T(8,128)(2,1)S(1)} %slice_bitcast_fusion), channel_id=1, source_target_pairs={{0,2},{1,3},{2,0},{3,1},{4,6},{5,7},{6,4},{7,5},{8,10},{9,11},{10,... | collective-permute-start | bytes 196616 | tf_op jit(solution)/shard_map/ppermute | solution.py:137
  31.9 5.7 %collective-permute-start.12 = (bf16[3,16,2048]{2,1,0:T(8,128)(2,1)S(1)}, bf16[3,16,2048]{2,1,0:T(8,128)(2,1)S(1)}, u32[]{:S(2)}, u32[]{:S(2)}) collective-permute-start(bf16[3,16,2048]{2,1,0:T(8,128)(2,1)S(1)} %pad_maximum_fusion.refs_0_), channel_id=1, source_target_pairs={{0,1},{1,2},{2,3},{3,0},{4,5},{5,6},{6,7},{7,4},{8,9},{9,10},{10,1... | collective-permute-start | bytes 589832 | tf_op jit(solution)/shard_map/ppermute | solution.py:137

commit v3 on v0

v3 whole, which is shorter than its diff:
```python
import jax
import jax.numpy as jnp
from jax import lax
from jax.experimental import pallas as pl
from jax.experimental.pallas import tpu as pltpu
from jax.sharding import PartitionSpec as P

beta_one = 0.9
beta_two = 0.95
learn_rate = 0.01
decay_rate = 0.1
epsilon = 1e-08
step_count = 100
F32 = jnp.float32
BF16 = jnp.bfloat16
BOTH = ("fsdp", "grp")
SHARES = [1, 1]
VMEM = pl.BlockSpec(memory_space=pltpu.VMEM)
ANY = pl.BlockSpec(memory_space=pl.ANY)
HBM = pl.BlockSpec(memory_space=pltpu.HBM)
LIMIT = 4 * 2**20


def swap(x, masks):
    n = lax.axis_size("fsdp") * lax.axis_size("grp")
    return lax.ppermute(x, BOTH, [(i, i ^ masks[i & 1]) for i in range(n)])


def pick(t, index, axis):
    return lax.dynamic_index_in_dim(t, index, axis, keepdims=False)


def updated(gradient, master, moment_one, moment_two):
    new_first = beta_one * moment_one + (1.0 - beta_one) * gradient
    new_second = beta_two * moment_two + (1.0 - beta_two) * gradient * gradient
    first_hat = new_first / (1.0 - beta_one**step_count)
    second_hat = new_second / (1.0 - beta_two**step_count)
    new_master = master - learn_rate * (
        first_hat / (jnp.sqrt(second_hat) + epsilon) + decay_rate * master
    )
    return new_master, new_first, new_second


def cut_up(cols):
    edges = [cols * sum(SHARES[:k]) // sum(SHARES) // 128 * 128 for k in range(len(SHARES))] + [cols]
    return [(a, b - a) for a, b in zip(edges, edges[1:]) if b > a]


def first_block(core, me_f, j, away):
    low, high = me_f & 1, (me_f >> 1) & 1
    return jnp.where(core == 0, low ^ away, j), jnp.where(core == 0, j, high ^ away)


def gathered(g, wanted, cut, rows, nf, ng):
    cols = g.shape[1] // ng
    blocks = g.reshape(nf // 4, 2, 2, rows, g.shape[1])

    def kernel(g_ref, *refs):
        outs, sem = refs[:-1], refs[-1]
        me_f, me_g = lax.axis_index("fsdp"), lax.axis_index("grp")
        moves = []
        for n, (sibling, away) in enumerate(wanted):
            core = (me_g & 1) ^ sibling
            for k, (start, width) in enumerate(cut):
                for j in range(2):
                    low, high = first_block(core, me_f, j, away)
                    for x in range(ng // 2):
                        column = pl.multiple_of((2 * x + core) * cols + start, 128)
                        moves.append(pltpu.make_async_copy(
                            g_ref.at[:, high, low, :, pl.ds(column, width)], outs[n * len(cut) + k].at[j, :, x], sem.at[len(moves)]))
        for m in moves:
            m.start()
        for m in moves:
            m.wait()

    flat = pl.pallas_call(
        kernel,
        out_shape=[jax.ShapeDtypeStruct((2, nf // 4, ng // 2, rows, w), g.dtype) for _ in wanted for _, w in cut],
        in_specs=[HBM],
        out_specs=[VMEM] * (len(wanted) * len(cut)),
        scratch_shapes=[pltpu.SemaphoreType.DMA((ng * len(wanted) * len(cut),))],
        compiler_params=pltpu.CompilerParams(vmem_limit_bytes=LIMIT),
        cost_estimate=pl.CostEstimate(flops=0, bytes_accessed=g.size * len(wanted), transcendentals=0),
    )(blocks)
    return [flat[n * len(cut) : (n + 1) * len(cut)] for n in range(len(wanted))]


def gathered_plain(g, wanted, cut, rows, nf, ng):
    cols = g.shape[1] // ng
    blocks = g.reshape(nf // 4, 2, 2, rows, g.shape[1])
    me_f, me_g = lax.axis_index("fsdp"), lax.axis_index("grp")

    def block(core, away, j, x, start, width):
        low, high = first_block(core, me_f, j, away)
        part = lax.dynamic_slice(blocks, (0, high, low, 0, (2 * x + core) * cols + start), (nf // 4, 1, 1, rows, width))
        return part[:, 0, 0]

    return [
        [jnp.stack([jnp.stack([block((me_g & 1) ^ sibling, away, j, x, a, w) for x in range(ng // 2)], 1) for j in range(2)]) for a, w in cut]
        for sibling, away in wanted
    ]


def finish(own, other, states, near, cols):
    parts, rows = len(own), own[0].shape[1]
    ng = 2 * len(states)
    edges = cut_up(cols)

    def kernel(*refs):
        refs = list(refs)
        take = lambda n: [refs.pop(0) for _ in range(n)]
        own, other, states, near = take(parts), take(parts), take(ng // 2), take(ng // 2)
        outs, weights, copies = take(3), take(1)[0], take(3)
        wide, thin, sem = take(3)
        me = lax.axis_index("grp")
        last = lax.rem(me + ng - 1, ng)
        moves = []

        def move(source, target):
            moves.append(pltpu.make_async_copy(source, target, sem.at[len(moves)]))
            moves[-1].start()

        order = [(0, 0)] + [(k, odd) for odd in (0, 1) for k in range(ng // 2) if k or odd]
        for n, (k, odd) in enumerate(order):
            x = (me >> 1) ^ k
            owner = me ^ (2 * k + odd)
            state = near[k] if odd else states[k]
            for part, (a, w) in zip(other if odd else own, edges):
                new = updated(part[x], *[state[i, :, a : a + w] for i in range(3)])
                thin[n, :, a : a + w] = new[0].astype(BF16)
                if n == 0:
                    for i in range(3):
                        wide[i, :, a : a + w] = new[i]
            if n == 0:
                for i in range(3):
                    move(wide.at[i], outs[i])
            move(thin.at[n], weights.at[:, pl.ds(pl.multiple_of(owner * cols, 128), cols)])
        for k in range(ng // 2):
            @pl.when((me ^ last) >> 1 == k)
            def _():
                for part, (a, w) in zip(other, edges):
                    new = updated(part[last >> 1], *[near[k][i, :, a : a + w] for i in range(3)])
                    for i in range(3):
                        wide[3 + i, :, a : a + w] = new[i]
        for i in range(3):
            move(wide.at[3 + i], copies[i])
        for m in moves:
            m.wait()

    shape = jax.ShapeDtypeStruct((rows, cols), F32)
    return pl.pallas_call(
        kernel,
        out_shape=[shape] * 3 + [jax.ShapeDtypeStruct((rows, cols * ng), BF16)] + [shape] * 3,
        in_specs=[VMEM] * (2 * parts + ng),
        out_specs=[ANY] * 7,
        scratch_shapes=[pltpu.VMEM((6, rows, cols), F32), pltpu.VMEM((ng, rows, cols), BF16), pltpu.SemaphoreType.DMA((ng + 6,))],
        compiler_params=pltpu.CompilerParams(vmem_limit_bytes=LIMIT),
    )(*own, *other, *states, *near)


def finish_plain(own, other, states, near, cols):
    me = lax.axis_index("grp")
    own, other = jnp.concatenate(own, -1), jnp.concatenate(other, -1)
    ng = 2 * len(states)
    weights = jnp.zeros((own.shape[1], cols * ng), BF16)
    last = (me + ng - 1) % ng
    for k in range(ng // 2):
        for odd, grad, state in ((0, own, states[k]), (1, other, near[k])):
            new = updated(pick(grad, (me >> 1) ^ k, 0), *state)
            owner = me ^ (2 * k + odd)
            weights = lax.dynamic_update_slice(weights, new[0].astype(BF16), (0, owner * cols))
            if k == 0 and odd == 0:
                mine = new
            if odd:
                copies = new if k == 0 else [jnp.where(owner == last, a, b) for a, b in zip(new, copies)]
    return (*mine, weights, *copies)


def shards(grads, master, moment_one, moment_two):
    ng, nf = lax.axis_size("grp"), lax.axis_size("fsdp")
    g_bits, f_bits = ng.bit_length() - 1, nf.bit_length() - 1
    me_f, me_g = lax.axis_index("fsdp"), lax.axis_index("grp")
    core = me_g & 1
    g = grads[0, 0]
    rows, cols = g.shape[0] // nf, g.shape[1] // ng
    cut = cut_up(cols)
    local = rows % 16 == 0 and cols % 128 == 0

    gather = gathered if local else gathered_plain
    (away_out,) = gather(g, [(1, 1)], cut, rows, nf, ng)
    kept_out, away_own, kept_own = gather(g, [(1, 0), (0, 1), (0, 0)], cut, rows, nf, ng)
    split = lambda t: t.reshape((2,) * (f_bits - 1) + t.shape[2:])
    got_away = [split(swap(t, [1, 1])) for t in away_out]
    got_kept = [split(swap(t, [1, 1])) for t in kept_out]
    sent = [(split(t).astype(F32) + x.astype(F32)).astype(BF16) for t, x in zip(away_own, got_away)]
    kept = [split(t).astype(F32) + x.astype(F32) for t, x in zip(kept_own, got_kept)]

    high = list(range(f_bits - 1, 1, -1))
    labels = [[1] + high, [0] + high]
    orders = [[0, 1, 2], [1, 2, 0]]
    orders = [o + [b for b in range(f_bits) if b not in o] for o in orders]
    for step in range(f_bits):
        masks = [ng << o[step] for o in orders]
        if step == 0:
            sent[-1], held = lax.optimization_barrier((sent[-1], (master, moment_one, moment_two)))
            states = [jnp.stack(held)]
            for b in range(1, g_bits):
                states = states + [swap(s, [1 << b] * 2) for s in states]
        got = [swap(s, masks) for s in sent]

        ts = [k + x.astype(F32) for k, x in zip(kept, got)]
        if step == f_bits - 1:
            break
        want = [o[step + 1] for o in orders]
        a, b = [l.index(w) for l, w in zip(labels, want)]
        bit = [(me_f >> w) & 1 for w in want]

        def choose(t, j, away):
            if a == b:
                return pick(t, jnp.where(core == 0, bit[0], bit[1]) ^ away, a)
            at = {a: jnp.where(core == 0, bit[0] ^ away, j), b: jnp.where(core == 0, j, bit[1] ^ away)}
            return pick(pick(t, at[max(a, b)], max(a, b)), at[min(a, b)], min(a, b))

        def chosen(t, away):
            return choose(t, 0, away) if a == b else jnp.stack([choose(t, j, away) for j in range(2)])

        sent = [chosen(t, 1).astype(BF16) for t in ts]
        kept = [chosen(t, 0) for t in ts]
        rest = [[x for i, x in enumerate(l) if i not in (a, b)] for l in labels]
        labels = rest if a == b else [[labels[0][b]] + rest[0], [labels[1][a]] + rest[1]]

    for b in range(1, g_bits):
        rounded = [t.astype(BF16) for t in ts]
        if b == g_bits - 1:
            rounded, states = lax.optimization_barrier((rounded, states))
            near = [swap(s, [1, 1]) for s in states]

        got = [swap(t, [1 << b] * 2) for t in rounded]
        ts = [t.astype(F32) + x.astype(F32) for t, x in zip(rounded, got)]
    own = [t / (ng * nf) for t in ts]
    other = [swap(t, [1, 1]) for t in own]
    return (finish if local else finish_plain)(own, other, states, near, cols)


def solution(mesh):
    return jax.shard_map(
        shards,
        mesh=mesh,
        in_specs=(P("grp", "fsdp", None, None), P("fsdp", "grp"), P("fsdp", "grp"), P("fsdp", "grp")),
        out_specs=(P("fsdp", "grp"), P("fsdp", "grp"), P("fsdp", "grp"), P("fsdp", None), P("fsdp", "grp"), P("fsdp", "grp"), P("fsdp", "grp")),
        check_vma=False,
    )
```

time: 132 us -> 35.2 us (0.27)
  waiting for transfers between devices: 103 us -> 10.7 us
  starting transfers between devices: 1.78 us -> 18.7 us
  between operations: 14.1 us -> 0.85 us
  blocking collectives: 7.44 us -> 0 us
  other arithmetic: 3.15 us -> 0.54 us
  Pallas kernels: 0 us -> 2.47 us
    reduce_scatter x2 -> x0, waiting for transfers between devices: 102 us -> none  [the longest x1 65.2 us: shards(): lax.psum_scatter(column_share, 'fsdp', scatter_dimension=0, tiled=True)]
    ppermute x3 -> x17, starting transfers between devices: 1.7 us -> 18.7 us  [swap(): return lax.ppermute(x, BOTH, [(i, i ^ masks[i & 1]) for i in range(n)])]
    ppermute x3 -> x17, waiting for transfers between devices: 0.01 us -> 10.7 us  [swap(): return lax.ppermute(x, BOTH, [(i, i ^ masks[i & 1]) for i in range(n)])]
    all_gather x1 -> x0, blocking collectives: 7.44 us -> none  [shards(): lax.all_gather(new_master.astype(jnp.bfloat16), 'grp', axis=1, tiled=True)]
    convert_element_type x2 -> x4, other arithmetic: 3.15 us -> 0.16 us  [the longest x2 0.13 us: shards(): (split(t).astype(F32) + x.astype(F32)).astype(BF16)]
    pallas_call x0 -> x3, Pallas kernels: none -> 2.47 us  [the longest x1 1.36 us: finish(): pl.pallas_call(kernel, out_shape=[shape] * 3 + [jax.ShapeDtypeStruct((row...]
    unnamed x16 -> x8, local copies, waits for them, and re-layouts: 2.7 us -> 1.6 us
  transfers between devices with their start and end apart: 5 -> 17, of which waited for: 2 -> 8; matrix products, arithmetic and copies ran while one was open for 0% -> 2% of each run, Pallas kernels for 0% -> 2%
where the time goes in v3:
time: 35.2 us; the launch traced here: 35 us
  starting transfers between devices  18.7 us (53%)
  waiting for transfers between devices  10.7 us (30%)
  Pallas kernels  2.47 us (7%)
  local copies, waits for them, and re-layouts  1.74 us (5%)
  between operations  0.85 us (2%)
  other arithmetic  0.54 us (2%)
    ppermute x17, starting transfers between devices, swap(): return lax.ppermute(x, BOTH, [(i, i ^ masks[i & 1]) for i in range(n)])  18.7 us
    ppermute x17, waiting for transfers between devices, swap(): return lax.ppermute(x, BOTH, [(i, i ^ masks[i & 1]) for i in range(n)])  10.7 us
    unnamed x8, local copies, waits for them, and re-layouts  1.6 us
    pallas_call x1, Pallas kernels, finish(): pl.pallas_call(kernel, out_shape=[shape] * 3 + [jax.ShapeDtypeStruct((row...  1.36 us
    pallas_call x2, Pallas kernels, gathered(): pl.pallas_call(kernel, out_shape=[jax.ShapeDtypeStruct((2, nf // 4, ng //...  1.11 us
  transfers between devices with their start and end apart: 17, of which 8 were waited for; matrix products, arithmetic and copies ran while one was open for 2% of the time, Pallas kernels for 2%

profile of v3, /device:TPU:0, one launch (start us, length us, event | category | flops | bytes accessed | tf_op | source)
XLA Modules:
  0.0 35.0 jit_solution(3631641883883038663)
XLA Ops:
  0.6 0.0 copy-start
  0.6 1.6 %copy-done = bf16[1,1,128,8192]{3,2,1,0:T(8,128)(2,1)S(1)} copy-done((bf16[1,1,128,8192]{3,2,1,0:T(8,128)(2,1)S(1)}, bf16[1,1,128,8192]{3,2,1,0:T(8,128)(2,1)}, u32[]{:S(2)}) %copy-start) | copy-done | bytes 2097176
  2.2 0.3 shard_map.100
  2.5 0.0 copy-start.1
  2.5 0.0 copy-start.2
  2.5 0.0 copy-start.3
  2.5 0.5 %collective-permute-start.1 = (bf16[2,2,2,16,1024]{4,3,2,1,0:T(8,128)(2,1)S(1)}, bf16[2,2,2,16,1024]{4,3,2,1,0:T(8,128)(2,1)S(1)}, u32[]{:S(2)}, u32[]{:S(2)}) collective-permute-start(bf16[2,2,2,16,1024]{4,3,2,1,0:T(8,128)(2,1)S(1)} %get-tuple-element.26), channel_id=1, source_target_pairs={{0,1},{1,0},{2,3},{3,2},{4,5},{5,4},{6,7},{7,6},{8,9},{9,8},{10,11... | collective-permute-start | bytes 786440 | tf_op jit(solution)/shard_map/ppermute | solution.py:26
  3.0 0.1 collective-permute-start.6
  3.1 0.9 %shard_map.99 = (bf16[2,2,2,16,1024]{4,3,2,1,0:T(8,128)(2,1)S(1)}, bf16[2,2,2,16,1024]{4,3,2,1,0:T(8,128)(2,1)S(1)}, bf16[2,2,2,16,1024]{4,3,2,1,0:T(8,128)(2,1)...) custom-call(bf16[2,2,2,16,8192]{4,3,2,1,0:T(8,128)(2,1)S(1)} %bitcast.33), custom_call_target="tpu_custom_call" | custom-call | bytes 3145728 | tf_op jit(solution)/shard_map/pallas_call | solution.py:76
  4.0 0.5 %collective-permute-start = (bf16[2,2,2,16,1024]{4,3,2,1,0:T(8,128)(2,1)S(1)}, bf16[2,2,2,16,1024]{4,3,2,1,0:T(8,128)(2,1)S(1)}, u32[]{:S(2)}, u32[]{:S(2)}) collective-permute-start(bf16[2,2,2,16,1024]{4,3,2,1,0:T(8,128)(2,1)S(1)} %get-tuple-element.24), channel_id=1, source_target_pairs={{0,1},{1,0},{2,3},{3,2},{4,5},{5,4},{6,7},{7,6},{8,9},{9,8},{10,11... | collective-permute-start | bytes 786440 | tf_op jit(solution)/shard_map/ppermute | solution.py:26
  4.5 0.1 collective-permute-start.5
  4.6 0.0 collective-permute-done.1
  4.6 0.1 add_convert_fusion.1
  4.6 3.0 %collective-permute-start.2 = (bf16[2,2,2,16,1024]{4,3,2,1,0:T(8,128)(2,1)S(1)}, bf16[2,2,2,16,1024]{4,3,2,1,0:T(8,128)(2,1)S(1)}, u32[]{:S(2)}, u32[]{:S(2)}) collective-permute-start(bf16[2,2,2,16,1024]{4,3,2,1,0:T(8,128)(2,1)S(1)} %add_convert_fusion.1), channel_id=1, source_target_pairs={{0,4},{1,9},{2,6},{3,11},{4,0},{5,13},{6,2},{7,15},{8,12},{9,1},{1... | collective-permute-start | bytes 786440 | tf_op jit(solution)/shard_map/ppermute | solution.py:26
  7.6 0.0 collective-permute-done.6
  7.6 0.1 add_convert_fusion
  7.7 0.1 collective-permute-start.7
  7.8 0.0 copy-done.1
  7.8 0.0 copy-done.2
  7.8 0.0 copy-done.3
  7.9 2.0 %collective-permute-start.10 = (f32[3,16,2048]{2,1,0:T(8,128)S(1)}, f32[3,16,2048]{2,1,0:T(8,128)S(1)}, u32[]{:S(2)}, u32[]{:S(2)}) collective-permute-start(f32[3,16,2048]{2,1,0:T(8,128)S(1)} %pad_maximum_fusion.refs_4_), channel_id=1, source_target_pairs={{0,2},{1,3},{2,0},{3,1},{4,6},{5,7},{6,4},{7,5},{8,10},{9,11},{10,... | collective-permute-start | bytes 1179656 | tf_op jit(solution)/shard_map/ppermute | solution.py:26
  9.9 0.0 collective-permute-done
  9.9 2.1 %collective-permute-done.2 = bf16[2,2,2,16,1024]{4,3,2,1,0:T(8,128)(2,1)S(1)} collective-permute-done((bf16[2,2,2,16,1024]{4,3,2,1,0:T(8,128)(2,1)S(1)}, bf16[2,2,2,16,1024]{4,3,2,1,0:T(8,128)(2,1)S(1)}, u32[]{:S(2)}, u32[]{:S(2)}) %collective-permute-start.2) | collective-permute-done | bytes 262176 | tf_op jit(solution)/shard_map/ppermute | solution.py:26
  12.0 0.1 convert_add_fusion.1
  12.2 2.1 %collective-permute-start.3 = (bf16[2,2,16,1024]{3,2,1,0:T(8,128)(2,1)S(1)}, bf16[2,2,16,1024]{3,2,1,0:T(8,128)(2,1)S(1)}, u32[]{:S(2)}, u32[]{:S(2)}) collective-permute-start(bf16[2,2,16,1024]{3,2,1,0:T(8,128)(2,1)S(1)} %pad_maximum_fusion.1), channel_id=1, source_target_pairs={{0,8},{1,17},{2,10},{3,19},{4,12},{5,21},{6,14},{7,23},{8,0},{9,25... | collective-permute-start | bytes 393224 | tf_op jit(solution)/shard_map/ppermute | solution.py:26
  14.3 0.0 collective-permute-done.5
  14.3 0.5 %collective-permute-done.7 = bf16[2,2,2,16,1024]{4,3,2,1,0:T(8,128)(2,1)S(1)} collective-permute-done((bf16[2,2,2,16,1024]{4,3,2,1,0:T(8,128)(2,1)S(1)}, bf16[2,2,2,16,1024]{4,3,2,1,0:T(8,128)(2,1)S(1)}, u32[]{:S(2)}, u32[]{:S(2)}) %collective-permute-start.7) | collective-permute-done | bytes 262176 | tf_op jit(solution)/shard_map/ppermute | solution.py:26
  14.8 0.1 convert_add_fusion
  15.0 2.1 %collective-permute-start.8 = (bf16[2,2,16,1024]{3,2,1,0:T(8,128)(2,1)S(1)}, bf16[2,2,16,1024]{3,2,1,0:T(8,128)(2,1)S(1)}, u32[]{:S(2)}, u32[]{:S(2)}) collective-permute-start(bf16[2,2,16,1024]{3,2,1,0:T(8,128)(2,1)S(1)} %pad_maximum_fusion.2), channel_id=1, source_target_pairs={{0,8},{1,17},{2,10},{3,19},{4,12},{5,21},{6,14},{7,23},{8,0},{9,25... | collective-permute-start | bytes 393224 | tf_op jit(solution)/shard_map/ppermute | solution.py:26
  17.2 0.8 %collective-permute-done.3 = bf16[2,2,16,1024]{3,2,1,0:T(8,128)(2,1)S(1)} collective-permute-done((bf16[2,2,16,1024]{3,2,1,0:T(8,128)(2,1)S(1)}, bf16[2,2,16,1024]{3,2,1,0:T(8,128)(2,1)S(1)}, u32[]{:S(2)}, u32[]{:S(2)}) %collective-permute-start.3) | collective-permute-done | bytes 131104 | tf_op jit(solution)/shard_map/ppermute | solution.py:26
  18.0 2.9 %collective-permute-start.4 = (bf16[2,16,1024]{2,1,0:T(8,128)(2,1)S(1)}, bf16[2,16,1024]{2,1,0:T(8,128)(2,1)S(1)}, u32[]{:S(2)}, u32[]{:S(2)}) collective-permute-start(bf16[2,16,1024]{2,1,0:T(8,128)(2,1)S(1)} %fusion.4), channel_id=1, source_target_pairs={{0,16},{1,5},{2,18},{3,7},{4,20},{5,1},{6,22},{7,3},{8,24},{9,13},... | collective-permute-start | bytes 196616 | tf_op jit(solution)/shard_map/ppermute | solution.py:26
  20.9 0.1 collective-permute-done.8
  21.1 2.5 %collective-permute-start.9 = (bf16[2,16,1024]{2,1,0:T(8,128)(2,1)S(1)}, bf16[2,16,1024]{2,1,0:T(8,128)(2,1)S(1)}, u32[]{:S(2)}, u32[]{:S(2)}) collective-permute-start(bf16[2,16,1024]{2,1,0:T(8,128)(2,1)S(1)} %fusion.7), channel_id=1, source_target_pairs={{0,16},{1,5},{2,18},{3,7},{4,20},{5,1},{6,22},{7,3},{8,24},{9,13},... | collective-permute-start | bytes 196616 | tf_op jit(solution)/shard_map/ppermute | solution.py:26
  23.6 0.0 collective-permute-done.4
  23.6 2.7 %collective-permute-done.9 = bf16[2,16,1024]{2,1,0:T(8,128)(2,1)S(1)} collective-permute-done((bf16[2,16,1024]{2,1,0:T(8,128)(2,1)S(1)}, bf16[2,16,1024]{2,1,0:T(8,128)(2,1)S(1)}, u32[]{:S(2)}, u32[]{:S(2)}) %collective-permute-start.9) | collective-permute-done | bytes 65568 | tf_op jit(solution)/shard_map/ppermute | solution.py:26
  26.3 0.0 collective-permute-done.10.refs_5_
  26.3 1.6 %collective-permute-start.12 = (bf16[2,16,1024]{2,1,0:T(8,128)(2,1)S(1)}, bf16[2,16,1024]{2,1,0:T(8,128)(2,1)S(1)}, u32[]{:S(2)}, u32[]{:S(2)}) collective-permute-start(bf16[2,16,1024]{2,1,0:T(8,128)(2,1)S(1)} %fusion), channel_id=1, source_target_pairs={{0,2},{1,3},{2,0},{3,1},{4,6},{5,7},{6,4},{7,5},{8,10},{9,11},{10,... | collective-permute-start | bytes 196616 | tf_op jit(solution)/shard_map/ppermute | solution.py:26
  27.9 0.5 %collective-permute-start.11 = (bf16[2,16,1024]{2,1,0:T(8,128)(2,1)S(1)}, bf16[2,16,1024]{2,1,0:T(8,128)(2,1)S(1)}, u32[]{:S(2)}, u32[]{:S(2)}) collective-permute-start(bf16[2,16,1024]{2,1,0:T(8,128)(2,1)S(1)} %fusion.1), channel_id=1, source_target_pairs={{0,2},{1,3},{2,0},{3,1},{4,6},{5,7},{6,4},{7,5},{8,10},{9,11},{10,... | collective-permute-start | bytes 196616 | tf_op jit(solution)/shard_map/ppermute | solution.py:26
  28.4 0.0 collective-permute-start.15
  28.4 0.5 %collective-permute-start.16 = (f32[3,16,2048]{2,1,0:T(8,128)S(1)}, f32[3,16,2048]{2,1,0:T(8,128)S(1)}, u32[]{:S(2)}, u32[]{:S(2)}) collective-permute-start(f32[3,16,2048]{2,1,0:T(8,128)S(1)} %collective-permute-done.10.refs_5_), channel_id=1, source_target_pairs={{0,1},{1,0},{2,3},{3,2},{4,5},{5,4},{6,7},{7,6},{8,9},{9,8},{10,11... | collective-permute-start | bytes 1179656 | tf_op jit(solution)/shard_map/ppermute | solution.py:26
  28.9 1.7 %collective-permute-done.12 = bf16[2,16,1024]{2,1,0:T(8,128)(2,1)S(1)} collective-permute-done((bf16[2,16,1024]{2,1,0:T(8,128)(2,1)S(1)}, bf16[2,16,1024]{2,1,0:T(8,128)(2,1)S(1)}, u32[]{:S(2)}, u32[]{:S(2)}) %collective-permute-start.12) | collective-permute-done | bytes 65568 | tf_op jit(solution)/shard_map/ppermute | solution.py:26
  30.7 0.1 collective-permute-start.14
  30.8 1.4 %collective-permute-done.11 = bf16[2,16,1024]{2,1,0:T(8,128)(2,1)S(1)} collective-permute-done((bf16[2,16,1024]{2,1,0:T(8,128)(2,1)S(1)}, bf16[2,16,1024]{2,1,0:T(8,128)(2,1)S(1)}, u32[]{:S(2)}, u32[]{:S(2)}) %collective-permute-start.11) | collective-permute-done | bytes 65568 | tf_op jit(solution)/shard_map/ppermute | solution.py:26
  32.2 0.1 collective-permute-start.13
  32.3 0.0 collective-permute-done.14.refs_3_
  32.3 1.3 %collective-permute-done.13.refs_2_ = f32[2,16,1024]{2,1,0:T(8,128)S(1)} collective-permute-done((f32[2,16,1024]{2,1,0:T(8,128)S(1)}, f32[2,16,1024]{2,1,0:T(8,128)S(1)}, u32[]{:S(2)}, u32[]{:S(2)}) %collective-permute-start.13) | collective-permute-done | bytes 131104 | tf_op jit(solution)/shard_map/ppermute | solution.py:26
  33.6 0.0 collective-permute-done.15.refs_6_
  33.7 0.0 collective-permute-done.16.refs_7_
  33.7 1.4 %shard_map.101 = (f32[16,2048]{1,0:T(8,128)}, f32[16,2048]{1,0:T(8,128)}, f32[16,2048]{1,0:T(8,128)}, bf16[16,8192]{1,0:T(8,128)(2,1)}, f32[16,2048]{1,0:T(8,128...) custom-call(f32[2,16,1024]{2,1,0:T(8,128)S(1)} %add_multiply_fusion.1.refs_0_, f32[2,16,1024]{2,1,0:T(8,128)S(1)} %add_multiply_fusion.refs_1_, ...), custom_call_target="tpu_custom_call" | custom-call | tf_op jit(solution)/shard_map/pallas_call | solution.py:151
  (15 shorter events, 0.3 us)
Async XLA Ops:
  0.6 1.6 %copy-start = (bf16[1,1,128,8192]{3,2,1,0:T(8,128)(2,1)S(1)}, bf16[1,1,128,8192]{3,2,1,0:T(8,128)(2,1)}, u32[]{:S(2)}) copy-start(bf16[1,1,128,8192]{3,2,1,0:T(8,128)(2,1)} %param.4) | copy-start | bytes 6291460
  2.5 5.3 %copy-start.1 = (f32[16,2048]{1,0:T(8,128)S(1)}, f32[16,2048]{1,0:T(8,128)}, u32[]{:S(2)}) copy-start(f32[16,2048]{1,0:T(8,128)} %param.7) | copy-start | bytes 393220
  2.5 5.3 %copy-start.2 = (f32[16,2048]{1,0:T(8,128)S(1)}, f32[16,2048]{1,0:T(8,128)}, u32[]{:S(2)}) copy-start(f32[16,2048]{1,0:T(8,128)} %param.6) | copy-start | bytes 393220
  2.5 5.3 %copy-start.3 = (f32[16,2048]{1,0:T(8,128)S(1)}, f32[16,2048]{1,0:T(8,128)}, u32[]{:S(2)}) copy-start(f32[16,2048]{1,0:T(8,128)} %param.5) | copy-start | bytes 393220
  2.5 2.0 %collective-permute-start.1 = (bf16[2,2,2,16,1024]{4,3,2,1,0:T(8,128)(2,1)S(1)}, bf16[2,2,2,16,1024]{4,3,2,1,0:T(8,128)(2,1)S(1)}, u32[]{:S(2)}, u32[]{:S(2)}) collective-permute-start(bf16[2,2,2,16,1024]{4,3,2,1,0:T(8,128)(2,1)S(1)} %get-tuple-element.26), channel_id=1, source_target_pairs={{0,1},{1,0},{2,3},{3,2},{4,5},{5,4},{6,7},{7,6},{8,9},{9,8},{10,11... | collective-permute-start | bytes 786440 | tf_op jit(solution)/shard_map/ppermute | solution.py:26
  3.0 4.6 %collective-permute-start.6 = (bf16[2,2,2,16,1024]{4,3,2,1,0:T(8,128)(2,1)S(1)}, bf16[2,2,2,16,1024]{4,3,2,1,0:T(8,128)(2,1)S(1)}, u32[]{:S(2)}, u32[]{:S(2)}) collective-permute-start(bf16[2,2,2,16,1024]{4,3,2,1,0:T(8,128)(2,1)S(1)} %get-tuple-element.30), channel_id=1, source_target_pairs={{0,1},{1,0},{2,3},{3,2},{4,5},{5,4},{6,7},{7,6},{8,9},{9,8},{10,11... | collective-permute-start | bytes 786440 | tf_op jit(solution)/shard_map/ppermute | solution.py:26
  4.0 5.9 %collective-permute-start = (bf16[2,2,2,16,1024]{4,3,2,1,0:T(8,128)(2,1)S(1)}, bf16[2,2,2,16,1024]{4,3,2,1,0:T(8,128)(2,1)S(1)}, u32[]{:S(2)}, u32[]{:S(2)}) collective-permute-start(bf16[2,2,2,16,1024]{4,3,2,1,0:T(8,128)(2,1)S(1)} %get-tuple-element.24), channel_id=1, source_target_pairs={{0,1},{1,0},{2,3},{3,2},{4,5},{5,4},{6,7},{7,6},{8,9},{9,8},{10,11... | collective-permute-start | bytes 786440 | tf_op jit(solution)/shard_map/ppermute | solution.py:26
  4.5 9.8 %collective-permute-start.5 = (bf16[2,2,2,16,1024]{4,3,2,1,0:T(8,128)(2,1)S(1)}, bf16[2,2,2,16,1024]{4,3,2,1,0:T(8,128)(2,1)S(1)}, u32[]{:S(2)}, u32[]{:S(2)}) collective-permute-start(bf16[2,2,2,16,1024]{4,3,2,1,0:T(8,128)(2,1)S(1)} %get-tuple-element.28), channel_id=1, source_target_pairs={{0,1},{1,0},{2,3},{3,2},{4,5},{5,4},{6,7},{7,6},{8,9},{9,8},{10,11... | collective-permute-start | bytes 786440 | tf_op jit(solution)/shard_map/ppermute | solution.py:26
  4.6 7.4 %collective-permute-start.2 = (bf16[2,2,2,16,1024]{4,3,2,1,0:T(8,128)(2,1)S(1)}, bf16[2,2,2,16,1024]{4,3,2,1,0:T(8,128)(2,1)S(1)}, u32[]{:S(2)}, u32[]{:S(2)}) collective-permute-start(bf16[2,2,2,16,1024]{4,3,2,1,0:T(8,128)(2,1)S(1)} %add_convert_fusion.1), channel_id=1, source_target_pairs={{0,4},{1,9},{2,6},{3,11},{4,0},{5,13},{6,2},{7,15},{8,12},{9,1},{1... | collective-permute-start | bytes 786440 | tf_op jit(solution)/shard_map/ppermute | solution.py:26
  7.7 7.1 %collective-permute-start.7 = (bf16[2,2,2,16,1024]{4,3,2,1,0:T(8,128)(2,1)S(1)}, bf16[2,2,2,16,1024]{4,3,2,1,0:T(8,128)(2,1)S(1)}, u32[]{:S(2)}, u32[]{:S(2)}) collective-permute-start(bf16[2,2,2,16,1024]{4,3,2,1,0:T(8,128)(2,1)S(1)} %add_convert_fusion), channel_id=1, source_target_pairs={{0,4},{1,9},{2,6},{3,11},{4,0},{5,13},{6,2},{7,15},{8,12},{9,1},{1... | collective-permute-start | bytes 786440 | tf_op jit(solution)/shard_map/ppermute | solution.py:26
  7.9 18.5 %collective-permute-start.10 = (f32[3,16,2048]{2,1,0:T(8,128)S(1)}, f32[3,16,2048]{2,1,0:T(8,128)S(1)}, u32[]{:S(2)}, u32[]{:S(2)}) collective-permute-start(f32[3,16,2048]{2,1,0:T(8,128)S(1)} %pad_maximum_fusion.refs_4_), channel_id=1, source_target_pairs={{0,2},{1,3},{2,0},{3,1},{4,6},{5,7},{6,4},{7,5},{8,10},{9,11},{10,... | collective-permute-start | bytes 1179656 | tf_op jit(solution)/shard_map/ppermute | solution.py:26
  12.2 5.8 %collective-permute-start.3 = (bf16[2,2,16,1024]{3,2,1,0:T(8,128)(2,1)S(1)}, bf16[2,2,16,1024]{3,2,1,0:T(8,128)(2,1)S(1)}, u32[]{:S(2)}, u32[]{:S(2)}) collective-permute-start(bf16[2,2,16,1024]{3,2,1,0:T(8,128)(2,1)S(1)} %pad_maximum_fusion.1), channel_id=1, source_target_pairs={{0,8},{1,17},{2,10},{3,19},{4,12},{5,21},{6,14},{7,23},{8,0},{9,25... | collective-permute-start | bytes 393224 | tf_op jit(solution)/shard_map/ppermute | solution.py:26
  15.0 6.0 %collective-permute-start.8 = (bf16[2,2,16,1024]{3,2,1,0:T(8,128)(2,1)S(1)}, bf16[2,2,16,1024]{3,2,1,0:T(8,128)(2,1)S(1)}, u32[]{:S(2)}, u32[]{:S(2)}) collective-permute-start(bf16[2,2,16,1024]{3,2,1,0:T(8,128)(2,1)S(1)} %pad_maximum_fusion.2), channel_id=1, source_target_pairs={{0,8},{1,17},{2,10},{3,19},{4,12},{5,21},{6,14},{7,23},{8,0},{9,25... | collective-permute-start | bytes 393224 | tf_op jit(solution)/shard_map/ppermute | solution.py:26
  18.0 5.6 %collective-permute-start.4 = (bf16[2,16,1024]{2,1,0:T(8,128)(2,1)S(1)}, bf16[2,16,1024]{2,1,0:T(8,128)(2,1)S(1)}, u32[]{:S(2)}, u32[]{:S(2)}) collective-permute-start(bf16[2,16,1024]{2,1,0:T(8,128)(2,1)S(1)} %fusion.4), channel_id=1, source_target_pairs={{0,16},{1,5},{2,18},{3,7},{4,20},{5,1},{6,22},{7,3},{8,24},{9,13},... | collective-permute-start | bytes 196616 | tf_op jit(solution)/shard_map/ppermute | solution.py:26
  21.1 5.2 %collective-permute-start.9 = (bf16[2,16,1024]{2,1,0:T(8,128)(2,1)S(1)}, bf16[2,16,1024]{2,1,0:T(8,128)(2,1)S(1)}, u32[]{:S(2)}, u32[]{:S(2)}) collective-permute-start(bf16[2,16,1024]{2,1,0:T(8,128)(2,1)S(1)} %fusion.7), channel_id=1, source_target_pairs={{0,16},{1,5},{2,18},{3,7},{4,20},{5,1},{6,22},{7,3},{8,24},{9,13},... | collective-permute-start | bytes 196616 | tf_op jit(solution)/shard_map/ppermute | solution.py:26
  26.3 4.3 %collective-permute-start.12 = (bf16[2,16,1024]{2,1,0:T(8,128)(2,1)S(1)}, bf16[2,16,1024]{2,1,0:T(8,128)(2,1)S(1)}, u32[]{:S(2)}, u32[]{:S(2)}) collective-permute-start(bf16[2,16,1024]{2,1,0:T(8,128)(2,1)S(1)} %fusion), channel_id=1, source_target_pairs={{0,2},{1,3},{2,0},{3,1},{4,6},{5,7},{6,4},{7,5},{8,10},{9,11},{10,... | collective-permute-start | bytes 196616 | tf_op jit(solution)/shard_map/ppermute | solution.py:26
  27.9 4.3 %collective-permute-start.11 = (bf16[2,16,1024]{2,1,0:T(8,128)(2,1)S(1)}, bf16[2,16,1024]{2,1,0:T(8,128)(2,1)S(1)}, u32[]{:S(2)}, u32[]{:S(2)}) collective-permute-start(bf16[2,16,1024]{2,1,0:T(8,128)(2,1)S(1)} %fusion.1), channel_id=1, source_target_pairs={{0,2},{1,3},{2,0},{3,1},{4,6},{5,7},{6,4},{7,5},{8,10},{9,11},{10,... | collective-permute-start | bytes 196616 | tf_op jit(solution)/shard_map/ppermute | solution.py:26
  28.4 5.2 %collective-permute-start.15 = (f32[3,16,2048]{2,1,0:T(8,128)S(1)}, f32[3,16,2048]{2,1,0:T(8,128)S(1)}, u32[]{:S(2)}, u32[]{:S(2)}) collective-permute-start(f32[3,16,2048]{2,1,0:T(8,128)S(1)} %pad_maximum_fusion.refs_4_), channel_id=1, source_target_pairs={{0,1},{1,0},{2,3},{3,2},{4,5},{5,4},{6,7},{7,6},{8,9},{9,8},{10,11... | collective-permute-start | bytes 1179656 | tf_op jit(solution)/shard_map/ppermute | solution.py:26
  28.4 5.2 %collective-permute-start.16 = (f32[3,16,2048]{2,1,0:T(8,128)S(1)}, f32[3,16,2048]{2,1,0:T(8,128)S(1)}, u32[]{:S(2)}, u32[]{:S(2)}) collective-permute-start(f32[3,16,2048]{2,1,0:T(8,128)S(1)} %collective-permute-done.10.refs_5_), channel_id=1, source_target_pairs={{0,1},{1,0},{2,3},{3,2},{4,5},{5,4},{6,7},{7,6},{8,9},{9,8},{10,11... | collective-permute-start | bytes 1179656 | tf_op jit(solution)/shard_map/ppermute | solution.py:26
  30.7 1.6 %collective-permute-start.14 = (f32[2,16,1024]{2,1,0:T(8,128)S(1)}, f32[2,16,1024]{2,1,0:T(8,128)S(1)}, u32[]{:S(2)}, u32[]{:S(2)}) collective-permute-start(f32[2,16,1024]{2,1,0:T(8,128)S(1)} %add_multiply_fusion.refs_1_), channel_id=1, source_target_pairs={{0,1},{1,0},{2,3},{3,2},{4,5},{5,4},{6,7},{7,6},{8,9},{9,8},{10,11... | collective-permute-start | bytes 393224 | tf_op jit(solution)/shard_map/ppermute | solution.py:26
  32.2 1.4 %collective-permute-start.13 = (f32[2,16,1024]{2,1,0:T(8,128)S(1)}, f32[2,16,1024]{2,1,0:T(8,128)S(1)}, u32[]{:S(2)}, u32[]{:S(2)}) collective-permute-start(f32[2,16,1024]{2,1,0:T(8,128)S(1)} %add_multiply_fusion.1.refs_0_), channel_id=1, source_target_pairs={{0,1},{1,0},{2,3},{3,2},{4,5},{5,4},{6,7},{7,6},{8,9},{9,8},{10,11... | collective-permute-start | bytes 393224 | tf_op jit(solution)/shard_map/ppermute | solution.py:26

commit v4 on v3

--- a/solution.py
+++ b/solution.py
@@ -18,6 +18,7 @@
 VMEM = pl.BlockSpec(memory_space=pltpu.VMEM)
 ANY = pl.BlockSpec(memory_space=pl.ANY)
 HBM = pl.BlockSpec(memory_space=pltpu.HBM)
+GLIMIT = 32 * 2**17
 LIMIT = 4 * 2**20
 
 
@@ -79,7 +80,7 @@
         in_specs=[HBM],
         out_specs=[VMEM] * (len(wanted) * len(cut)),
         scratch_shapes=[pltpu.SemaphoreType.DMA((ng * len(wanted) * len(cut),))],
-        compiler_params=pltpu.CompilerParams(vmem_limit_bytes=LIMIT),
+        compiler_params=pltpu.CompilerParams(vmem_limit_bytes=GLIMIT),
         cost_estimate=pl.CostEstimate(flops=0, bytes_accessed=g.size * len(wanted), transcendentals=0),
     )(blocks)
     return [flat[n * len(cut) : (n + 1) * len(cut)] for n in range(len(wanted))]
@@ -232,7 +233,7 @@
     for b in range(1, g_bits):
         rounded = [t.astype(BF16) for t in ts]
         if b == g_bits - 1:
-            rounded, states = lax.optimization_barrier((rounded, states))
+            rounded[-1], states = lax.optimization_barrier((rounded[-1], states))
             near = [swap(s, [1, 1]) for s in states]
 
         got = [swap(t, [1 << b] * 2) for t in rounded]

time: 35.2 us -> 33.6 us (0.955)
  waiting for transfers between devices: 10.7 us -> 8.11 us
  starting transfers between devices: 18.7 us -> 19.8 us
    ppermute x17, waiting for transfers between devices: 10.7 us -> 8.11 us  [swap(): return lax.ppermute(x, BOTH, [(i, i ^ masks[i & 1]) for i in range(n)])]
    ppermute x17, starting transfers between devices: 18.7 us -> 19.8 us  [swap(): return lax.ppermute(x, BOTH, [(i, i ^ masks[i & 1]) for i in range(n)])]
  transfers between devices with their start and end apart: 17 -> 17, of which waited for: 8 -> 7; matrix products, arithmetic and copies ran while one was open for 2% -> 2% of each run, Pallas kernels for 2% -> 3%
where the time goes in v4:
time: 33.6 us; the launch traced here: 33.5 us
  starting transfers between devices  19.8 us (59%)
  waiting for transfers between devices  8.11 us (24%)
  Pallas kernels  2.47 us (7%)
  local copies, waits for them, and re-layouts  1.74 us (5%)
  between operations  0.85 us (3%)
  other arithmetic  0.54 us (2%)
    ppermute x17, starting transfers between devices, swap(): return lax.ppermute(x, BOTH, [(i, i ^ masks[i & 1]) for i in range(n)])  19.8 us
    ppermute x17, waiting for transfers between devices, swap(): return lax.ppermute(x, BOTH, [(i, i ^ masks[i & 1]) for i in range(n)])  8.11 us
    unnamed x8, local copies, waits for them, and re-layouts  1.6 us
    pallas_call x1, Pallas kernels, finish(): pl.pallas_call(kernel, out_shape=[shape] * 3 + [jax.ShapeDtypeStruct((row...  1.36 us
    pallas_call x2, Pallas kernels, gathered(): pl.pallas_call(kernel, out_shape=[jax.ShapeDtypeStruct((2, nf // 4, ng //...  1.11 us
  transfers between devices with their start and end apart: 17, of which 7 were waited for; matrix products, arithmetic and copies ran while one was open for 2% of the time, Pallas kernels for 3%

profile of v4, /device:TPU:0, one launch (start us, length us, event | category | flops | bytes accessed | tf_op | source)
XLA Modules:
  0.0 33.5 jit_solution(8624104170061971164)
XLA Ops:
  0.6 0.0 copy-start
  0.6 1.6 %copy-done = bf16[1,1,128,8192]{3,2,1,0:T(8,128)(2,1)S(1)} copy-done((bf16[1,1,128,8192]{3,2,1,0:T(8,128)(2,1)S(1)}, bf16[1,1,128,8192]{3,2,1,0:T(8,128)(2,1)}, u32[]{:S(2)}) %copy-start) | copy-done | bytes 2097176
  2.2 0.3 shard_map.100
  2.5 0.0 copy-start.1
  2.5 0.0 copy-start.2
  2.5 0.0 copy-start.3
  2.5 0.5 %collective-permute-start.1 = (bf16[2,2,2,16,1024]{4,3,2,1,0:T(8,128)(2,1)S(1)}, bf16[2,2,2,16,1024]{4,3,2,1,0:T(8,128)(2,1)S(1)}, u32[]{:S(2)}, u32[]{:S(2)}) collective-permute-start(bf16[2,2,2,16,1024]{4,3,2,1,0:T(8,128)(2,1)S(1)} %get-tuple-element.25), channel_id=1, source_target_pairs={{0,1},{1,0},{2,3},{3,2},{4,5},{5,4},{6,7},{7,6},{8,9},{9,8},{10,11... | collective-permute-start | bytes 786440 | tf_op jit(solution)/shard_map/ppermute | solution.py:27
  3.0 0.1 collective-permute-start.7
  3.1 0.9 %shard_map.99 = (bf16[2,2,2,16,1024]{4,3,2,1,0:T(8,128)(2,1)S(1)}, bf16[2,2,2,16,1024]{4,3,2,1,0:T(8,128)(2,1)S(1)}, bf16[2,2,2,16,1024]{4,3,2,1,0:T(8,128)(2,1)...) custom-call(bf16[2,2,2,16,8192]{4,3,2,1,0:T(8,128)(2,1)S(1)} %bitcast.33), custom_call_target="tpu_custom_call" | custom-call | bytes 3145728 | tf_op jit(solution)/shard_map/pallas_call | solution.py:77
  4.0 0.5 %collective-permute-start = (bf16[2,2,2,16,1024]{4,3,2,1,0:T(8,128)(2,1)S(1)}, bf16[2,2,2,16,1024]{4,3,2,1,0:T(8,128)(2,1)S(1)}, u32[]{:S(2)}, u32[]{:S(2)}) collective-permute-start(bf16[2,2,2,16,1024]{4,3,2,1,0:T(8,128)(2,1)S(1)} %get-tuple-element.23), channel_id=1, source_target_pairs={{0,1},{1,0},{2,3},{3,2},{4,5},{5,4},{6,7},{7,6},{8,9},{9,8},{10,11... | collective-permute-start | bytes 786440 | tf_op jit(solution)/shard_map/ppermute | solution.py:27
  4.5 0.1 collective-permute-start.6
  4.6 0.0 collective-permute-done.1
  4.6 0.1 add_convert_fusion.1
  4.6 3.0 %collective-permute-start.2 = (bf16[2,2,2,16,1024]{4,3,2,1,0:T(8,128)(2,1)S(1)}, bf16[2,2,2,16,1024]{4,3,2,1,0:T(8,128)(2,1)S(1)}, u32[]{:S(2)}, u32[]{:S(2)}) collective-permute-start(bf16[2,2,2,16,1024]{4,3,2,1,0:T(8,128)(2,1)S(1)} %add_convert_fusion.1), channel_id=1, source_target_pairs={{0,4},{1,9},{2,6},{3,11},{4,0},{5,13},{6,2},{7,15},{8,12},{9,1},{1... | collective-permute-start | bytes 786440 | tf_op jit(solution)/shard_map/ppermute | solution.py:27
  7.6 0.0 collective-permute-done.7
  7.6 0.1 add_convert_fusion
  7.7 0.1 collective-permute-start.8
  7.8 0.0 copy-done.1
  7.8 0.0 copy-done.2
  7.8 0.0 copy-done.3
  7.9 2.0 %collective-permute-start.11 = (f32[3,16,2048]{2,1,0:T(8,128)S(1)}, f32[3,16,2048]{2,1,0:T(8,128)S(1)}, u32[]{:S(2)}, u32[]{:S(2)}) collective-permute-start(f32[3,16,2048]{2,1,0:T(8,128)S(1)} %pad_maximum_fusion.refs_4_), channel_id=1, source_target_pairs={{0,2},{1,3},{2,0},{3,1},{4,6},{5,7},{6,4},{7,5},{8,10},{9,11},{10,... | collective-permute-start | bytes 1179656 | tf_op jit(solution)/shard_map/ppermute | solution.py:27
  9.9 0.0 collective-permute-done
  9.9 2.1 %collective-permute-done.2 = bf16[2,2,2,16,1024]{4,3,2,1,0:T(8,128)(2,1)S(1)} collective-permute-done((bf16[2,2,2,16,1024]{4,3,2,1,0:T(8,128)(2,1)S(1)}, bf16[2,2,2,16,1024]{4,3,2,1,0:T(8,128)(2,1)S(1)}, u32[]{:S(2)}, u32[]{:S(2)}) %collective-permute-start.2) | collective-permute-done | bytes 262176 | tf_op jit(solution)/shard_map/ppermute | solution.py:27
  12.0 0.1 convert_add_fusion.1
  12.2 2.1 %collective-permute-start.3 = (bf16[2,2,16,1024]{3,2,1,0:T(8,128)(2,1)S(1)}, bf16[2,2,16,1024]{3,2,1,0:T(8,128)(2,1)S(1)}, u32[]{:S(2)}, u32[]{:S(2)}) collective-permute-start(bf16[2,2,16,1024]{3,2,1,0:T(8,128)(2,1)S(1)} %pad_maximum_fusion.1), channel_id=1, source_target_pairs={{0,8},{1,17},{2,10},{3,19},{4,12},{5,21},{6,14},{7,23},{8,0},{9,25... | collective-permute-start | bytes 393224 | tf_op jit(solution)/shard_map/ppermute | solution.py:27
  14.3 0.0 collective-permute-done.6
  14.3 0.5 %collective-permute-done.8 = bf16[2,2,2,16,1024]{4,3,2,1,0:T(8,128)(2,1)S(1)} collective-permute-done((bf16[2,2,2,16,1024]{4,3,2,1,0:T(8,128)(2,1)S(1)}, bf16[2,2,2,16,1024]{4,3,2,1,0:T(8,128)(2,1)S(1)}, u32[]{:S(2)}, u32[]{:S(2)}) %collective-permute-start.8) | collective-permute-done | bytes 262176 | tf_op jit(solution)/shard_map/ppermute | solution.py:27
  14.8 0.1 convert_add_fusion
  15.0 2.1 %collective-permute-start.9 = (bf16[2,2,16,1024]{3,2,1,0:T(8,128)(2,1)S(1)}, bf16[2,2,16,1024]{3,2,1,0:T(8,128)(2,1)S(1)}, u32[]{:S(2)}, u32[]{:S(2)}) collective-permute-start(bf16[2,2,16,1024]{3,2,1,0:T(8,128)(2,1)S(1)} %pad_maximum_fusion.2), channel_id=1, source_target_pairs={{0,8},{1,17},{2,10},{3,19},{4,12},{5,21},{6,14},{7,23},{8,0},{9,25... | collective-permute-start | bytes 393224 | tf_op jit(solution)/shard_map/ppermute | solution.py:27
  17.2 0.8 %collective-permute-done.3 = bf16[2,2,16,1024]{3,2,1,0:T(8,128)(2,1)S(1)} collective-permute-done((bf16[2,2,16,1024]{3,2,1,0:T(8,128)(2,1)S(1)}, bf16[2,2,16,1024]{3,2,1,0:T(8,128)(2,1)S(1)}, u32[]{:S(2)}, u32[]{:S(2)}) %collective-permute-start.3) | collective-permute-done | bytes 131104 | tf_op jit(solution)/shard_map/ppermute | solution.py:27
  18.0 2.9 %collective-permute-start.4 = (bf16[2,16,1024]{2,1,0:T(8,128)(2,1)S(1)}, bf16[2,16,1024]{2,1,0:T(8,128)(2,1)S(1)}, u32[]{:S(2)}, u32[]{:S(2)}) collective-permute-start(bf16[2,16,1024]{2,1,0:T(8,128)(2,1)S(1)} %fusion.4), channel_id=1, source_target_pairs={{0,16},{1,5},{2,18},{3,7},{4,20},{5,1},{6,22},{7,3},{8,24},{9,13},... | collective-permute-start | bytes 196616 | tf_op jit(solution)/shard_map/ppermute | solution.py:27
  20.9 0.1 collective-permute-done.9
  21.1 2.5 %collective-permute-start.10 = (bf16[2,16,1024]{2,1,0:T(8,128)(2,1)S(1)}, bf16[2,16,1024]{2,1,0:T(8,128)(2,1)S(1)}, u32[]{:S(2)}, u32[]{:S(2)}) collective-permute-start(bf16[2,16,1024]{2,1,0:T(8,128)(2,1)S(1)} %fusion.7), channel_id=1, source_target_pairs={{0,16},{1,5},{2,18},{3,7},{4,20},{5,1},{6,22},{7,3},{8,24},{9,13},... | collective-permute-start | bytes 196616 | tf_op jit(solution)/shard_map/ppermute | solution.py:27
  23.6 0.0 collective-permute-done.4
  23.6 1.6 %collective-permute-start.5 = (bf16[2,16,1024]{2,1,0:T(8,128)(2,1)S(1)}, bf16[2,16,1024]{2,1,0:T(8,128)(2,1)S(1)}, u32[]{:S(2)}, u32[]{:S(2)}) collective-permute-start(bf16[2,16,1024]{2,1,0:T(8,128)(2,1)S(1)} %fusion.1), channel_id=1, source_target_pairs={{0,2},{1,3},{2,0},{3,1},{4,6},{5,7},{6,4},{7,5},{8,10},{9,11},{10,... | collective-permute-start | bytes 196616 | tf_op jit(solution)/shard_map/ppermute | solution.py:27
  25.2 1.1 %collective-permute-done.10 = bf16[2,16,1024]{2,1,0:T(8,128)(2,1)S(1)} collective-permute-done((bf16[2,16,1024]{2,1,0:T(8,128)(2,1)S(1)}, bf16[2,16,1024]{2,1,0:T(8,128)(2,1)S(1)}, u32[]{:S(2)}, u32[]{:S(2)}) %collective-permute-start.10) | collective-permute-done | bytes 65568 | tf_op jit(solution)/shard_map/ppermute | solution.py:27
  26.3 0.0 collective-permute-done.11.refs_5_
  26.3 1.6 %collective-permute-start.12 = (bf16[2,16,1024]{2,1,0:T(8,128)(2,1)S(1)}, bf16[2,16,1024]{2,1,0:T(8,128)(2,1)S(1)}, u32[]{:S(2)}, u32[]{:S(2)}) collective-permute-start(bf16[2,16,1024]{2,1,0:T(8,128)(2,1)S(1)} %fusion), channel_id=1, source_target_pairs={{0,2},{1,3},{2,0},{3,1},{4,6},{5,7},{6,4},{7,5},{8,10},{9,11},{10,... | collective-permute-start | bytes 196616 | tf_op jit(solution)/shard_map/ppermute | solution.py:27
  27.9 0.0 collective-permute-start.15
  27.9 0.5 %collective-permute-start.16 = (f32[3,16,2048]{2,1,0:T(8,128)S(1)}, f32[3,16,2048]{2,1,0:T(8,128)S(1)}, u32[]{:S(2)}, u32[]{:S(2)}) collective-permute-start(f32[3,16,2048]{2,1,0:T(8,128)S(1)} %collective-permute-done.11.refs_5_), channel_id=1, source_target_pairs={{0,1},{1,0},{2,3},{3,2},{4,5},{5,4},{6,7},{7,6},{8,9},{9,8},{10,11... | collective-permute-start | bytes 1179656 | tf_op jit(solution)/shard_map/ppermute | solution.py:27
  28.5 0.0 collective-permute-done.5
  28.5 0.1 collective-permute-start.13
  28.6 2.1 %collective-permute-done.12 = bf16[2,16,1024]{2,1,0:T(8,128)(2,1)S(1)} collective-permute-done((bf16[2,16,1024]{2,1,0:T(8,128)(2,1)S(1)}, bf16[2,16,1024]{2,1,0:T(8,128)(2,1)S(1)}, u32[]{:S(2)}, u32[]{:S(2)}) %collective-permute-start.12) | collective-permute-done | bytes 65568 | tf_op jit(solution)/shard_map/ppermute | solution.py:27
  30.7 0.1 collective-permute-start.14
  30.8 0.0 collective-permute-done.13.refs_2_
  30.8 1.3 %collective-permute-done.14.refs_3_ = f32[2,16,1024]{2,1,0:T(8,128)S(1)} collective-permute-done((f32[2,16,1024]{2,1,0:T(8,128)S(1)}, f32[2,16,1024]{2,1,0:T(8,128)S(1)}, u32[]{:S(2)}, u32[]{:S(2)}) %collective-permute-start.14) | collective-permute-done | bytes 131104 | tf_op jit(solution)/shard_map/ppermute | solution.py:27
  32.1 0.0 collective-permute-done.15.refs_6_
  32.1 0.0 collective-permute-done.16.refs_7_
  32.1 1.4 %shard_map.101 = (f32[16,2048]{1,0:T(8,128)}, f32[16,2048]{1,0:T(8,128)}, f32[16,2048]{1,0:T(8,128)}, bf16[16,8192]{1,0:T(8,128)(2,1)}, f32[16,2048]{1,0:T(8,128...) custom-call(f32[2,16,1024]{2,1,0:T(8,128)S(1)} %add_multiply_fusion.1.refs_0_, f32[2,16,1024]{2,1,0:T(8,128)S(1)} %add_multiply_fusion.refs_1_, ...), custom_call_target="tpu_custom_call" | custom-call | tf_op jit(solution)/shard_map/pallas_call | solution.py:152
  (15 shorter events, 0.3 us)
Async XLA Ops:
  0.6 1.6 %copy-start = (bf16[1,1,128,8192]{3,2,1,0:T(8,128)(2,1)S(1)}, bf16[1,1,128,8192]{3,2,1,0:T(8,128)(2,1)}, u32[]{:S(2)}) copy-start(bf16[1,1,128,8192]{3,2,1,0:T(8,128)(2,1)} %param.4) | copy-start | bytes 6291460
  2.5 5.3 %copy-start.1 = (f32[16,2048]{1,0:T(8,128)S(1)}, f32[16,2048]{1,0:T(8,128)}, u32[]{:S(2)}) copy-start(f32[16,2048]{1,0:T(8,128)} %param.7) | copy-start | bytes 393220
  2.5 5.3 %copy-start.2 = (f32[16,2048]{1,0:T(8,128)S(1)}, f32[16,2048]{1,0:T(8,128)}, u32[]{:S(2)}) copy-start(f32[16,2048]{1,0:T(8,128)} %param.6) | copy-start | bytes 393220
  2.5 5.3 %copy-start.3 = (f32[16,2048]{1,0:T(8,128)S(1)}, f32[16,2048]{1,0:T(8,128)}, u32[]{:S(2)}) copy-start(f32[16,2048]{1,0:T(8,128)} %param.5) | copy-start | bytes 393220
  2.5 2.0 %collective-permute-start.1 = (bf16[2,2,2,16,1024]{4,3,2,1,0:T(8,128)(2,1)S(1)}, bf16[2,2,2,16,1024]{4,3,2,1,0:T(8,128)(2,1)S(1)}, u32[]{:S(2)}, u32[]{:S(2)}) collective-permute-start(bf16[2,2,2,16,1024]{4,3,2,1,0:T(8,128)(2,1)S(1)} %get-tuple-element.25), channel_id=1, source_target_pairs={{0,1},{1,0},{2,3},{3,2},{4,5},{5,4},{6,7},{7,6},{8,9},{9,8},{10,11... | collective-permute-start | bytes 786440 | tf_op jit(solution)/shard_map/ppermute | solution.py:27
  3.0 4.6 %collective-permute-start.7 = (bf16[2,2,2,16,1024]{4,3,2,1,0:T(8,128)(2,1)S(1)}, bf16[2,2,2,16,1024]{4,3,2,1,0:T(8,128)(2,1)S(1)}, u32[]{:S(2)}, u32[]{:S(2)}) collective-permute-start(bf16[2,2,2,16,1024]{4,3,2,1,0:T(8,128)(2,1)S(1)} %get-tuple-element.29), channel_id=1, source_target_pairs={{0,1},{1,0},{2,3},{3,2},{4,5},{5,4},{6,7},{7,6},{8,9},{9,8},{10,11... | collective-permute-start | bytes 786440 | tf_op jit(solution)/shard_map/ppermute | solution.py:27
  4.0 5.9 %collective-permute-start = (bf16[2,2,2,16,1024]{4,3,2,1,0:T(8,128)(2,1)S(1)}, bf16[2,2,2,16,1024]{4,3,2,1,0:T(8,128)(2,1)S(1)}, u32[]{:S(2)}, u32[]{:S(2)}) collective-permute-start(bf16[2,2,2,16,1024]{4,3,2,1,0:T(8,128)(2,1)S(1)} %get-tuple-element.23), channel_id=1, source_target_pairs={{0,1},{1,0},{2,3},{3,2},{4,5},{5,4},{6,7},{7,6},{8,9},{9,8},{10,11... | collective-permute-start | bytes 786440 | tf_op jit(solution)/shard_map/ppermute | solution.py:27
  4.5 9.8 %collective-permute-start.6 = (bf16[2,2,2,16,1024]{4,3,2,1,0:T(8,128)(2,1)S(1)}, bf16[2,2,2,16,1024]{4,3,2,1,0:T(8,128)(2,1)S(1)}, u32[]{:S(2)}, u32[]{:S(2)}) collective-permute-start(bf16[2,2,2,16,1024]{4,3,2,1,0:T(8,128)(2,1)S(1)} %get-tuple-element.27), channel_id=1, source_target_pairs={{0,1},{1,0},{2,3},{3,2},{4,5},{5,4},{6,7},{7,6},{8,9},{9,8},{10,11... | collective-permute-start | bytes 786440 | tf_op jit(solution)/shard_map/ppermute | solution.py:27
  4.6 7.4 %collective-permute-start.2 = (bf16[2,2,2,16,1024]{4,3,2,1,0:T(8,128)(2,1)S(1)}, bf16[2,2,2,16,1024]{4,3,2,1,0:T(8,128)(2,1)S(1)}, u32[]{:S(2)}, u32[]{:S(2)}) collective-permute-start(bf16[2,2,2,16,1024]{4,3,2,1,0:T(8,128)(2,1)S(1)} %add_convert_fusion.1), channel_id=1, source_target_pairs={{0,4},{1,9},{2,6},{3,11},{4,0},{5,13},{6,2},{7,15},{8,12},{9,1},{1... | collective-permute-start | bytes 786440 | tf_op jit(solution)/shard_map/ppermute | solution.py:27
  7.7 7.1 %collective-permute-start.8 = (bf16[2,2,2,16,1024]{4,3,2,1,0:T(8,128)(2,1)S(1)}, bf16[2,2,2,16,1024]{4,3,2,1,0:T(8,128)(2,1)S(1)}, u32[]{:S(2)}, u32[]{:S(2)}) collective-permute-start(bf16[2,2,2,16,1024]{4,3,2,1,0:T(8,128)(2,1)S(1)} %add_convert_fusion), channel_id=1, source_target_pairs={{0,4},{1,9},{2,6},{3,11},{4,0},{5,13},{6,2},{7,15},{8,12},{9,1},{1... | collective-permute-start | bytes 786440 | tf_op jit(solution)/shard_map/ppermute | solution.py:27
  7.9 18.5 %collective-permute-start.11 = (f32[3,16,2048]{2,1,0:T(8,128)S(1)}, f32[3,16,2048]{2,1,0:T(8,128)S(1)}, u32[]{:S(2)}, u32[]{:S(2)}) collective-permute-start(f32[3,16,2048]{2,1,0:T(8,128)S(1)} %pad_maximum_fusion.refs_4_), channel_id=1, source_target_pairs={{0,2},{1,3},{2,0},{3,1},{4,6},{5,7},{6,4},{7,5},{8,10},{9,11},{10,... | collective-permute-start | bytes 1179656 | tf_op jit(solution)/shard_map/ppermute | solution.py:27
  12.2 5.8 %collective-permute-start.3 = (bf16[2,2,16,1024]{3,2,1,0:T(8,128)(2,1)S(1)}, bf16[2,2,16,1024]{3,2,1,0:T(8,128)(2,1)S(1)}, u32[]{:S(2)}, u32[]{:S(2)}) collective-permute-start(bf16[2,2,16,1024]{3,2,1,0:T(8,128)(2,1)S(1)} %pad_maximum_fusion.1), channel_id=1, source_target_pairs={{0,8},{1,17},{2,10},{3,19},{4,12},{5,21},{6,14},{7,23},{8,0},{9,25... | collective-permute-start | bytes 393224 | tf_op jit(solution)/shard_map/ppermute | solution.py:27
  15.0 6.0 %collective-permute-start.9 = (bf16[2,2,16,1024]{3,2,1,0:T(8,128)(2,1)S(1)}, bf16[2,2,16,1024]{3,2,1,0:T(8,128)(2,1)S(1)}, u32[]{:S(2)}, u32[]{:S(2)}) collective-permute-start(bf16[2,2,16,1024]{3,2,1,0:T(8,128)(2,1)S(1)} %pad_maximum_fusion.2), channel_id=1, source_target_pairs={{0,8},{1,17},{2,10},{3,19},{4,12},{5,21},{6,14},{7,23},{8,0},{9,25... | collective-permute-start | bytes 393224 | tf_op jit(solution)/shard_map/ppermute | solution.py:27
  18.0 5.6 %collective-permute-start.4 = (bf16[2,16,1024]{2,1,0:T(8,128)(2,1)S(1)}, bf16[2,16,1024]{2,1,0:T(8,128)(2,1)S(1)}, u32[]{:S(2)}, u32[]{:S(2)}) collective-permute-start(bf16[2,16,1024]{2,1,0:T(8,128)(2,1)S(1)} %fusion.4), channel_id=1, source_target_pairs={{0,16},{1,5},{2,18},{3,7},{4,20},{5,1},{6,22},{7,3},{8,24},{9,13},... | collective-permute-start | bytes 196616 | tf_op jit(solution)/shard_map/ppermute | solution.py:27
  21.1 5.2 %collective-permute-start.10 = (bf16[2,16,1024]{2,1,0:T(8,128)(2,1)S(1)}, bf16[2,16,1024]{2,1,0:T(8,128)(2,1)S(1)}, u32[]{:S(2)}, u32[]{:S(2)}) collective-permute-start(bf16[2,16,1024]{2,1,0:T(8,128)(2,1)S(1)} %fusion.7), channel_id=1, source_target_pairs={{0,16},{1,5},{2,18},{3,7},{4,20},{5,1},{6,22},{7,3},{8,24},{9,13},... | collective-permute-start | bytes 196616 | tf_op jit(solution)/shard_map/ppermute | solution.py:27
  23.6 4.8 %collective-permute-start.5 = (bf16[2,16,1024]{2,1,0:T(8,128)(2,1)S(1)}, bf16[2,16,1024]{2,1,0:T(8,128)(2,1)S(1)}, u32[]{:S(2)}, u32[]{:S(2)}) collective-permute-start(bf16[2,16,1024]{2,1,0:T(8,128)(2,1)S(1)} %fusion.1), channel_id=1, source_target_pairs={{0,2},{1,3},{2,0},{3,1},{4,6},{5,7},{6,4},{7,5},{8,10},{9,11},{10,... | collective-permute-start | bytes 196616 | tf_op jit(solution)/shard_map/ppermute | solution.py:27
  26.3 4.3 %collective-permute-start.12 = (bf16[2,16,1024]{2,1,0:T(8,128)(2,1)S(1)}, bf16[2,16,1024]{2,1,0:T(8,128)(2,1)S(1)}, u32[]{:S(2)}, u32[]{:S(2)}) collective-permute-start(bf16[2,16,1024]{2,1,0:T(8,128)(2,1)S(1)} %fusion), channel_id=1, source_target_pairs={{0,2},{1,3},{2,0},{3,1},{4,6},{5,7},{6,4},{7,5},{8,10},{9,11},{10,... | collective-permute-start | bytes 196616 | tf_op jit(solution)/shard_map/ppermute | solution.py:27
  27.9 4.2 %collective-permute-start.15 = (f32[3,16,2048]{2,1,0:T(8,128)S(1)}, f32[3,16,2048]{2,1,0:T(8,128)S(1)}, u32[]{:S(2)}, u32[]{:S(2)}) collective-permute-start(f32[3,16,2048]{2,1,0:T(8,128)S(1)} %pad_maximum_fusion.refs_4_), channel_id=1, source_target_pairs={{0,1},{1,0},{2,3},{3,2},{4,5},{5,4},{6,7},{7,6},{8,9},{9,8},{10,11... | collective-permute-start | bytes 1179656 | tf_op jit(solution)/shard_map/ppermute | solution.py:27
  27.9 4.2 %collective-permute-start.16 = (f32[3,16,2048]{2,1,0:T(8,128)S(1)}, f32[3,16,2048]{2,1,0:T(8,128)S(1)}, u32[]{:S(2)}, u32[]{:S(2)}) collective-permute-start(f32[3,16,2048]{2,1,0:T(8,128)S(1)} %collective-permute-done.11.refs_5_), channel_id=1, source_target_pairs={{0,1},{1,0},{2,3},{3,2},{4,5},{5,4},{6,7},{7,6},{8,9},{9,8},{10,11... | collective-permute-start | bytes 1179656 | tf_op jit(solution)/shard_map/ppermute | solution.py:27
  28.5 2.3 %collective-permute-start.13 = (f32[2,16,1024]{2,1,0:T(8,128)S(1)}, f32[2,16,1024]{2,1,0:T(8,128)S(1)}, u32[]{:S(2)}, u32[]{:S(2)}) collective-permute-start(f32[2,16,1024]{2,1,0:T(8,128)S(1)} %add_multiply_fusion.1.refs_0_), channel_id=1, source_target_pairs={{0,1},{1,0},{2,3},{3,2},{4,5},{5,4},{6,7},{7,6},{8,9},{9,8},{10,11... | collective-permute-start | bytes 393224 | tf_op jit(solution)/shard_map/ppermute | solution.py:27
  30.7 1.4 %collective-permute-start.14 = (f32[2,16,1024]{2,1,0:T(8,128)S(1)}, f32[2,16,1024]{2,1,0:T(8,128)S(1)}, u32[]{:S(2)}, u32[]{:S(2)}) collective-permute-start(f32[2,16,1024]{2,1,0:T(8,128)S(1)} %add_multiply_fusion.refs_1_), channel_id=1, source_target_pairs={{0,1},{1,0},{2,3},{3,2},{4,5},{5,4},{6,7},{7,6},{8,9},{9,8},{10,11... | collective-permute-start | bytes 393224 | tf_op jit(solution)/shard_map/ppermute | solution.py:27

commit v5 on v4

--- a/solution.py
+++ b/solution.py
@@ -1,3 +1,5 @@
+import functools
+
 import jax
 import jax.numpy as jnp
 from jax import lax
@@ -15,6 +17,7 @@
 BF16 = jnp.bfloat16
 BOTH = ("fsdp", "grp")
 SHARES = [1, 1]
+ROLES = 0
 VMEM = pl.BlockSpec(memory_space=pltpu.VMEM)
 ANY = pl.BlockSpec(memory_space=pl.ANY)
 HBM = pl.BlockSpec(memory_space=pltpu.HBM)
@@ -52,7 +55,11 @@
     return jnp.where(core == 0, low ^ away, j), jnp.where(core == 0, j, high ^ away)
 
 
-def gathered(g, wanted, cut, rows, nf, ng):
+def role(k):
+    return ROLES * (k % 2)
+
+
+def gathered(g, wanted, cut, rows, nf, ng, limit):
     cols = g.shape[1] // ng
     blocks = g.reshape(nf // 4, 2, 2, rows, g.shape[1])
 
@@ -64,7 +71,7 @@
             core = (me_g & 1) ^ sibling
             for k, (start, width) in enumerate(cut):
                 for j in range(2):
-                    low, high = first_block(core, me_f, j, away)
+                    low, high = first_block(core ^ role(k), me_f, j, away)
                     for x in range(ng // 2):
                         column = pl.multiple_of((2 * x + core) * cols + start, 128)
                         moves.append(pltpu.make_async_copy(
@@ -80,24 +87,24 @@
         in_specs=[HBM],
         out_specs=[VMEM] * (len(wanted) * len(cut)),
         scratch_shapes=[pltpu.SemaphoreType.DMA((ng * len(wanted) * len(cut),))],
-        compiler_params=pltpu.CompilerParams(vmem_limit_bytes=GLIMIT),
+        compiler_params=pltpu.CompilerParams(vmem_limit_bytes=limit),
         cost_estimate=pl.CostEstimate(flops=0, bytes_accessed=g.size * len(wanted), transcendentals=0),
     )(blocks)
-    return [flat[n * len(cut) : (n + 1) * len(cut)] for n in range(len(wanted))]
-
-
-def gathered_plain(g, wanted, cut, rows, nf, ng):
+    return [list(flat[n * len(cut) : (n + 1) * len(cut)]) for n in range(len(wanted))]
+
+
+def gathered_plain(g, wanted, cut, rows, nf, ng, limit):
     cols = g.shape[1] // ng
     blocks = g.reshape(nf // 4, 2, 2, rows, g.shape[1])
     me_f, me_g = lax.axis_index("fsdp"), lax.axis_index("grp")
 
-    def block(core, away, j, x, start, width):
-        low, high = first_block(core, me_f, j, away)
+    def block(core, k, away, j, x, start, width):
+        low, high = first_block(core ^ role(k), me_f, j, away)
         part = lax.dynamic_slice(blocks, (0, high, low, 0, (2 * x + core) * cols + start), (nf // 4, 1, 1, rows, width))
         return part[:, 0, 0]
 
     return [
-        [jnp.stack([jnp.stack([block((me_g & 1) ^ sibling, away, j, x, a, w) for x in range(ng // 2)], 1) for j in range(2)]) for a, w in cut]
+        [jnp.stack([jnp.stack([block((me_g & 1) ^ sibling, k, away, j, x, a, w) for x in range(ng // 2)], 1) for j in range(2)]) for k, (a, w) in enumerate(cut)]
         for sibling, away in wanted
     ]
 
@@ -107,11 +114,17 @@
     ng = 2 * len(states)
     edges = cut_up(cols)
 
-    def kernel(*refs):
+    def kernel(first, *refs):
         refs = list(refs)
         take = lambda n: [refs.pop(0) for _ in range(n)]
-        own, other, states, near = take(parts), take(parts), take(ng // 2), take(ng // 2)
-        outs, weights, copies = take(3), take(1)[0], take(3)
+        own = take(parts) if first else []
+        other = dict(zip(range(parts - 1) if first else [parts - 1], take(parts - 1 if first else 1)))
+        states, near = take(ng // 2) if first else [], take(ng // 2)
+        if first:
+            outs = take(3)
+        else:
+            take(4)
+        weights, copies = take(1)[0], take(3)
         wide, thin, sem = take(3)
         me = lax.axis_index("grp")
         last = lax.rem(me + ng - 1, ng)
@@ -121,42 +134,61 @@
             moves.append(pltpu.make_async_copy(source, target, sem.at[len(moves)]))
             moves[-1].start()
 
-        order = [(0, 0)] + [(k, odd) for odd in (0, 1) for k in range(ng // 2) if k or odd]
-        for n, (k, odd) in enumerate(order):
-            x = (me >> 1) ^ k
-            owner = me ^ (2 * k + odd)
-            state = near[k] if odd else states[k]
-            for part, (a, w) in zip(other if odd else own, edges):
-                new = updated(part[x], *[state[i, :, a : a + w] for i in range(3)])
-                thin[n, :, a : a + w] = new[0].astype(BF16)
-                if n == 0:
-                    for i in range(3):
-                        wide[i, :, a : a + w] = new[i]
-            if n == 0:
+        def block(n, part, state, x, edge, keep):
+            start, width = edge
+            new = updated(part[x], *[state[i, :, start : start + width] for i in range(3)])
+            thin[n, :, start : start + width] = new[0].astype(BF16)
+            if keep:
+                for i in range(3):
+                    wide[i, :, start : start + width] = new[i]
+
+        for k in range(len(states)):
+            for part, edge in zip(own, edges):
+                block(2 * k, part, states[k], (me >> 1) ^ k, edge, k == 0)
+            if k == 0:
                 for i in range(3):
                     move(wide.at[i], outs[i])
-            move(thin.at[n], weights.at[:, pl.ds(pl.multiple_of(owner * cols, 128), cols)])
-        for k in range(ng // 2):
-            @pl.when((me ^ last) >> 1 == k)
-            def _():
-                for part, (a, w) in zip(other, edges):
-                    new = updated(part[last >> 1], *[near[k][i, :, a : a + w] for i in range(3)])
+            move(thin.at[2 * k], weights.at[:, pl.ds(pl.multiple_of((me ^ (2 * k)) * cols, 128), cols)])
+        for index, part in other.items():
+            start, width = edges[index]
+            here = pl.ds(start, width)
+            for k in range(ng // 2):
+                @pl.when((me ^ last) >> 1 == k)
+                def _():
+                    new = updated(part[last >> 1], *[near[k][i, :, start : start + width] for i in range(3)])
                     for i in range(3):
-                        wide[3 + i, :, a : a + w] = new[i]
-        for i in range(3):
-            move(wide.at[3 + i], copies[i])
+                        wide[3 + i, :, start : start + width] = new[i]
+            for i in range(3):
+                move(wide.at[3 + i, :, here], copies[i].at[:, here])
+            for k in range(ng // 2):
+                block(2 * k + 1, part, near[k], (me >> 1) ^ k, edges[index], False)
+                column = pl.multiple_of((me ^ (2 * k + 1)) * cols + start, 128)
+                move(thin.at[2 * k + 1, :, here], weights.at[:, pl.ds(column, width)])
         for m in moves:
             m.wait()
 
     shape = jax.ShapeDtypeStruct((rows, cols), F32)
-    return pl.pallas_call(
-        kernel,
-        out_shape=[shape] * 3 + [jax.ShapeDtypeStruct((rows, cols * ng), BF16)] + [shape] * 3,
-        in_specs=[VMEM] * (2 * parts + ng),
+    shapes = [jax.ShapeDtypeStruct((rows, cols * ng), BF16)] + [shape] * 3
+    scratch = [pltpu.VMEM((6, rows, cols), F32), pltpu.VMEM((ng, rows, cols), BF16)]
+    early = pl.pallas_call(
+        functools.partial(kernel, True),
+        out_shape=[shape] * 3 + shapes,
+        in_specs=[VMEM] * (2 * parts - 1 + ng),
         out_specs=[ANY] * 7,
-        scratch_shapes=[pltpu.VMEM((6, rows, cols), F32), pltpu.VMEM((ng, rows, cols), BF16), pltpu.SemaphoreType.DMA((ng + 6,))],
+        scratch_shapes=scratch + [pltpu.SemaphoreType.DMA((3 + ng // 2 + (3 + ng // 2) * (parts - 1),))],
+        cost_estimate=pl.CostEstimate(flops=40 * rows * cols * ng, bytes_accessed=12 * rows * cols * ng, transcendentals=0),
         compiler_params=pltpu.CompilerParams(vmem_limit_bytes=LIMIT),
-    )(*own, *other, *states, *near)
+    )(*own, *other[:-1], *states, *near)
+    late = pl.pallas_call(
+        functools.partial(kernel, False),
+        out_shape=shapes,
+        in_specs=[VMEM] * (1 + ng // 2) + [ANY] * 4,
+        out_specs=[ANY] * 4,
+        scratch_shapes=scratch + [pltpu.SemaphoreType.DMA((3 + ng // 2,))],
+        input_output_aliases={1 + ng // 2 + i: i for i in range(4)},
+        compiler_params=pltpu.CompilerParams(vmem_limit_bytes=LIMIT),
+    )(other[-1], *near, *early[3:])
+    return (*early[:3], *late)
 
 
 def finish_plain(own, other, states, near, cols):
@@ -188,12 +220,12 @@
     local = rows % 16 == 0 and cols % 128 == 0
 
     gather = gathered if local else gathered_plain
-    (away_out,) = gather(g, [(1, 1)], cut, rows, nf, ng)
-    kept_out, away_own, kept_own = gather(g, [(1, 0), (0, 1), (0, 0)], cut, rows, nf, ng)
+    (away_out,) = gather(g, [(1, 1)], cut, rows, nf, ng, GLIMIT)
+    kept_out, away_own, kept_own = gather(g, [(1, 0), (0, 1), (0, 0)], cut, rows, nf, ng, LIMIT)
     split = lambda t: t.reshape((2,) * (f_bits - 1) + t.shape[2:])
     got_away = [split(swap(t, [1, 1])) for t in away_out]
+    sent = [(split(t).astype(F32) + x.astype(F32)).astype(BF16) for t, x in zip(away_own, got_away)]
     got_kept = [split(swap(t, [1, 1])) for t in kept_out]
-    sent = [(split(t).astype(F32) + x.astype(F32)).astype(BF16) for t, x in zip(away_own, got_away)]
     kept = [split(t).astype(F32) + x.astype(F32) for t, x in zip(kept_own, got_kept)]
 
     high = list(range(f_bits - 1, 1, -1))
@@ -203,11 +235,11 @@
     for step in range(f_bits):
         masks = [ng << o[step] for o in orders]
         if step == 0:
-            sent[-1], held = lax.optimization_barrier((sent[-1], (master, moment_one, moment_two)))
+            held = lax.optimization_barrier(((master, moment_one, moment_two), sent[-1]))[0]
             states = [jnp.stack(held)]
             for b in range(1, g_bits):
                 states = states + [swap(s, [1 << b] * 2) for s in states]
-        got = [swap(s, masks) for s in sent]
+        got = [swap(s, masks[::-1] if role(k) else masks) for k, s in enumerate(sent)]
 
         ts = [k + x.astype(F32) for k, x in zip(kept, got)]
         if step == f_bits - 1:
@@ -216,24 +248,25 @@
         a, b = [l.index(w) for l, w in zip(labels, want)]
         bit = [(me_f >> w) & 1 for w in want]
 
-        def choose(t, j, away):
+        def choose(t, k, j, away):
+            first = (core ^ role(k)) == 0
             if a == b:
-                return pick(t, jnp.where(core == 0, bit[0], bit[1]) ^ away, a)
-            at = {a: jnp.where(core == 0, bit[0] ^ away, j), b: jnp.where(core == 0, j, bit[1] ^ away)}
+                return pick(t, jnp.where(first, bit[0], bit[1]) ^ away, a)
+            at = {a: jnp.where(first, bit[0] ^ away, j), b: jnp.where(first, j, bit[1] ^ away)}
             return pick(pick(t, at[max(a, b)], max(a, b)), at[min(a, b)], min(a, b))
 
-        def chosen(t, away):
-            return choose(t, 0, away) if a == b else jnp.stack([choose(t, j, away) for j in range(2)])
-
-        sent = [chosen(t, 1).astype(BF16) for t in ts]
-        kept = [chosen(t, 0) for t in ts]
+        def chosen(t, k, away):
+            return choose(t, k, 0, away) if a == b else jnp.stack([choose(t, k, j, away) for j in range(2)])
+
+        sent = [chosen(t, k, 1).astype(BF16) for k, t in enumerate(ts)]
+        kept = [chosen(t, k, 0) for k, t in enumerate(ts)]
         rest = [[x for i, x in enumerate(l) if i not in (a, b)] for l in labels]
         labels = rest if a == b else [[labels[0][b]] + rest[0], [labels[1][a]] + rest[1]]
 
     for b in range(1, g_bits):
         rounded = [t.astype(BF16) for t in ts]
         if b == g_bits - 1:
-            rounded[-1], states = lax.optimization_barrier((rounded[-1], states))
+            states = lax.optimization_barrier((states, rounded[-1]))[0]
             near = [swap(s, [1, 1]) for s in states]
 
         got = [swap(t, [1 << b] * 2) for t in rounded]

time: 33.6 us -> 33.1 us (0.985)
  waiting for transfers between devices: 8.11 us -> 6.98 us
  Pallas kernels: 2.47 us -> 3.06 us
    ppermute x17, waiting for transfers between devices: 8.11 us -> 6.98 us  [swap(): return lax.ppermute(x, BOTH, [(i, i ^ masks[i & 1]) for i in range(n)])]
    pallas_call x1 -> x2, Pallas kernels: 1.36 us -> 1.95 us  [the longest x1 1.1 us: finish(): pl.pallas_call(functools.partial(kernel, True), out_shape=[shape] * 3 + s...]
  transfers between devices with their start and end apart: 17 -> 17, of which waited for: 7 -> 7; matrix products, arithmetic and copies ran while one was open for 2% -> 2% of each run, Pallas kernels for 3% -> 6%
where the time goes in v5:
time: 33.1 us; the launch traced here: 32.9 us
  starting transfers between devices  19.8 us (60%)
  waiting for transfers between devices  6.98 us (21%)
  Pallas kernels  3.06 us (9%)
  local copies, waits for them, and re-layouts  1.74 us (5%)
  between operations  0.87 us (3%)
  other arithmetic  0.54 us (2%)
    ppermute x17, starting transfers between devices, swap(): return lax.ppermute(x, BOTH, [(i, i ^ masks[i & 1]) for i in range(n)])  19.8 us
    ppermute x17, waiting for transfers between devices, swap(): return lax.ppermute(x, BOTH, [(i, i ^ masks[i & 1]) for i in range(n)])  6.98 us
    unnamed x8, local copies, waits for them, and re-layouts  1.6 us
    pallas_call x2, Pallas kernels, gathered(): pl.pallas_call(kernel, out_shape=[jax.ShapeDtypeStruct((2, nf // 4, ng //...  1.11 us
    pallas_call x1, Pallas kernels, finish(): pl.pallas_call(functools.partial(kernel, True), out_shape=[shape] * 3 + s...  1.1 us
    pallas_call x1, Pallas kernels, finish(): pl.pallas_call(functools.partial(kernel, False), out_shape=shapes, in_spe...  0.85 us
  transfers between devices with their start and end apart: 17, of which 7 were waited for; matrix products, arithmetic and copies ran while one was open for 2% of the time, Pallas kernels for 6%

profile of v5, /device:TPU:0, one launch (start us, length us, event | category | flops | bytes accessed | tf_op | source)
XLA Modules:
  0.0 32.9 jit_solution(845282043926663288)
XLA Ops:
  0.6 0.0 copy-start
  0.6 1.6 %copy-done = bf16[1,1,128,8192]{3,2,1,0:T(8,128)(2,1)S(1)} copy-done((bf16[1,1,128,8192]{3,2,1,0:T(8,128)(2,1)S(1)}, bf16[1,1,128,8192]{3,2,1,0:T(8,128)(2,1)}, u32[]{:S(2)}) %copy-start) | copy-done | bytes 2097176
  2.2 0.3 shard_map.100
  2.5 0.0 copy-start.1
  2.5 0.0 copy-start.2
  2.5 0.0 copy-start.3
  2.5 0.5 %collective-permute-start.1 = (bf16[2,2,2,16,1024]{4,3,2,1,0:T(8,128)(2,1)S(1)}, bf16[2,2,2,16,1024]{4,3,2,1,0:T(8,128)(2,1)S(1)}, u32[]{:S(2)}, u32[]{:S(2)}) collective-permute-start(bf16[2,2,2,16,1024]{4,3,2,1,0:T(8,128)(2,1)S(1)} %get-tuple-element.34), channel_id=1, source_target_pairs={{0,1},{1,0},{2,3},{3,2},{4,5},{5,4},{6,7},{7,6},{8,9},{9,8},{10,11... | collective-permute-start | bytes 786440 | tf_op jit(solution)/shard_map/ppermute | solution.py:30
  3.0 0.1 collective-permute-start.7
  3.1 0.9 %shard_map.99 = (bf16[2,2,2,16,1024]{4,3,2,1,0:T(8,128)(2,1)S(1)}, bf16[2,2,2,16,1024]{4,3,2,1,0:T(8,128)(2,1)S(1)}, bf16[2,2,2,16,1024]{4,3,2,1,0:T(8,128)(2,1)...) custom-call(bf16[2,2,2,16,8192]{4,3,2,1,0:T(8,128)(2,1)S(1)} %bitcast.33), custom_call_target="tpu_custom_call" | custom-call | bytes 3145728 | tf_op jit(solution)/shard_map/pallas_call | solution.py:84
  4.0 0.5 %collective-permute-start = (bf16[2,2,2,16,1024]{4,3,2,1,0:T(8,128)(2,1)S(1)}, bf16[2,2,2,16,1024]{4,3,2,1,0:T(8,128)(2,1)S(1)}, u32[]{:S(2)}, u32[]{:S(2)}) collective-permute-start(bf16[2,2,2,16,1024]{4,3,2,1,0:T(8,128)(2,1)S(1)} %get-tuple-element.32), channel_id=1, source_target_pairs={{0,1},{1,0},{2,3},{3,2},{4,5},{5,4},{6,7},{7,6},{8,9},{9,8},{10,11... | collective-permute-start | bytes 786440 | tf_op jit(solution)/shard_map/ppermute | solution.py:30
  4.5 0.1 collective-permute-start.6
  4.6 0.0 collective-permute-done.1
  4.6 0.1 add_convert_fusion.1
  4.6 3.0 %collective-permute-start.2 = (bf16[2,2,2,16,1024]{4,3,2,1,0:T(8,128)(2,1)S(1)}, bf16[2,2,2,16,1024]{4,3,2,1,0:T(8,128)(2,1)S(1)}, u32[]{:S(2)}, u32[]{:S(2)}) collective-permute-start(bf16[2,2,2,16,1024]{4,3,2,1,0:T(8,128)(2,1)S(1)} %add_convert_fusion.1), channel_id=1, source_target_pairs={{0,4},{1,9},{2,6},{3,11},{4,0},{5,13},{6,2},{7,15},{8,12},{9,1},{1... | collective-permute-start | bytes 786440 | tf_op jit(solution)/shard_map/ppermute | solution.py:30
  7.6 0.0 collective-permute-done.7
  7.6 0.1 add_convert_fusion
  7.7 0.1 collective-permute-start.8
  7.8 0.0 copy-done.1
  7.8 0.0 copy-done.2
  7.8 0.0 copy-done.3
  7.9 2.0 %collective-permute-start.13 = (f32[3,16,2048]{2,1,0:T(8,128)S(1)}, f32[3,16,2048]{2,1,0:T(8,128)S(1)}, u32[]{:S(2)}, u32[]{:S(2)}) collective-permute-start(f32[3,16,2048]{2,1,0:T(8,128)S(1)} %pad_maximum_fusion.refs_3_), channel_id=1, source_target_pairs={{0,2},{1,3},{2,0},{3,1},{4,6},{5,7},{6,4},{7,5},{8,10},{9,11},{10,... | collective-permute-start | bytes 1179656 | tf_op jit(solution)/shard_map/ppermute | solution.py:30
  9.9 0.0 collective-permute-done
  9.9 2.1 %collective-permute-done.2 = bf16[2,2,2,16,1024]{4,3,2,1,0:T(8,128)(2,1)S(1)} collective-permute-done((bf16[2,2,2,16,1024]{4,3,2,1,0:T(8,128)(2,1)S(1)}, bf16[2,2,2,16,1024]{4,3,2,1,0:T(8,128)(2,1)S(1)}, u32[]{:S(2)}, u32[]{:S(2)}) %collective-permute-start.2) | collective-permute-done | bytes 262176 | tf_op jit(solution)/shard_map/ppermute | solution.py:30
  12.0 0.1 convert_add_fusion.1
  12.2 2.1 %collective-permute-start.3 = (bf16[2,2,16,1024]{3,2,1,0:T(8,128)(2,1)S(1)}, bf16[2,2,16,1024]{3,2,1,0:T(8,128)(2,1)S(1)}, u32[]{:S(2)}, u32[]{:S(2)}) collective-permute-start(bf16[2,2,16,1024]{3,2,1,0:T(8,128)(2,1)S(1)} %pad_maximum_fusion.1), channel_id=1, source_target_pairs={{0,8},{1,17},{2,10},{3,19},{4,12},{5,21},{6,14},{7,23},{8,0},{9,25... | collective-permute-start | bytes 393224 | tf_op jit(solution)/shard_map/ppermute | solution.py:30
  14.3 0.0 collective-permute-done.6
  14.3 0.5 %collective-permute-done.8 = bf16[2,2,2,16,1024]{4,3,2,1,0:T(8,128)(2,1)S(1)} collective-permute-done((bf16[2,2,2,16,1024]{4,3,2,1,0:T(8,128)(2,1)S(1)}, bf16[2,2,2,16,1024]{4,3,2,1,0:T(8,128)(2,1)S(1)}, u32[]{:S(2)}, u32[]{:S(2)}) %collective-permute-start.8) | collective-permute-done | bytes 262176 | tf_op jit(solution)/shard_map/ppermute | solution.py:30
  14.8 0.1 convert_add_fusion
  15.0 2.1 %collective-permute-start.9 = (bf16[2,2,16,1024]{3,2,1,0:T(8,128)(2,1)S(1)}, bf16[2,2,16,1024]{3,2,1,0:T(8,128)(2,1)S(1)}, u32[]{:S(2)}, u32[]{:S(2)}) collective-permute-start(bf16[2,2,16,1024]{3,2,1,0:T(8,128)(2,1)S(1)} %pad_maximum_fusion.2), channel_id=1, source_target_pairs={{0,8},{1,17},{2,10},{3,19},{4,12},{5,21},{6,14},{7,23},{8,0},{9,25... | collective-permute-start | bytes 393224 | tf_op jit(solution)/shard_map/ppermute | solution.py:30
  17.2 0.8 %collective-permute-done.3 = bf16[2,2,16,1024]{3,2,1,0:T(8,128)(2,1)S(1)} collective-permute-done((bf16[2,2,16,1024]{3,2,1,0:T(8,128)(2,1)S(1)}, bf16[2,2,16,1024]{3,2,1,0:T(8,128)(2,1)S(1)}, u32[]{:S(2)}, u32[]{:S(2)}) %collective-permute-start.3) | collective-permute-done | bytes 131104 | tf_op jit(solution)/shard_map/ppermute | solution.py:30
  18.0 2.9 %collective-permute-start.4 = (bf16[2,16,1024]{2,1,0:T(8,128)(2,1)S(1)}, bf16[2,16,1024]{2,1,0:T(8,128)(2,1)S(1)}, u32[]{:S(2)}, u32[]{:S(2)}) collective-permute-start(bf16[2,16,1024]{2,1,0:T(8,128)(2,1)S(1)} %fusion.4), channel_id=1, source_target_pairs={{0,16},{1,5},{2,18},{3,7},{4,20},{5,1},{6,22},{7,3},{8,24},{9,13},... | collective-permute-start | bytes 196616 | tf_op jit(solution)/shard_map/ppermute | solution.py:30
  20.9 0.1 collective-permute-done.9
  21.1 2.5 %collective-permute-start.10 = (bf16[2,16,1024]{2,1,0:T(8,128)(2,1)S(1)}, bf16[2,16,1024]{2,1,0:T(8,128)(2,1)S(1)}, u32[]{:S(2)}, u32[]{:S(2)}) collective-permute-start(bf16[2,16,1024]{2,1,0:T(8,128)(2,1)S(1)} %fusion.7), channel_id=1, source_target_pairs={{0,16},{1,5},{2,18},{3,7},{4,20},{5,1},{6,22},{7,3},{8,24},{9,13},... | collective-permute-start | bytes 196616 | tf_op jit(solution)/shard_map/ppermute | solution.py:30
  23.6 0.0 collective-permute-done.4
  23.6 1.6 %collective-permute-start.5 = (bf16[2,16,1024]{2,1,0:T(8,128)(2,1)S(1)}, bf16[2,16,1024]{2,1,0:T(8,128)(2,1)S(1)}, u32[]{:S(2)}, u32[]{:S(2)}) collective-permute-start(bf16[2,16,1024]{2,1,0:T(8,128)(2,1)S(1)} %fusion.1), channel_id=1, source_target_pairs={{0,2},{1,3},{2,0},{3,1},{4,6},{5,7},{6,4},{7,5},{8,10},{9,11},{10,... | collective-permute-start | bytes 196616 | tf_op jit(solution)/shard_map/ppermute | solution.py:30
  25.2 1.1 %collective-permute-done.10 = bf16[2,16,1024]{2,1,0:T(8,128)(2,1)S(1)} collective-permute-done((bf16[2,16,1024]{2,1,0:T(8,128)(2,1)S(1)}, bf16[2,16,1024]{2,1,0:T(8,128)(2,1)S(1)}, u32[]{:S(2)}, u32[]{:S(2)}) %collective-permute-start.10) | collective-permute-done | bytes 65568 | tf_op jit(solution)/shard_map/ppermute | solution.py:30
  26.3 1.6 %collective-permute-start.11 = (bf16[2,16,1024]{2,1,0:T(8,128)(2,1)S(1)}, bf16[2,16,1024]{2,1,0:T(8,128)(2,1)S(1)}, u32[]{:S(2)}, u32[]{:S(2)}) collective-permute-start(bf16[2,16,1024]{2,1,0:T(8,128)(2,1)S(1)} %fusion), channel_id=1, source_target_pairs={{0,2},{1,3},{2,0},{3,1},{4,6},{5,7},{6,4},{7,5},{8,10},{9,11},{10,... | collective-permute-start | bytes 196616 | tf_op jit(solution)/shard_map/ppermute | solution.py:30
  27.9 0.0 collective-permute-done.13.refs_4_
  27.9 0.0 collective-permute-start.14
  27.9 0.5 %collective-permute-start.15 = (f32[3,16,2048]{2,1,0:T(8,128)S(1)}, f32[3,16,2048]{2,1,0:T(8,128)S(1)}, u32[]{:S(2)}, u32[]{:S(2)}) collective-permute-start(f32[3,16,2048]{2,1,0:T(8,128)S(1)} %collective-permute-done.13.refs_4_), channel_id=1, source_target_pairs={{0,1},{1,0},{2,3},{3,2},{4,5},{5,4},{6,7},{7,6},{8,9},{9,8},{10,11... | collective-permute-start | bytes 1179656 | tf_op jit(solution)/shard_map/ppermute | solution.py:30
  28.4 0.0 collective-permute-done.5
  28.5 0.1 collective-permute-start.12
  28.6 2.1 %collective-permute-done.11 = bf16[2,16,1024]{2,1,0:T(8,128)(2,1)S(1)} collective-permute-done((bf16[2,16,1024]{2,1,0:T(8,128)(2,1)S(1)}, bf16[2,16,1024]{2,1,0:T(8,128)(2,1)S(1)}, u32[]{:S(2)}, u32[]{:S(2)}) %collective-permute-start.11) | collective-permute-done | bytes 65568 | tf_op jit(solution)/shard_map/ppermute | solution.py:30
  30.7 0.1 collective-permute-start.16
  30.8 0.0 collective-permute-done.12.refs_2_
  30.8 0.0 collective-permute-done.14.refs_5_.refs_1_
  30.8 0.0 collective-permute-done.15.refs_6_.refs_2_
  30.8 1.1 %shard_map.101 = (f32[16,2048]{1,0:T(8,128)}, f32[16,2048]{1,0:T(8,128)}, f32[16,2048]{1,0:T(8,128)}, bf16[16,8192]{1,0:T(8,128)(2,1)}, f32[16,2048]{1,0:T(8,128...) custom-call(f32[2,16,1024]{2,1,0:T(8,128)S(1)} %add_multiply_fusion.1.refs_0_, f32[2,16,1024]{2,1,0:T(8,128)S(1)} %add_multiply_fusion.refs_1_, ...), custom_call_target="tpu_custom_call" | custom-call | flops 5242880 | bytes 1572864 | tf_op jit(solution)/shard_map/pallas_call | solution.py:173
  31.9 0.2 collective-permute-done.16.refs_0_
  32.1 0.8 %shard_map.102 = (bf16[16,8192]{1,0:T(8,128)(2,1)}, f32[16,2048]{1,0:T(8,128)}, f32[16,2048]{1,0:T(8,128)}, f32[16,2048]{1,0:T(8,128)}) custom-call(f32[2,16,1024]{2,1,0:T(8,128)S(1)} %collective-permute-done.16.refs_0_, ...), custom_call_target="tpu_custom_call", output_to_operand_aliasing={{0}: (3, {}), {1}: (4, {}), {2}: (5, {}), {3}: (6, {})} | custom-call | tf_op jit(solution)/shard_map/pallas_call | solution.py:182
  (15 shorter events, 0.3 us)
Async XLA Ops:
  0.6 1.6 %copy-start = (bf16[1,1,128,8192]{3,2,1,0:T(8,128)(2,1)S(1)}, bf16[1,1,128,8192]{3,2,1,0:T(8,128)(2,1)}, u32[]{:S(2)}) copy-start(bf16[1,1,128,8192]{3,2,1,0:T(8,128)(2,1)} %param.4) | copy-start | bytes 6291460
  2.5 5.3 %copy-start.1 = (f32[16,2048]{1,0:T(8,128)S(1)}, f32[16,2048]{1,0:T(8,128)}, u32[]{:S(2)}) copy-start(f32[16,2048]{1,0:T(8,128)} %param.7) | copy-start | bytes 393220
  2.5 5.3 %copy-start.2 = (f32[16,2048]{1,0:T(8,128)S(1)}, f32[16,2048]{1,0:T(8,128)}, u32[]{:S(2)}) copy-start(f32[16,2048]{1,0:T(8,128)} %param.6) | copy-start | bytes 393220
  2.5 5.3 %copy-start.3 = (f32[16,2048]{1,0:T(8,128)S(1)}, f32[16,2048]{1,0:T(8,128)}, u32[]{:S(2)}) copy-start(f32[16,2048]{1,0:T(8,128)} %param.5) | copy-start | bytes 393220
  2.5 2.0 %collective-permute-start.1 = (bf16[2,2,2,16,1024]{4,3,2,1,0:T(8,128)(2,1)S(1)}, bf16[2,2,2,16,1024]{4,3,2,1,0:T(8,128)(2,1)S(1)}, u32[]{:S(2)}, u32[]{:S(2)}) collective-permute-start(bf16[2,2,2,16,1024]{4,3,2,1,0:T(8,128)(2,1)S(1)} %get-tuple-element.34), channel_id=1, source_target_pairs={{0,1},{1,0},{2,3},{3,2},{4,5},{5,4},{6,7},{7,6},{8,9},{9,8},{10,11... | collective-permute-start | bytes 786440 | tf_op jit(solution)/shard_map/ppermute | solution.py:30
  3.0 4.6 %collective-permute-start.7 = (bf16[2,2,2,16,1024]{4,3,2,1,0:T(8,128)(2,1)S(1)}, bf16[2,2,2,16,1024]{4,3,2,1,0:T(8,128)(2,1)S(1)}, u32[]{:S(2)}, u32[]{:S(2)}) collective-permute-start(bf16[2,2,2,16,1024]{4,3,2,1,0:T(8,128)(2,1)S(1)} %get-tuple-element.38), channel_id=1, source_target_pairs={{0,1},{1,0},{2,3},{3,2},{4,5},{5,4},{6,7},{7,6},{8,9},{9,8},{10,11... | collective-permute-start | bytes 786440 | tf_op jit(solution)/shard_map/ppermute | solution.py:30
  4.0 5.9 %collective-permute-start = (bf16[2,2,2,16,1024]{4,3,2,1,0:T(8,128)(2,1)S(1)}, bf16[2,2,2,16,1024]{4,3,2,1,0:T(8,128)(2,1)S(1)}, u32[]{:S(2)}, u32[]{:S(2)}) collective-permute-start(bf16[2,2,2,16,1024]{4,3,2,1,0:T(8,128)(2,1)S(1)} %get-tuple-element.32), channel_id=1, source_target_pairs={{0,1},{1,0},{2,3},{3,2},{4,5},{5,4},{6,7},{7,6},{8,9},{9,8},{10,11... | collective-permute-start | bytes 786440 | tf_op jit(solution)/shard_map/ppermute | solution.py:30
  4.5 9.8 %collective-permute-start.6 = (bf16[2,2,2,16,1024]{4,3,2,1,0:T(8,128)(2,1)S(1)}, bf16[2,2,2,16,1024]{4,3,2,1,0:T(8,128)(2,1)S(1)}, u32[]{:S(2)}, u32[]{:S(2)}) collective-permute-start(bf16[2,2,2,16,1024]{4,3,2,1,0:T(8,128)(2,1)S(1)} %get-tuple-element.36), channel_id=1, source_target_pairs={{0,1},{1,0},{2,3},{3,2},{4,5},{5,4},{6,7},{7,6},{8,9},{9,8},{10,11... | collective-permute-start | bytes 786440 | tf_op jit(solution)/shard_map/ppermute | solution.py:30
  4.6 7.4 %collective-permute-start.2 = (bf16[2,2,2,16,1024]{4,3,2,1,0:T(8,128)(2,1)S(1)}, bf16[2,2,2,16,1024]{4,3,2,1,0:T(8,128)(2,1)S(1)}, u32[]{:S(2)}, u32[]{:S(2)}) collective-permute-start(bf16[2,2,2,16,1024]{4,3,2,1,0:T(8,128)(2,1)S(1)} %add_convert_fusion.1), channel_id=1, source_target_pairs={{0,4},{1,9},{2,6},{3,11},{4,0},{5,13},{6,2},{7,15},{8,12},{9,1},{1... | collective-permute-start | bytes 786440 | tf_op jit(solution)/shard_map/ppermute | solution.py:30
  7.7 7.1 %collective-permute-start.8 = (bf16[2,2,2,16,1024]{4,3,2,1,0:T(8,128)(2,1)S(1)}, bf16[2,2,2,16,1024]{4,3,2,1,0:T(8,128)(2,1)S(1)}, u32[]{:S(2)}, u32[]{:S(2)}) collective-permute-start(bf16[2,2,2,16,1024]{4,3,2,1,0:T(8,128)(2,1)S(1)} %add_convert_fusion), channel_id=1, source_target_pairs={{0,4},{1,9},{2,6},{3,11},{4,0},{5,13},{6,2},{7,15},{8,12},{9,1},{1... | collective-permute-start | bytes 786440 | tf_op jit(solution)/shard_map/ppermute | solution.py:30
  7.9 20.1 %collective-permute-start.13 = (f32[3,16,2048]{2,1,0:T(8,128)S(1)}, f32[3,16,2048]{2,1,0:T(8,128)S(1)}, u32[]{:S(2)}, u32[]{:S(2)}) collective-permute-start(f32[3,16,2048]{2,1,0:T(8,128)S(1)} %pad_maximum_fusion.refs_3_), channel_id=1, source_target_pairs={{0,2},{1,3},{2,0},{3,1},{4,6},{5,7},{6,4},{7,5},{8,10},{9,11},{10,... | collective-permute-start | bytes 1179656 | tf_op jit(solution)/shard_map/ppermute | solution.py:30
  12.2 5.8 %collective-permute-start.3 = (bf16[2,2,16,1024]{3,2,1,0:T(8,128)(2,1)S(1)}, bf16[2,2,16,1024]{3,2,1,0:T(8,128)(2,1)S(1)}, u32[]{:S(2)}, u32[]{:S(2)}) collective-permute-start(bf16[2,2,16,1024]{3,2,1,0:T(8,128)(2,1)S(1)} %pad_maximum_fusion.1), channel_id=1, source_target_pairs={{0,8},{1,17},{2,10},{3,19},{4,12},{5,21},{6,14},{7,23},{8,0},{9,25... | collective-permute-start | bytes 393224 | tf_op jit(solution)/shard_map/ppermute | solution.py:30
  15.0 6.0 %collective-permute-start.9 = (bf16[2,2,16,1024]{3,2,1,0:T(8,128)(2,1)S(1)}, bf16[2,2,16,1024]{3,2,1,0:T(8,128)(2,1)S(1)}, u32[]{:S(2)}, u32[]{:S(2)}) collective-permute-start(bf16[2,2,16,1024]{3,2,1,0:T(8,128)(2,1)S(1)} %pad_maximum_fusion.2), channel_id=1, source_target_pairs={{0,8},{1,17},{2,10},{3,19},{4,12},{5,21},{6,14},{7,23},{8,0},{9,25... | collective-permute-start | bytes 393224 | tf_op jit(solution)/shard_map/ppermute | solution.py:30
  18.0 5.6 %collective-permute-start.4 = (bf16[2,16,1024]{2,1,0:T(8,128)(2,1)S(1)}, bf16[2,16,1024]{2,1,0:T(8,128)(2,1)S(1)}, u32[]{:S(2)}, u32[]{:S(2)}) collective-permute-start(bf16[2,16,1024]{2,1,0:T(8,128)(2,1)S(1)} %fusion.4), channel_id=1, source_target_pairs={{0,16},{1,5},{2,18},{3,7},{4,20},{5,1},{6,22},{7,3},{8,24},{9,13},... | collective-permute-start | bytes 196616 | tf_op jit(solution)/shard_map/ppermute | solution.py:30
  21.1 5.2 %collective-permute-start.10 = (bf16[2,16,1024]{2,1,0:T(8,128)(2,1)S(1)}, bf16[2,16,1024]{2,1,0:T(8,128)(2,1)S(1)}, u32[]{:S(2)}, u32[]{:S(2)}) collective-permute-start(bf16[2,16,1024]{2,1,0:T(8,128)(2,1)S(1)} %fusion.7), channel_id=1, source_target_pairs={{0,16},{1,5},{2,18},{3,7},{4,20},{5,1},{6,22},{7,3},{8,24},{9,13},... | collective-permute-start | bytes 196616 | tf_op jit(solution)/shard_map/ppermute | solution.py:30
  23.6 4.8 %collective-permute-start.5 = (bf16[2,16,1024]{2,1,0:T(8,128)(2,1)S(1)}, bf16[2,16,1024]{2,1,0:T(8,128)(2,1)S(1)}, u32[]{:S(2)}, u32[]{:S(2)}) collective-permute-start(bf16[2,16,1024]{2,1,0:T(8,128)(2,1)S(1)} %fusion.1), channel_id=1, source_target_pairs={{0,2},{1,3},{2,0},{3,1},{4,6},{5,7},{6,4},{7,5},{8,10},{9,11},{10,... | collective-permute-start | bytes 196616 | tf_op jit(solution)/shard_map/ppermute | solution.py:30
  26.3 4.3 %collective-permute-start.11 = (bf16[2,16,1024]{2,1,0:T(8,128)(2,1)S(1)}, bf16[2,16,1024]{2,1,0:T(8,128)(2,1)S(1)}, u32[]{:S(2)}, u32[]{:S(2)}) collective-permute-start(bf16[2,16,1024]{2,1,0:T(8,128)(2,1)S(1)} %fusion), channel_id=1, source_target_pairs={{0,2},{1,3},{2,0},{3,1},{4,6},{5,7},{6,4},{7,5},{8,10},{9,11},{10,... | collective-permute-start | bytes 196616 | tf_op jit(solution)/shard_map/ppermute | solution.py:30
  27.9 2.8 %collective-permute-start.14 = (f32[3,16,2048]{2,1,0:T(8,128)S(1)}, f32[3,16,2048]{2,1,0:T(8,128)S(1)}, u32[]{:S(2)}, u32[]{:S(2)}) collective-permute-start(f32[3,16,2048]{2,1,0:T(8,128)S(1)} %pad_maximum_fusion.refs_3_), channel_id=1, source_target_pairs={{0,1},{1,0},{2,3},{3,2},{4,5},{5,4},{6,7},{7,6},{8,9},{9,8},{10,11... | collective-permute-start | bytes 1179656 | tf_op jit(solution)/shard_map/ppermute | solution.py:30
  27.9 2.8 %collective-permute-start.15 = (f32[3,16,2048]{2,1,0:T(8,128)S(1)}, f32[3,16,2048]{2,1,0:T(8,128)S(1)}, u32[]{:S(2)}, u32[]{:S(2)}) collective-permute-start(f32[3,16,2048]{2,1,0:T(8,128)S(1)} %collective-permute-done.13.refs_4_), channel_id=1, source_target_pairs={{0,1},{1,0},{2,3},{3,2},{4,5},{5,4},{6,7},{7,6},{8,9},{9,8},{10,11... | collective-permute-start | bytes 1179656 | tf_op jit(solution)/shard_map/ppermute | solution.py:30
  28.5 2.3 %collective-permute-start.12 = (f32[2,16,1024]{2,1,0:T(8,128)S(1)}, f32[2,16,1024]{2,1,0:T(8,128)S(1)}, u32[]{:S(2)}, u32[]{:S(2)}) collective-permute-start(f32[2,16,1024]{2,1,0:T(8,128)S(1)} %add_multiply_fusion.1.refs_0_), channel_id=1, source_target_pairs={{0,1},{1,0},{2,3},{3,2},{4,5},{5,4},{6,7},{7,6},{8,9},{9,8},{10,11... | collective-permute-start | bytes 393224 | tf_op jit(solution)/shard_map/ppermute | solution.py:30
  30.7 1.4 %collective-permute-start.16 = (f32[2,16,1024]{2,1,0:T(8,128)S(1)}, f32[2,16,1024]{2,1,0:T(8,128)S(1)}, u32[]{:S(2)}, u32[]{:S(2)}) collective-permute-start(f32[2,16,1024]{2,1,0:T(8,128)S(1)} %add_multiply_fusion.refs_1_), channel_id=1, source_target_pairs={{0,1},{1,0},{2,3},{3,2},{4,5},{5,4},{6,7},{7,6},{8,9},{9,8},{10,11... | collective-permute-start | bytes 393224 | tf_op jit(solution)/shard_map/ppermute | solution.py:30

commit v6 on v5

--- a/solution.py
+++ b/solution.py
@@ -17,11 +17,10 @@
 BF16 = jnp.bfloat16
 BOTH = ("fsdp", "grp")
 SHARES = [1, 1]
-ROLES = 0
+ORDERS = [[[0, 1, 2], [1, 2, 0]], [[0, 1, 2], [1, 2, 0]]]
 VMEM = pl.BlockSpec(memory_space=pltpu.VMEM)
 ANY = pl.BlockSpec(memory_space=pl.ANY)
-HBM = pl.BlockSpec(memory_space=pltpu.HBM)
-GLIMIT = 32 * 2**17
+HBM = pl.BlockSpec(memory_space=pl.ANY)
 LIMIT = 4 * 2**20
 
 
@@ -55,10 +54,6 @@
     return jnp.where(core == 0, low ^ away, j), jnp.where(core == 0, j, high ^ away)
 
 
-def role(k):
-    return ROLES * (k % 2)
-
-
 def gathered(g, wanted, cut, rows, nf, ng, limit):
     cols = g.shape[1] // ng
     blocks = g.reshape(nf // 4, 2, 2, rows, g.shape[1])
@@ -71,7 +66,7 @@
             core = (me_g & 1) ^ sibling
             for k, (start, width) in enumerate(cut):
                 for j in range(2):
-                    low, high = first_block(core ^ role(k), me_f, j, away)
+                    low, high = first_block(core, me_f, j, away)
                     for x in range(ng // 2):
                         column = pl.multiple_of((2 * x + core) * cols + start, 128)
                         moves.append(pltpu.make_async_copy(
@@ -99,7 +94,7 @@
     me_f, me_g = lax.axis_index("fsdp"), lax.axis_index("grp")
 
     def block(core, k, away, j, x, start, width):
-        low, high = first_block(core ^ role(k), me_f, j, away)
+        low, high = first_block(core, me_f, j, away)
         part = lax.dynamic_slice(blocks, (0, high, low, 0, (2 * x + core) * cols + start), (nf // 4, 1, 1, rows, width))
         return part[:, 0, 0]
 
@@ -209,6 +204,24 @@
     return (*mine, weights, *copies)
 
 
+def onward(t, core, me_f, labels, want):
+    a, b = [names.index(w) for names, w in zip(labels, want)]
+    bit = [(me_f >> w) & 1 for w in want]
+
+    def choose(j, away):
+        if a == b:
+            return pick(t, jnp.where(core == 0, bit[0], bit[1]) ^ away, a)
+        at = {a: jnp.where(core == 0, bit[0] ^ away, j), b: jnp.where(core == 0, j, bit[1] ^ away)}
+        return pick(pick(t, at[max(a, b)], max(a, b)), at[min(a, b)], min(a, b))
+
+    def chosen(away):
+        return choose(0, away) if a == b else jnp.stack([choose(j, away) for j in range(2)])
+
+    rest = [[name for i, name in enumerate(names) if i not in (a, b)] for names in labels]
+    left = rest if a == b else [[labels[0][b]] + rest[0], [labels[1][a]] + rest[1]]
+    return chosen(1).astype(BF16), chosen(0), left
+
+
 def shards(grads, master, moment_one, moment_two):
     ng, nf = lax.axis_size("grp"), lax.axis_size("fsdp")
     g_bits, f_bits = ng.bit_length() - 1, nf.bit_length() - 1
@@ -220,48 +233,38 @@
     local = rows % 16 == 0 and cols % 128 == 0
 
     gather = gathered if local else gathered_plain
-    (away_out,) = gather(g, [(1, 1)], cut, rows, nf, ng, GLIMIT)
-    kept_out, away_own, kept_own = gather(g, [(1, 0), (0, 1), (0, 0)], cut, rows, nf, ng, LIMIT)
+    away_out, away_own = [], []
+    source = g
+    for edge in cut:
+        (out,), (mine,) = gather(source, [(1, 1), (0, 1)], [edge], rows, nf, ng, LIMIT)
+        source = lax.optimization_barrier((g, out))[0]
+        away_out.append(out)
+        away_own.append(mine)
     split = lambda t: t.reshape((2,) * (f_bits - 1) + t.shape[2:])
     got_away = [split(swap(t, [1, 1])) for t in away_out]
     sent = [(split(t).astype(F32) + x.astype(F32)).astype(BF16) for t, x in zip(away_own, got_away)]
+    later = lax.optimization_barrier((g, sent[-1]))[0]
+    kept_out, kept_own = gather(later, [(1, 0), (0, 0)], cut, rows, nf, ng, LIMIT)
     got_kept = [split(swap(t, [1, 1])) for t in kept_out]
     kept = [split(t).astype(F32) + x.astype(F32) for t, x in zip(kept_own, got_kept)]
 
     high = list(range(f_bits - 1, 1, -1))
-    labels = [[1] + high, [0] + high]
-    orders = [[0, 1, 2], [1, 2, 0]]
-    orders = [o + [b for b in range(f_bits) if b not in o] for o in orders]
+    labels = [[[1] + high, [0] + high] for _ in cut]
+    orders = [[o + [b for b in range(f_bits) if b not in o] for o in ORDERS[k % 2]] for k in range(len(cut))]
     for step in range(f_bits):
-        masks = [ng << o[step] for o in orders]
+        masks = [[ng << o[step] for o in pair] for pair in orders]
         if step == 0:
             held = lax.optimization_barrier(((master, moment_one, moment_two), sent[-1]))[0]
             states = [jnp.stack(held)]
             for b in range(1, g_bits):
                 states = states + [swap(s, [1 << b] * 2) for s in states]
-        got = [swap(s, masks[::-1] if role(k) else masks) for k, s in enumerate(sent)]
+        got = [swap(s, m) for s, m in zip(sent, masks)]
 
         ts = [k + x.astype(F32) for k, x in zip(kept, got)]
         if step == f_bits - 1:
             break
-        want = [o[step + 1] for o in orders]
-        a, b = [l.index(w) for l, w in zip(labels, want)]
-        bit = [(me_f >> w) & 1 for w in want]
-
-        def choose(t, k, j, away):
-            first = (core ^ role(k)) == 0
-            if a == b:
-                return pick(t, jnp.where(first, bit[0], bit[1]) ^ away, a)
-            at = {a: jnp.where(first, bit[0] ^ away, j), b: jnp.where(first, j, bit[1] ^ away)}
-            return pick(pick(t, at[max(a, b)], max(a, b)), at[min(a, b)], min(a, b))
-
-        def chosen(t, k, away):
-            return choose(t, k, 0, away) if a == b else jnp.stack([choose(t, k, j, away) for j in range(2)])
-
-        sent = [chosen(t, k, 1).astype(BF16) for k, t in enumerate(ts)]
-        kept = [chosen(t, k, 0) for k, t in enumerate(ts)]
-        rest = [[x for i, x in enumerate(l) if i not in (a, b)] for l in labels]
-        labels = rest if a == b else [[labels[0][b]] + rest[0], [labels[1][a]] + rest[1]]
+        moved = [onward(t, core, me_f, pair, [o[step + 1] for o in order]) for t, pair, order in zip(ts, labels, orders)]
+        sent, kept, labels = [list(m) for m in zip(*moved)]
 
     for b in range(1, g_bits):
         rounded = [t.astype(BF16) for t in ts]

time: 33.1 us -> 32.7 us (0.988)
  waiting for transfers between devices: 6.98 us -> 6.12 us
  starting transfers between devices: 19.8 us -> 20.2 us
    ppermute x17, waiting for transfers between devices: 6.98 us -> 6.12 us  [swap(): return lax.ppermute(x, BOTH, [(i, i ^ masks[i & 1]) for i in range(n)])]
    ppermute x17, starting transfers between devices: 19.8 us -> 20.2 us  [swap(): return lax.ppermute(x, BOTH, [(i, i ^ masks[i & 1]) for i in range(n)])]
    pallas_call x2 -> x3, Pallas kernels: 1.11 us -> 1.09 us  [gathered(): pl.pallas_call(kernel, out_shape=[jax.ShapeDtypeStruct((2, nf // 4, ng //...]
    unnamed x8 -> x10, local copies, waits for them, and re-layouts: 1.6 us -> 1.61 us
  transfers between devices with their start and end apart: 17 -> 17, of which waited for: 7 -> 8; matrix products, arithmetic and copies ran while one was open for 2% -> 2% of each run, Pallas kernels for 6% -> 6%
where the time goes in v6:
time: 32.7 us; the launch traced here: 32.6 us
  starting transfers between devices  20.2 us (62%)
  waiting for transfers between devices  6.12 us (19%)
  Pallas kernels  3.04 us (9%)
  local copies, waits for them, and re-layouts  1.75 us (5%)
  between operations  0.95 us (3%)
  other arithmetic  0.53 us (2%)
    ppermute x17, starting transfers between devices, swap(): return lax.ppermute(x, BOTH, [(i, i ^ masks[i & 1]) for i in range(n)])  20.2 us
    ppermute x17, waiting for transfers between devices, swap(): return lax.ppermute(x, BOTH, [(i, i ^ masks[i & 1]) for i in range(n)])  6.12 us
    unnamed x10, local copies, waits for them, and re-layouts  1.61 us
    pallas_call x1, Pallas kernels, finish(): pl.pallas_call(functools.partial(kernel, True), out_shape=[shape] * 3 + s...  1.1 us
    pallas_call x3, Pallas kernels, gathered(): pl.pallas_call(kernel, out_shape=[jax.ShapeDtypeStruct((2, nf // 4, ng //...  1.09 us
    pallas_call x1, Pallas kernels, finish(): pl.pallas_call(functools.partial(kernel, False), out_shape=shapes, in_spe...  0.85 us
  transfers between devices with their start and end apart: 17, of which 8 were waited for; matrix products, arithmetic and copies ran while one was open for 2% of the time, Pallas kernels for 6%

profile of v6, /device:TPU:0, one launch (start us, length us, event | category | flops | bytes accessed | tf_op | source)
XLA Modules:
  0.0 32.6 jit_solution(7693106099911942449)
XLA Ops:
  0.6 0.0 copy-start
  0.6 1.6 %copy-done = bf16[1,1,128,8192]{3,2,1,0:T(8,128)(2,1)S(1)} copy-done((bf16[1,1,128,8192]{3,2,1,0:T(8,128)(2,1)S(1)}, bf16[1,1,128,8192]{3,2,1,0:T(8,128)(2,1)}, u32[]{:S(2)}) %copy-start) | copy-done | bytes 2097176
  2.2 0.3 shard_map.99
  2.5 0.0 copy-start.1
  2.5 0.5 %collective-permute-start.2 = (bf16[2,2,2,16,1024]{4,3,2,1,0:T(8,128)(2,1)S(1)}, bf16[2,2,2,16,1024]{4,3,2,1,0:T(8,128)(2,1)S(1)}, u32[]{:S(2)}, u32[]{:S(2)}) collective-permute-start(bf16[2,2,2,16,1024]{4,3,2,1,0:T(8,128)(2,1)S(1)} %get-tuple-element.33), channel_id=1, source_target_pairs={{0,1},{1,0},{2,3},{3,2},{4,5},{5,4},{6,7},{7,6},{8,9},{9,8},{10,11... | collective-permute-start | bytes 786440 | tf_op jit(solution)/shard_map/ppermute | solution.py:29
  3.0 0.3 shard_map.100
  3.3 0.0 copy-start.2
  3.3 0.0 copy-start.3
  3.3 0.0 copy-start.4
  3.3 0.1 collective-permute-start
  3.4 0.7 %collective-permute-done.2 = bf16[2,2,2,16,1024]{4,3,2,1,0:T(8,128)(2,1)S(1)} collective-permute-done((bf16[2,2,2,16,1024]{4,3,2,1,0:T(8,128)(2,1)S(1)}, bf16[2,2,2,16,1024]{4,3,2,1,0:T(8,128)(2,1)S(1)}, u32[]{:S(2)}, u32[]{:S(2)}) %collective-permute-start.2) | collective-permute-done | bytes 262176 | tf_op jit(solution)/shard_map/ppermute | solution.py:29
  4.2 0.1 add_convert_fusion
  4.3 3.0 %collective-permute-start.3 = (bf16[2,2,2,16,1024]{4,3,2,1,0:T(8,128)(2,1)S(1)}, bf16[2,2,2,16,1024]{4,3,2,1,0:T(8,128)(2,1)S(1)}, u32[]{:S(2)}, u32[]{:S(2)}) collective-permute-start(bf16[2,2,2,16,1024]{4,3,2,1,0:T(8,128)(2,1)S(1)} %add_convert_fusion), channel_id=1, source_target_pairs={{0,4},{1,9},{2,6},{3,11},{4,0},{5,13},{6,2},{7,15},{8,12},{9,1},{1... | collective-permute-start | bytes 786440 | tf_op jit(solution)/shard_map/ppermute | solution.py:29
  7.2 0.0 collective-permute-done
  7.2 0.1 add_convert_fusion.1
  7.3 0.0 copy-done.1
  7.3 0.6 %shard_map.101 = (bf16[2,2,2,16,1024]{4,3,2,1,0:T(8,128)(2,1)S(1)}, bf16[2,2,2,16,1024]{4,3,2,1,0:T(8,128)(2,1)S(1)}, bf16[2,2,2,16,1024]{4,3,2,1,0:T(8,128)(2,1)S(1)}, bf16[2,2,2,16,1024]{4,3,2,1,0:T(8,128)(2,1)S(1)}) custom-call(bf16[2,2,2,16,8192]{4,3,2,1,0:T(8,128)(2,1)S(1)} %bitcast.37), custom_call_target="tpu_custom_call" | custom-call | bytes 2097152 | tf_op jit(solution)/shard_map/pallas_call | solution.py:79
  7.9 0.1 collective-permute-start.1
  8.0 1.3 %collective-permute-start.8 = (bf16[2,2,2,16,1024]{4,3,2,1,0:T(8,128)(2,1)S(1)}, bf16[2,2,2,16,1024]{4,3,2,1,0:T(8,128)(2,1)S(1)}, u32[]{:S(2)}, u32[]{:S(2)}) collective-permute-start(bf16[2,2,2,16,1024]{4,3,2,1,0:T(8,128)(2,1)S(1)} %add_convert_fusion.1), channel_id=1, source_target_pairs={{0,4},{1,9},{2,6},{3,11},{4,0},{5,13},{6,2},{7,15},{8,12},{9,1},{1... | collective-permute-start | bytes 786440 | tf_op jit(solution)/shard_map/ppermute | solution.py:29
  9.4 0.4 %collective-permute-start.7 = (bf16[2,2,2,16,1024]{4,3,2,1,0:T(8,128)(2,1)S(1)}, bf16[2,2,2,16,1024]{4,3,2,1,0:T(8,128)(2,1)S(1)}, u32[]{:S(2)}, u32[]{:S(2)}) collective-permute-start(bf16[2,2,2,16,1024]{4,3,2,1,0:T(8,128)(2,1)S(1)} %get-tuple-element.42), channel_id=1, source_target_pairs={{0,1},{1,0},{2,3},{3,2},{4,5},{5,4},{6,7},{7,6},{8,9},{9,8},{10,11... | collective-permute-start | bytes 786440 | tf_op jit(solution)/shard_map/ppermute | solution.py:29
  9.7 0.0 copy-done.2
  9.8 0.0 copy-done.3
  9.8 0.0 copy-done.4
  9.8 1.6 %collective-permute-start.13 = (f32[3,16,2048]{2,1,0:T(8,128)S(1)}, f32[3,16,2048]{2,1,0:T(8,128)S(1)}, u32[]{:S(2)}, u32[]{:S(2)}) collective-permute-start(f32[3,16,2048]{2,1,0:T(8,128)S(1)} %pad_maximum_fusion.refs_3_), channel_id=1, source_target_pairs={{0,2},{1,3},{2,0},{3,1},{4,6},{5,7},{6,4},{7,5},{8,10},{9,11},{10,... | collective-permute-start | bytes 1179656 | tf_op jit(solution)/shard_map/ppermute | solution.py:29
  11.3 0.2 collective-permute-done.3
  11.6 0.0 collective-permute-done.1
  11.6 0.1 convert_add_fusion.1
  11.7 2.1 %collective-permute-start.4 = (bf16[2,2,16,1024]{3,2,1,0:T(8,128)(2,1)S(1)}, bf16[2,2,16,1024]{3,2,1,0:T(8,128)(2,1)S(1)}, u32[]{:S(2)}, u32[]{:S(2)}) collective-permute-start(bf16[2,2,16,1024]{3,2,1,0:T(8,128)(2,1)S(1)} %pad_maximum_fusion.1), channel_id=1, source_target_pairs={{0,8},{1,17},{2,10},{3,19},{4,12},{5,21},{6,14},{7,23},{8,0},{9,25... | collective-permute-start | bytes 393224 | tf_op jit(solution)/shard_map/ppermute | solution.py:29
  13.9 0.6 %collective-permute-done.8 = bf16[2,2,2,16,1024]{4,3,2,1,0:T(8,128)(2,1)S(1)} collective-permute-done((bf16[2,2,2,16,1024]{4,3,2,1,0:T(8,128)(2,1)S(1)}, bf16[2,2,2,16,1024]{4,3,2,1,0:T(8,128)(2,1)S(1)}, u32[]{:S(2)}, u32[]{:S(2)}) %collective-permute-start.8) | collective-permute-done | bytes 262176 | tf_op jit(solution)/shard_map/ppermute | solution.py:29
  14.5 0.0 collective-permute-done.7
  14.5 0.1 convert_add_fusion
  14.6 2.0 %collective-permute-start.9 = (bf16[2,2,16,1024]{3,2,1,0:T(8,128)(2,1)S(1)}, bf16[2,2,16,1024]{3,2,1,0:T(8,128)(2,1)S(1)}, u32[]{:S(2)}, u32[]{:S(2)}) collective-permute-start(bf16[2,2,16,1024]{3,2,1,0:T(8,128)(2,1)S(1)} %pad_maximum_fusion.2), channel_id=1, source_target_pairs={{0,8},{1,17},{2,10},{3,19},{4,12},{5,21},{6,14},{7,23},{8,0},{9,25... | collective-permute-start | bytes 393224 | tf_op jit(solution)/shard_map/ppermute | solution.py:29
  16.7 0.8 %collective-permute-done.4 = bf16[2,2,16,1024]{3,2,1,0:T(8,128)(2,1)S(1)} collective-permute-done((bf16[2,2,16,1024]{3,2,1,0:T(8,128)(2,1)S(1)}, bf16[2,2,16,1024]{3,2,1,0:T(8,128)(2,1)S(1)}, u32[]{:S(2)}, u32[]{:S(2)}) %collective-permute-start.4) | collective-permute-done | bytes 131104 | tf_op jit(solution)/shard_map/ppermute | solution.py:29
  17.7 2.8 %collective-permute-start.5 = (bf16[2,16,1024]{2,1,0:T(8,128)(2,1)S(1)}, bf16[2,16,1024]{2,1,0:T(8,128)(2,1)S(1)}, u32[]{:S(2)}, u32[]{:S(2)}) collective-permute-start(bf16[2,16,1024]{2,1,0:T(8,128)(2,1)S(1)} %fusion.4), channel_id=1, source_target_pairs={{0,16},{1,5},{2,18},{3,7},{4,20},{5,1},{6,22},{7,3},{8,24},{9,13},... | collective-permute-start | bytes 196616 | tf_op jit(solution)/shard_map/ppermute | solution.py:29
  20.4 0.2 collective-permute-done.9
  20.7 2.5 %collective-permute-start.10 = (bf16[2,16,1024]{2,1,0:T(8,128)(2,1)S(1)}, bf16[2,16,1024]{2,1,0:T(8,128)(2,1)S(1)}, u32[]{:S(2)}, u32[]{:S(2)}) collective-permute-start(bf16[2,16,1024]{2,1,0:T(8,128)(2,1)S(1)} %fusion.7), channel_id=1, source_target_pairs={{0,16},{1,5},{2,18},{3,7},{4,20},{5,1},{6,22},{7,3},{8,24},{9,13},... | collective-permute-start | bytes 196616 | tf_op jit(solution)/shard_map/ppermute | solution.py:29
  23.1 0.0 collective-permute-done.5
  23.2 1.6 %collective-permute-start.6 = (bf16[2,16,1024]{2,1,0:T(8,128)(2,1)S(1)}, bf16[2,16,1024]{2,1,0:T(8,128)(2,1)S(1)}, u32[]{:S(2)}, u32[]{:S(2)}) collective-permute-start(bf16[2,16,1024]{2,1,0:T(8,128)(2,1)S(1)} %fusion.1), channel_id=1, source_target_pairs={{0,2},{1,3},{2,0},{3,1},{4,6},{5,7},{6,4},{7,5},{8,10},{9,11},{10,... | collective-permute-start | bytes 196616 | tf_op jit(solution)/shard_map/ppermute | solution.py:29
  24.7 1.2 %collective-permute-done.10 = bf16[2,16,1024]{2,1,0:T(8,128)(2,1)S(1)} collective-permute-done((bf16[2,16,1024]{2,1,0:T(8,128)(2,1)S(1)}, bf16[2,16,1024]{2,1,0:T(8,128)(2,1)S(1)}, u32[]{:S(2)}, u32[]{:S(2)}) %collective-permute-start.10) | collective-permute-done | bytes 65568 | tf_op jit(solution)/shard_map/ppermute | solution.py:29
  25.9 1.6 %collective-permute-start.11 = (bf16[2,16,1024]{2,1,0:T(8,128)(2,1)S(1)}, bf16[2,16,1024]{2,1,0:T(8,128)(2,1)S(1)}, u32[]{:S(2)}, u32[]{:S(2)}) collective-permute-start(bf16[2,16,1024]{2,1,0:T(8,128)(2,1)S(1)} %fusion), channel_id=1, source_target_pairs={{0,2},{1,3},{2,0},{3,1},{4,6},{5,7},{6,4},{7,5},{8,10},{9,11},{10,... | collective-permute-start | bytes 196616 | tf_op jit(solution)/shard_map/ppermute | solution.py:29
  27.6 0.0 collective-permute-done.13.refs_4_
  27.6 0.0 collective-permute-start.14
  27.6 0.5 %collective-permute-start.15 = (f32[3,16,2048]{2,1,0:T(8,128)S(1)}, f32[3,16,2048]{2,1,0:T(8,128)S(1)}, u32[]{:S(2)}, u32[]{:S(2)}) collective-permute-start(f32[3,16,2048]{2,1,0:T(8,128)S(1)} %collective-permute-done.13.refs_4_), channel_id=1, source_target_pairs={{0,1},{1,0},{2,3},{3,2},{4,5},{5,4},{6,7},{7,6},{8,9},{9,8},{10,11... | collective-permute-start | bytes 1179656 | tf_op jit(solution)/shard_map/ppermute | solution.py:29
  28.1 0.0 collective-permute-done.6
  28.1 0.1 collective-permute-start.12
  28.2 2.1 %collective-permute-done.11 = bf16[2,16,1024]{2,1,0:T(8,128)(2,1)S(1)} collective-permute-done((bf16[2,16,1024]{2,1,0:T(8,128)(2,1)S(1)}, bf16[2,16,1024]{2,1,0:T(8,128)(2,1)S(1)}, u32[]{:S(2)}, u32[]{:S(2)}) %collective-permute-start.11) | collective-permute-done | bytes 65568 | tf_op jit(solution)/shard_map/ppermute | solution.py:29
  30.3 0.1 collective-permute-start.16
  30.4 0.0 collective-permute-done.12.refs_2_
  30.4 0.0 collective-permute-done.14.refs_5_.refs_1_
  30.4 0.0 collective-permute-done.15.refs_6_.refs_2_
  30.4 1.1 %shard_map.102 = (f32[16,2048]{1,0:T(8,128)}, f32[16,2048]{1,0:T(8,128)}, f32[16,2048]{1,0:T(8,128)}, bf16[16,8192]{1,0:T(8,128)(2,1)}, f32[16,2048]{1,0:T(8,128...) custom-call(f32[2,16,1024]{2,1,0:T(8,128)S(1)} %add_multiply_fusion.1.refs_0_, f32[2,16,1024]{2,1,0:T(8,128)S(1)} %add_multiply_fusion.refs_1_, ...), custom_call_target="tpu_custom_call" | custom-call | flops 5242880 | bytes 1572864 | tf_op jit(solution)/shard_map/pallas_call | solution.py:168
  31.5 0.2 collective-permute-done.16.refs_0_
  31.7 0.8 %shard_map.103 = (bf16[16,8192]{1,0:T(8,128)(2,1)}, f32[16,2048]{1,0:T(8,128)}, f32[16,2048]{1,0:T(8,128)}, f32[16,2048]{1,0:T(8,128)}) custom-call(f32[2,16,1024]{2,1,0:T(8,128)S(1)} %collective-permute-done.16.refs_0_, ...), custom_call_target="tpu_custom_call", output_to_operand_aliasing={{0}: (3, {}), {1}: (4, {}), {2}: (5, {}), {3}: (6, {})} | custom-call | tf_op jit(solution)/shard_map/pallas_call | solution.py:177
  (15 shorter events, 0.3 us)
Async XLA Ops:
  0.6 1.6 %copy-start = (bf16[1,1,128,8192]{3,2,1,0:T(8,128)(2,1)S(1)}, bf16[1,1,128,8192]{3,2,1,0:T(8,128)(2,1)}, u32[]{:S(2)}) copy-start(bf16[1,1,128,8192]{3,2,1,0:T(8,128)(2,1)} %param.4) | copy-start | bytes 6291460
  2.5 4.8 %copy-start.1 = (bf16[1,1,128,8192]{3,2,1,0:T(8,128)(2,1)S(1)}, bf16[1,1,128,8192]{3,2,1,0:T(8,128)(2,1)}, u32[]{:S(2)}) copy-start(bf16[1,1,128,8192]{3,2,1,0:T(8,128)(2,1)} %param.4) | copy-start | bytes 6291460
  2.5 1.7 %collective-permute-start.2 = (bf16[2,2,2,16,1024]{4,3,2,1,0:T(8,128)(2,1)S(1)}, bf16[2,2,2,16,1024]{4,3,2,1,0:T(8,128)(2,1)S(1)}, u32[]{:S(2)}, u32[]{:S(2)}) collective-permute-start(bf16[2,2,2,16,1024]{4,3,2,1,0:T(8,128)(2,1)S(1)} %get-tuple-element.33), channel_id=1, source_target_pairs={{0,1},{1,0},{2,3},{3,2},{4,5},{5,4},{6,7},{7,6},{8,9},{9,8},{10,11... | collective-permute-start | bytes 786440 | tf_op jit(solution)/shard_map/ppermute | solution.py:29
  3.3 6.5 %copy-start.2 = (f32[16,2048]{1,0:T(8,128)S(1)}, f32[16,2048]{1,0:T(8,128)}, u32[]{:S(2)}) copy-start(f32[16,2048]{1,0:T(8,128)} %param.7) | copy-start | bytes 393220
  3.3 6.5 %copy-start.3 = (f32[16,2048]{1,0:T(8,128)S(1)}, f32[16,2048]{1,0:T(8,128)}, u32[]{:S(2)}) copy-start(f32[16,2048]{1,0:T(8,128)} %param.6) | copy-start | bytes 393220
  3.3 6.4 %copy-start.4 = (f32[16,2048]{1,0:T(8,128)S(1)}, f32[16,2048]{1,0:T(8,128)}, u32[]{:S(2)}) copy-start(f32[16,2048]{1,0:T(8,128)} %param.5) | copy-start | bytes 393220
  3.3 3.9 %collective-permute-start = (bf16[2,2,2,16,1024]{4,3,2,1,0:T(8,128)(2,1)S(1)}, bf16[2,2,2,16,1024]{4,3,2,1,0:T(8,128)(2,1)S(1)}, u32[]{:S(2)}, u32[]{:S(2)}) collective-permute-start(bf16[2,2,2,16,1024]{4,3,2,1,0:T(8,128)(2,1)S(1)} %get-tuple-element.36), channel_id=1, source_target_pairs={{0,1},{1,0},{2,3},{3,2},{4,5},{5,4},{6,7},{7,6},{8,9},{9,8},{10,11... | collective-permute-start | bytes 786440 | tf_op jit(solution)/shard_map/ppermute | solution.py:29
  4.3 7.3 %collective-permute-start.3 = (bf16[2,2,2,16,1024]{4,3,2,1,0:T(8,128)(2,1)S(1)}, bf16[2,2,2,16,1024]{4,3,2,1,0:T(8,128)(2,1)S(1)}, u32[]{:S(2)}, u32[]{:S(2)}) collective-permute-start(bf16[2,2,2,16,1024]{4,3,2,1,0:T(8,128)(2,1)S(1)} %add_convert_fusion), channel_id=1, source_target_pairs={{0,4},{1,9},{2,6},{3,11},{4,0},{5,13},{6,2},{7,15},{8,12},{9,1},{1... | collective-permute-start | bytes 786440 | tf_op jit(solution)/shard_map/ppermute | solution.py:29
  7.9 3.7 %collective-permute-start.1 = (bf16[2,2,2,16,1024]{4,3,2,1,0:T(8,128)(2,1)S(1)}, bf16[2,2,2,16,1024]{4,3,2,1,0:T(8,128)(2,1)S(1)}, u32[]{:S(2)}, u32[]{:S(2)}) collective-permute-start(bf16[2,2,2,16,1024]{4,3,2,1,0:T(8,128)(2,1)S(1)} %get-tuple-element.39), channel_id=1, source_target_pairs={{0,1},{1,0},{2,3},{3,2},{4,5},{5,4},{6,7},{7,6},{8,9},{9,8},{10,11... | collective-permute-start | bytes 786440 | tf_op jit(solution)/shard_map/ppermute | solution.py:29
  8.0 6.4 %collective-permute-start.8 = (bf16[2,2,2,16,1024]{4,3,2,1,0:T(8,128)(2,1)S(1)}, bf16[2,2,2,16,1024]{4,3,2,1,0:T(8,128)(2,1)S(1)}, u32[]{:S(2)}, u32[]{:S(2)}) collective-permute-start(bf16[2,2,2,16,1024]{4,3,2,1,0:T(8,128)(2,1)S(1)} %add_convert_fusion.1), channel_id=1, source_target_pairs={{0,4},{1,9},{2,6},{3,11},{4,0},{5,13},{6,2},{7,15},{8,12},{9,1},{1... | collective-permute-start | bytes 786440 | tf_op jit(solution)/shard_map/ppermute | solution.py:29
  9.4 5.1 %collective-permute-start.7 = (bf16[2,2,2,16,1024]{4,3,2,1,0:T(8,128)(2,1)S(1)}, bf16[2,2,2,16,1024]{4,3,2,1,0:T(8,128)(2,1)S(1)}, u32[]{:S(2)}, u32[]{:S(2)}) collective-permute-start(bf16[2,2,2,16,1024]{4,3,2,1,0:T(8,128)(2,1)S(1)} %get-tuple-element.42), channel_id=1, source_target_pairs={{0,1},{1,0},{2,3},{3,2},{4,5},{5,4},{6,7},{7,6},{8,9},{9,8},{10,11... | collective-permute-start | bytes 786440 | tf_op jit(solution)/shard_map/ppermute | solution.py:29
  9.8 17.8 %collective-permute-start.13 = (f32[3,16,2048]{2,1,0:T(8,128)S(1)}, f32[3,16,2048]{2,1,0:T(8,128)S(1)}, u32[]{:S(2)}, u32[]{:S(2)}) collective-permute-start(f32[3,16,2048]{2,1,0:T(8,128)S(1)} %pad_maximum_fusion.refs_3_), channel_id=1, source_target_pairs={{0,2},{1,3},{2,0},{3,1},{4,6},{5,7},{6,4},{7,5},{8,10},{9,11},{10,... | collective-permute-start | bytes 1179656 | tf_op jit(solution)/shard_map/ppermute | solution.py:29
  11.7 5.9 %collective-permute-start.4 = (bf16[2,2,16,1024]{3,2,1,0:T(8,128)(2,1)S(1)}, bf16[2,2,16,1024]{3,2,1,0:T(8,128)(2,1)S(1)}, u32[]{:S(2)}, u32[]{:S(2)}) collective-permute-start(bf16[2,2,16,1024]{3,2,1,0:T(8,128)(2,1)S(1)} %pad_maximum_fusion.1), channel_id=1, source_target_pairs={{0,8},{1,17},{2,10},{3,19},{4,12},{5,21},{6,14},{7,23},{8,0},{9,25... | collective-permute-start | bytes 393224 | tf_op jit(solution)/shard_map/ppermute | solution.py:29
  14.6 6.0 %collective-permute-start.9 = (bf16[2,2,16,1024]{3,2,1,0:T(8,128)(2,1)S(1)}, bf16[2,2,16,1024]{3,2,1,0:T(8,128)(2,1)S(1)}, u32[]{:S(2)}, u32[]{:S(2)}) collective-permute-start(bf16[2,2,16,1024]{3,2,1,0:T(8,128)(2,1)S(1)} %pad_maximum_fusion.2), channel_id=1, source_target_pairs={{0,8},{1,17},{2,10},{3,19},{4,12},{5,21},{6,14},{7,23},{8,0},{9,25... | collective-permute-start | bytes 393224 | tf_op jit(solution)/shard_map/ppermute | solution.py:29
  17.7 5.5 %collective-permute-start.5 = (bf16[2,16,1024]{2,1,0:T(8,128)(2,1)S(1)}, bf16[2,16,1024]{2,1,0:T(8,128)(2,1)S(1)}, u32[]{:S(2)}, u32[]{:S(2)}) collective-permute-start(bf16[2,16,1024]{2,1,0:T(8,128)(2,1)S(1)} %fusion.4), channel_id=1, source_target_pairs={{0,16},{1,5},{2,18},{3,7},{4,20},{5,1},{6,22},{7,3},{8,24},{9,13},... | collective-permute-start | bytes 196616 | tf_op jit(solution)/shard_map/ppermute | solution.py:29
  20.7 5.2 %collective-permute-start.10 = (bf16[2,16,1024]{2,1,0:T(8,128)(2,1)S(1)}, bf16[2,16,1024]{2,1,0:T(8,128)(2,1)S(1)}, u32[]{:S(2)}, u32[]{:S(2)}) collective-permute-start(bf16[2,16,1024]{2,1,0:T(8,128)(2,1)S(1)} %fusion.7), channel_id=1, source_target_pairs={{0,16},{1,5},{2,18},{3,7},{4,20},{5,1},{6,22},{7,3},{8,24},{9,13},... | collective-permute-start | bytes 196616 | tf_op jit(solution)/shard_map/ppermute | solution.py:29
  23.2 4.9 %collective-permute-start.6 = (bf16[2,16,1024]{2,1,0:T(8,128)(2,1)S(1)}, bf16[2,16,1024]{2,1,0:T(8,128)(2,1)S(1)}, u32[]{:S(2)}, u32[]{:S(2)}) collective-permute-start(bf16[2,16,1024]{2,1,0:T(8,128)(2,1)S(1)} %fusion.1), channel_id=1, source_target_pairs={{0,2},{1,3},{2,0},{3,1},{4,6},{5,7},{6,4},{7,5},{8,10},{9,11},{10,... | collective-permute-start | bytes 196616 | tf_op jit(solution)/shard_map/ppermute | solution.py:29
  25.9 4.3 %collective-permute-start.11 = (bf16[2,16,1024]{2,1,0:T(8,128)(2,1)S(1)}, bf16[2,16,1024]{2,1,0:T(8,128)(2,1)S(1)}, u32[]{:S(2)}, u32[]{:S(2)}) collective-permute-start(bf16[2,16,1024]{2,1,0:T(8,128)(2,1)S(1)} %fusion), channel_id=1, source_target_pairs={{0,2},{1,3},{2,0},{3,1},{4,6},{5,7},{6,4},{7,5},{8,10},{9,11},{10,... | collective-permute-start | bytes 196616 | tf_op jit(solution)/shard_map/ppermute | solution.py:29
  27.6 2.8 %collective-permute-start.14 = (f32[3,16,2048]{2,1,0:T(8,128)S(1)}, f32[3,16,2048]{2,1,0:T(8,128)S(1)}, u32[]{:S(2)}, u32[]{:S(2)}) collective-permute-start(f32[3,16,2048]{2,1,0:T(8,128)S(1)} %pad_maximum_fusion.refs_3_), channel_id=1, source_target_pairs={{0,1},{1,0},{2,3},{3,2},{4,5},{5,4},{6,7},{7,6},{8,9},{9,8},{10,11... | collective-permute-start | bytes 1179656 | tf_op jit(solution)/shard_map/ppermute | solution.py:29
  27.6 2.8 %collective-permute-start.15 = (f32[3,16,2048]{2,1,0:T(8,128)S(1)}, f32[3,16,2048]{2,1,0:T(8,128)S(1)}, u32[]{:S(2)}, u32[]{:S(2)}) collective-permute-start(f32[3,16,2048]{2,1,0:T(8,128)S(1)} %collective-permute-done.13.refs_4_), channel_id=1, source_target_pairs={{0,1},{1,0},{2,3},{3,2},{4,5},{5,4},{6,7},{7,6},{8,9},{9,8},{10,11... | collective-permute-start | bytes 1179656 | tf_op jit(solution)/shard_map/ppermute | solution.py:29
  28.1 2.3 %collective-permute-start.12 = (f32[2,16,1024]{2,1,0:T(8,128)S(1)}, f32[2,16,1024]{2,1,0:T(8,128)S(1)}, u32[]{:S(2)}, u32[]{:S(2)}) collective-permute-start(f32[2,16,1024]{2,1,0:T(8,128)S(1)} %add_multiply_fusion.1.refs_0_), channel_id=1, source_target_pairs={{0,1},{1,0},{2,3},{3,2},{4,5},{5,4},{6,7},{7,6},{8,9},{9,8},{10,11... | collective-permute-start | bytes 393224 | tf_op jit(solution)/shard_map/ppermute | solution.py:29
  30.3 1.4 %collective-permute-start.16 = (f32[2,16,1024]{2,1,0:T(8,128)S(1)}, f32[2,16,1024]{2,1,0:T(8,128)S(1)}, u32[]{:S(2)}, u32[]{:S(2)}) collective-permute-start(f32[2,16,1024]{2,1,0:T(8,128)S(1)} %add_multiply_fusion.refs_1_), channel_id=1, source_target_pairs={{0,1},{1,0},{2,3},{3,2},{4,5},{5,4},{6,7},{7,6},{8,9},{9,8},{10,11... | collective-permute-start | bytes 393224 | tf_op jit(solution)/shard_map/ppermute | solution.py:29

commit v7 on v6

--- a/solution.py
+++ b/solution.py
@@ -17,10 +17,9 @@
 BF16 = jnp.bfloat16
 BOTH = ("fsdp", "grp")
 SHARES = [1, 1]
-ORDERS = [[[0, 1, 2], [1, 2, 0]], [[0, 1, 2], [1, 2, 0]]]
+ORDERS = [[1, 0], [0, 1]]
 VMEM = pl.BlockSpec(memory_space=pltpu.VMEM)
 ANY = pl.BlockSpec(memory_space=pl.ANY)
-HBM = pl.BlockSpec(memory_space=pl.ANY)
 LIMIT = 4 * 2**20
 
 
@@ -51,10 +50,10 @@
 
 def first_block(core, me_f, j, away):
     low, high = me_f & 1, (me_f >> 1) & 1
-    return jnp.where(core == 0, low ^ away, j), jnp.where(core == 0, j, high ^ away)
-
-
-def gathered(g, wanted, cut, rows, nf, ng, limit):
+    return jnp.where(core == 0, j, low ^ away), jnp.where(core == 0, high ^ away, j)
+
+
+def gathered(g, wanted, cut, rows, nf, ng):
     cols = g.shape[1] // ng
     blocks = g.reshape(nf // 4, 2, 2, rows, g.shape[1])
 
@@ -79,27 +78,27 @@
     flat = pl.pallas_call(
         kernel,
         out_shape=[jax.ShapeDtypeStruct((2, nf // 4, ng // 2, rows, w), g.dtype) for _ in wanted for _, w in cut],
-        in_specs=[HBM],
+        in_specs=[ANY],
         out_specs=[VMEM] * (len(wanted) * len(cut)),
         scratch_shapes=[pltpu.SemaphoreType.DMA((ng * len(wanted) * len(cut),))],
-        compiler_params=pltpu.CompilerParams(vmem_limit_bytes=limit),
+        compiler_params=pltpu.CompilerParams(vmem_limit_bytes=LIMIT),
         cost_estimate=pl.CostEstimate(flops=0, bytes_accessed=g.size * len(wanted), transcendentals=0),
     )(blocks)
     return [list(flat[n * len(cut) : (n + 1) * len(cut)]) for n in range(len(wanted))]
 
 
-def gathered_plain(g, wanted, cut, rows, nf, ng, limit):
+def gathered_plain(g, wanted, cut, rows, nf, ng):
     cols = g.shape[1] // ng
     blocks = g.reshape(nf // 4, 2, 2, rows, g.shape[1])
     me_f, me_g = lax.axis_index("fsdp"), lax.axis_index("grp")
 
-    def block(core, k, away, j, x, start, width):
+    def block(core, away, j, x, start, width):
         low, high = first_block(core, me_f, j, away)
         part = lax.dynamic_slice(blocks, (0, high, low, 0, (2 * x + core) * cols + start), (nf // 4, 1, 1, rows, width))
         return part[:, 0, 0]
 
     return [
-        [jnp.stack([jnp.stack([block((me_g & 1) ^ sibling, k, away, j, x, a, w) for x in range(ng // 2)], 1) for j in range(2)]) for k, (a, w) in enumerate(cut)]
+        [jnp.stack([jnp.stack([block((me_g & 1) ^ sibling, away, j, x, a, w) for x in range(ng // 2)], 1) for j in range(2)]) for a, w in cut]
         for sibling, away in wanted
     ]
 
@@ -190,18 +189,15 @@
     me = lax.axis_index("grp")
     own, other = jnp.concatenate(own, -1), jnp.concatenate(other, -1)
     ng = 2 * len(states)
+    gradient = jnp.stack([pick((own, other)[r & 1], (me >> 1) ^ (r >> 1), 0) for r in range(ng)])
+    state = jnp.stack([(states, near)[r & 1][r >> 1] for r in range(ng)])
+    new = updated(gradient, state[:, 0], state[:, 1], state[:, 2])
+    blocks = new[0].astype(BF16)
     weights = jnp.zeros((own.shape[1], cols * ng), BF16)
+    for r in range(ng):
+        weights = lax.dynamic_update_slice(weights, blocks[r], (0, (me ^ r) * cols))
     last = (me + ng - 1) % ng
-    for k in range(ng // 2):
-        for odd, grad, state in ((0, own, states[k]), (1, other, near[k])):
-            new = updated(pick(grad, (me >> 1) ^ k, 0), *state)
-            owner = me ^ (2 * k + odd)
-            weights = lax.dynamic_update_slice(weights, new[0].astype(BF16), (0, owner * cols))
-            if k == 0 and odd == 0:
-                mine = new
-            if odd:
-                copies = new if k == 0 else [jnp.where(owner == last, a, b) for a, b in zip(new, copies)]
-    return (*mine, weights, *copies)
+    return (*[n[0] for n in new], weights, *[pick(n, me ^ last, 0) for n in new])
 
 
 def onward(t, core, me_f, labels, want):
@@ -234,36 +230,34 @@
 
     gather = gathered if local else gathered_plain
     away_out, away_own = [], []
-    source = g
     for edge in cut:
-        (out,), (mine,) = gather(source, [(1, 1), (0, 1)], [edge], rows, nf, ng, LIMIT)
-        source = lax.optimization_barrier((g, out))[0]
+        (out,), (mine,) = gather(g, [(1, 1), (0, 1)], [edge], rows, nf, ng)
         away_out.append(out)
         away_own.append(mine)
     split = lambda t: t.reshape((2,) * (f_bits - 1) + t.shape[2:])
     got_away = [split(swap(t, [1, 1])) for t in away_out]
     sent = [(split(t).astype(F32) + x.astype(F32)).astype(BF16) for t, x in zip(away_own, got_away)]
     later = lax.optimization_barrier((g, sent[-1]))[0]
-    kept_out, kept_own = gather(later, [(1, 0), (0, 0)], cut, rows, nf, ng, LIMIT)
+    kept_out, kept_own = gather(later, [(1, 0), (0, 0)], cut, rows, nf, ng)
     got_kept = [split(swap(t, [1, 1])) for t in kept_out]
     kept = [split(t).astype(F32) + x.astype(F32) for t, x in zip(kept_own, got_kept)]
 
     high = list(range(f_bits - 1, 1, -1))
-    labels = [[[1] + high, [0] + high] for _ in cut]
-    orders = [[o + [b for b in range(f_bits) if b not in o] for o in ORDERS[k % 2]] for k in range(len(cut))]
+    labels = [[[0] + high, [1] + high] for _ in cut]
+    orders = [o + list(range(len(o), f_bits)) for o in ORDERS]
     for step in range(f_bits):
-        masks = [[ng << o[step] for o in pair] for pair in orders]
+        masks = [ng << o[step] for o in orders]
         if step == 0:
             held = lax.optimization_barrier(((master, moment_one, moment_two), sent[-1]))[0]
             states = [jnp.stack(held)]
             for b in range(1, g_bits):
                 states = states + [swap(s, [1 << b] * 2) for s in states]
-        got = [swap(s, m) for s, m in zip(sent, masks)]
-
+        got = [swap(s, masks) for s in sent]
         ts = [k + x.astype(F32) for k, x in zip(kept, got)]
         if step == f_bits - 1:
             break
-        moved = [onward(t, core, me_f, pair, [o[step + 1] for o in order]) for t, pair, order in zip(ts, labels, orders)]
+        want = [o[step + 1] for o in orders]
+        moved = [onward(t, core, me_f, names, want) for t, names in zip(ts, labels)]
         sent, kept, labels = [list(m) for m in zip(*moved)]
 
     for b in range(1, g_bits):
@@ -271,7 +265,6 @@
         if b == g_bits - 1:
             states = lax.optimization_barrier((states, rounded[-1]))[0]
             near = [swap(s, [1, 1]) for s in states]
-
         got = [swap(t, [1 << b] * 2) for t in rounded]
         ts = [t.astype(F32) + x.astype(F32) for t, x in zip(rounded, got)]
     own = [t / (ng * nf) for t in ts]

time: 32.7 us -> 32.4 us (level)
  waiting for transfers between devices: 6.12 us -> 5.03 us
  starting transfers between devices: 20.2 us -> 21.2 us
    ppermute x17, waiting for transfers between devices: 6.12 us -> 5.03 us  [swap(): return lax.ppermute(x, BOTH, [(i, i ^ masks[i & 1]) for i in range(n)])]
    ppermute x17, starting transfers between devices: 20.2 us -> 21.2 us  [swap(): return lax.ppermute(x, BOTH, [(i, i ^ masks[i & 1]) for i in range(n)])]
where the time goes in v7:
time: 32.4 us; the launch traced here: 32.3 us
  starting transfers between devices  21.2 us (65%)
  waiting for transfers between devices  5.03 us (16%)
  Pallas kernels  3.04 us (9%)
  local copies, waits for them, and re-layouts  1.69 us (5%)
  between operations  0.88 us (3%)
  other arithmetic  0.49 us (2%)
    ppermute x17, starting transfers between devices, swap(): return lax.ppermute(x, BOTH, [(i, i ^ masks[i & 1]) for i in range(n)])  21.2 us
    ppermute x17, waiting for transfers between devices, swap(): return lax.ppermute(x, BOTH, [(i, i ^ masks[i & 1]) for i in range(n)])  5.03 us
    unnamed x10, local copies, waits for them, and re-layouts  1.61 us
    pallas_call x1, Pallas kernels, finish(): pl.pallas_call(functools.partial(kernel, True), out_shape=[shape] * 3 + s...  1.1 us
    pallas_call x3, Pallas kernels, gathered(): pl.pallas_call(kernel, out_shape=[jax.ShapeDtypeStruct((2, nf // 4, ng //...  1.09 us
    pallas_call x1, Pallas kernels, finish(): pl.pallas_call(functools.partial(kernel, False), out_shape=shapes, in_spe...  0.85 us
  transfers between devices with their start and end apart: 17, of which 8 were waited for; matrix products, arithmetic and copies ran while one was open for 2% of the time, Pallas kernels for 6%

profile of v7, /device:TPU:0, one launch (start us, length us, event | category | flops | bytes accessed | tf_op | source)
XLA Modules:
  0.0 32.3 jit_solution(5191228119916975067)
XLA Ops:
  0.6 0.0 copy-start
  0.6 1.6 %copy-done = bf16[1,1,128,8192]{3,2,1,0:T(8,128)(2,1)S(1)} copy-done((bf16[1,1,128,8192]{3,2,1,0:T(8,128)(2,1)S(1)}, bf16[1,1,128,8192]{3,2,1,0:T(8,128)(2,1)}, u32[]{:S(2)}) %copy-start) | copy-done | bytes 2097176
  2.2 0.3 shard_map.101
  2.5 0.0 copy-start.1
  2.5 0.5 %collective-permute-start.2 = (bf16[2,2,2,16,1024]{4,3,2,1,0:T(8,128)(2,1)S(1)}, bf16[2,2,2,16,1024]{4,3,2,1,0:T(8,128)(2,1)S(1)}, u32[]{:S(2)}, u32[]{:S(2)}) collective-permute-start(bf16[2,2,2,16,1024]{4,3,2,1,0:T(8,128)(2,1)S(1)} %get-tuple-element.38), channel_id=1, source_target_pairs={{0,1},{1,0},{2,3},{3,2},{4,5},{5,4},{6,7},{7,6},{8,9},{9,8},{10,11... | collective-permute-start | bytes 786440 | tf_op jit(solution)/shard_map/ppermute | solution.py:28
  3.0 0.3 shard_map.99
  3.3 0.0 copy-start.2
  3.3 0.0 copy-start.3
  3.3 0.0 copy-start.4
  3.3 0.1 collective-permute-start
  3.4 0.7 %collective-permute-done.2 = bf16[2,2,2,16,1024]{4,3,2,1,0:T(8,128)(2,1)S(1)} collective-permute-done((bf16[2,2,2,16,1024]{4,3,2,1,0:T(8,128)(2,1)S(1)}, bf16[2,2,2,16,1024]{4,3,2,1,0:T(8,128)(2,1)S(1)}, u32[]{:S(2)}, u32[]{:S(2)}) %collective-permute-start.2) | collective-permute-done | bytes 262176 | tf_op jit(solution)/shard_map/ppermute | solution.py:28
  4.2 0.1 add_convert_fusion
  4.3 3.0 %collective-permute-start.3 = (bf16[2,2,2,16,1024]{4,3,2,1,0:T(8,128)(2,1)S(1)}, bf16[2,2,2,16,1024]{4,3,2,1,0:T(8,128)(2,1)S(1)}, u32[]{:S(2)}, u32[]{:S(2)}) collective-permute-start(bf16[2,2,2,16,1024]{4,3,2,1,0:T(8,128)(2,1)S(1)} %add_convert_fusion), channel_id=1, source_target_pairs={{0,8},{1,5},{2,10},{3,7},{4,12},{5,1},{6,14},{7,3},{8,0},{9,13},{1... | collective-permute-start | bytes 786440 | tf_op jit(solution)/shard_map/ppermute | solution.py:28
  7.3 0.0 collective-permute-done
  7.3 0.1 add_convert_fusion.1
  7.3 0.0 copy-done.1
  7.3 0.6 %shard_map.100 = (bf16[2,2,2,16,1024]{4,3,2,1,0:T(8,128)(2,1)S(1)}, bf16[2,2,2,16,1024]{4,3,2,1,0:T(8,128)(2,1)S(1)}, bf16[2,2,2,16,1024]{4,3,2,1,0:T(8,128)(2,1)S(1)}, bf16[2,2,2,16,1024]{4,3,2,1,0:T(8,128)(2,1)S(1)}) custom-call(bf16[2,2,2,16,8192]{4,3,2,1,0:T(8,128)(2,1)S(1)} %bitcast.28), custom_call_target="tpu_custom_call" | custom-call | bytes 2097152 | tf_op jit(solution)/shard_map/pallas_call | solution.py:78
  7.9 0.1 collective-permute-start.1
  8.0 1.3 %collective-permute-start.8 = (bf16[2,2,2,16,1024]{4,3,2,1,0:T(8,128)(2,1)S(1)}, bf16[2,2,2,16,1024]{4,3,2,1,0:T(8,128)(2,1)S(1)}, u32[]{:S(2)}, u32[]{:S(2)}) collective-permute-start(bf16[2,2,2,16,1024]{4,3,2,1,0:T(8,128)(2,1)S(1)} %add_convert_fusion.1), channel_id=1, source_target_pairs={{0,8},{1,5},{2,10},{3,7},{4,12},{5,1},{6,14},{7,3},{8,0},{9,13},{1... | collective-permute-start | bytes 786440 | tf_op jit(solution)/shard_map/ppermute | solution.py:28
  9.4 0.4 %collective-permute-start.7 = (bf16[2,2,2,16,1024]{4,3,2,1,0:T(8,128)(2,1)S(1)}, bf16[2,2,2,16,1024]{4,3,2,1,0:T(8,128)(2,1)S(1)}, u32[]{:S(2)}, u32[]{:S(2)}) collective-permute-start(bf16[2,2,2,16,1024]{4,3,2,1,0:T(8,128)(2,1)S(1)} %get-tuple-element.40), channel_id=1, source_target_pairs={{0,1},{1,0},{2,3},{3,2},{4,5},{5,4},{6,7},{7,6},{8,9},{9,8},{10,11... | collective-permute-start | bytes 786440 | tf_op jit(solution)/shard_map/ppermute | solution.py:28
  9.7 0.0 copy-done.2
  9.8 0.0 copy-done.3
  9.8 0.0 copy-done.4
  9.8 1.6 %collective-permute-start.13 = (f32[3,16,2048]{2,1,0:T(8,128)S(1)}, f32[3,16,2048]{2,1,0:T(8,128)S(1)}, u32[]{:S(2)}, u32[]{:S(2)}) collective-permute-start(f32[3,16,2048]{2,1,0:T(8,128)S(1)} %pad_maximum_fusion.refs_3_), channel_id=1, source_target_pairs={{0,2},{1,3},{2,0},{3,1},{4,6},{5,7},{6,4},{7,5},{8,10},{9,11},{10,... | collective-permute-start | bytes 1179656 | tf_op jit(solution)/shard_map/ppermute | solution.py:28
  11.3 0.3 collective-permute-done.3
  11.6 0.0 collective-permute-done.1
  11.6 0.1 convert_add_fusion.1
  11.8 2.0 %collective-permute-start.4 = (bf16[2,2,16,1024]{3,2,1,0:T(8,128)(2,1)S(1)}, bf16[2,2,16,1024]{3,2,1,0:T(8,128)(2,1)S(1)}, u32[]{:S(2)}, u32[]{:S(2)}) collective-permute-start(bf16[2,2,16,1024]{3,2,1,0:T(8,128)(2,1)S(1)} %fusion), channel_id=1, source_target_pairs={{0,4},{1,9},{2,6},{3,11},{4,0},{5,13},{6,2},{7,15},{8,12},{9,1},{1... | collective-permute-start | bytes 393224 | tf_op jit(solution)/shard_map/ppermute | solution.py:28
  13.8 1.1 %collective-permute-done.8 = bf16[2,2,2,16,1024]{4,3,2,1,0:T(8,128)(2,1)S(1)} collective-permute-done((bf16[2,2,2,16,1024]{4,3,2,1,0:T(8,128)(2,1)S(1)}, bf16[2,2,2,16,1024]{4,3,2,1,0:T(8,128)(2,1)S(1)}, u32[]{:S(2)}, u32[]{:S(2)}) %collective-permute-start.8) | collective-permute-done | bytes 262176 | tf_op jit(solution)/shard_map/ppermute | solution.py:28
  14.9 0.0 collective-permute-done.7
  14.9 0.1 convert_add_fusion
  15.0 2.2 %collective-permute-start.9 = (bf16[2,2,16,1024]{3,2,1,0:T(8,128)(2,1)S(1)}, bf16[2,2,16,1024]{3,2,1,0:T(8,128)(2,1)S(1)}, u32[]{:S(2)}, u32[]{:S(2)}) collective-permute-start(bf16[2,2,16,1024]{3,2,1,0:T(8,128)(2,1)S(1)} %fusion.1), channel_id=1, source_target_pairs={{0,4},{1,9},{2,6},{3,11},{4,0},{5,13},{6,2},{7,15},{8,12},{9,1},{1... | collective-permute-start | bytes 393224 | tf_op jit(solution)/shard_map/ppermute | solution.py:28
  17.3 0.0 collective-permute-done.4
  17.3 2.7 %collective-permute-start.5 = (bf16[2,16,1024]{2,1,0:T(8,128)(2,1)S(1)}, bf16[2,16,1024]{2,1,0:T(8,128)(2,1)S(1)}, u32[]{:S(2)}, u32[]{:S(2)}) collective-permute-start(bf16[2,16,1024]{2,1,0:T(8,128)(2,1)S(1)} %fusion.4), channel_id=1, source_target_pairs={{0,16},{1,17},{2,18},{3,19},{4,20},{5,21},{6,22},{7,23},{8,24},{9,... | collective-permute-start | bytes 196616 | tf_op jit(solution)/shard_map/ppermute | solution.py:28
  20.0 0.2 collective-permute-done.9
  20.3 3.2 %collective-permute-start.10 = (bf16[2,16,1024]{2,1,0:T(8,128)(2,1)S(1)}, bf16[2,16,1024]{2,1,0:T(8,128)(2,1)S(1)}, u32[]{:S(2)}, u32[]{:S(2)}) collective-permute-start(bf16[2,16,1024]{2,1,0:T(8,128)(2,1)S(1)} %fusion.5), channel_id=1, source_target_pairs={{0,16},{1,17},{2,18},{3,19},{4,20},{5,21},{6,22},{7,23},{8,24},{9,... | collective-permute-start | bytes 196616 | tf_op jit(solution)/shard_map/ppermute | solution.py:28
  23.4 0.0 collective-permute-done.5
  23.4 1.6 %collective-permute-start.6 = (bf16[2,16,1024]{2,1,0:T(8,128)(2,1)S(1)}, bf16[2,16,1024]{2,1,0:T(8,128)(2,1)S(1)}, u32[]{:S(2)}, u32[]{:S(2)}) collective-permute-start(bf16[2,16,1024]{2,1,0:T(8,128)(2,1)S(1)} %fusion.3), channel_id=1, source_target_pairs={{0,2},{1,3},{2,0},{3,1},{4,6},{5,7},{6,4},{7,5},{8,10},{9,11},{10,... | collective-permute-start | bytes 196616 | tf_op jit(solution)/shard_map/ppermute | solution.py:28
  25.0 0.7 %collective-permute-done.10 = bf16[2,16,1024]{2,1,0:T(8,128)(2,1)S(1)} collective-permute-done((bf16[2,16,1024]{2,1,0:T(8,128)(2,1)S(1)}, bf16[2,16,1024]{2,1,0:T(8,128)(2,1)S(1)}, u32[]{:S(2)}, u32[]{:S(2)}) %collective-permute-start.10) | collective-permute-done | bytes 65568 | tf_op jit(solution)/shard_map/ppermute | solution.py:28
  25.7 1.9 %collective-permute-start.11 = (bf16[2,16,1024]{2,1,0:T(8,128)(2,1)S(1)}, bf16[2,16,1024]{2,1,0:T(8,128)(2,1)S(1)}, u32[]{:S(2)}, u32[]{:S(2)}) collective-permute-start(bf16[2,16,1024]{2,1,0:T(8,128)(2,1)S(1)} %fusion.2), channel_id=1, source_target_pairs={{0,2},{1,3},{2,0},{3,1},{4,6},{5,7},{6,4},{7,5},{8,10},{9,11},{10,... | collective-permute-start | bytes 196616 | tf_op jit(solution)/shard_map/ppermute | solution.py:28
  27.6 0.0 collective-permute-done.13.refs_4_
  27.6 0.0 collective-permute-start.14
  27.6 0.5 %collective-permute-start.15 = (f32[3,16,2048]{2,1,0:T(8,128)S(1)}, f32[3,16,2048]{2,1,0:T(8,128)S(1)}, u32[]{:S(2)}, u32[]{:S(2)}) collective-permute-start(f32[3,16,2048]{2,1,0:T(8,128)S(1)} %collective-permute-done.13.refs_4_), channel_id=1, source_target_pairs={{0,1},{1,0},{2,3},{3,2},{4,5},{5,4},{6,7},{7,6},{8,9},{9,8},{10,11... | collective-permute-start | bytes 1179656 | tf_op jit(solution)/shard_map/ppermute | solution.py:28
  28.1 0.3 collective-permute-done.6
  28.4 0.1 collective-permute-start.12
  28.5 1.5 %collective-permute-done.11 = bf16[2,16,1024]{2,1,0:T(8,128)(2,1)S(1)} collective-permute-done((bf16[2,16,1024]{2,1,0:T(8,128)(2,1)S(1)}, bf16[2,16,1024]{2,1,0:T(8,128)(2,1)S(1)}, u32[]{:S(2)}, u32[]{:S(2)}) %collective-permute-start.11) | collective-permute-done | bytes 65568 | tf_op jit(solution)/shard_map/ppermute | solution.py:28
  30.0 0.1 collective-permute-start.16
  30.1 0.0 collective-permute-done.12.refs_2_
  30.1 0.0 collective-permute-done.14.refs_5_.refs_1_
  30.1 0.0 collective-permute-done.15.refs_6_.refs_2_
  30.1 1.1 %shard_map.102 = (f32[16,2048]{1,0:T(8,128)}, f32[16,2048]{1,0:T(8,128)}, f32[16,2048]{1,0:T(8,128)}, bf16[16,8192]{1,0:T(8,128)(2,1)}, f32[16,2048]{1,0:T(8,128...) custom-call(f32[2,16,1024]{2,1,0:T(8,128)S(1)} %add_multiply_fusion.1.refs_0_, f32[2,16,1024]{2,1,0:T(8,128)S(1)} %add_multiply_fusion.refs_1_, ...), custom_call_target="tpu_custom_call" | custom-call | flops 5242880 | bytes 1572864 | tf_op jit(solution)/shard_map/pallas_call | solution.py:167
  31.3 0.2 collective-permute-done.16.refs_0_
  31.4 0.8 %shard_map.103 = (bf16[16,8192]{1,0:T(8,128)(2,1)}, f32[16,2048]{1,0:T(8,128)}, f32[16,2048]{1,0:T(8,128)}, f32[16,2048]{1,0:T(8,128)}) custom-call(f32[2,16,1024]{2,1,0:T(8,128)S(1)} %collective-permute-done.16.refs_0_, ...), custom_call_target="tpu_custom_call", output_to_operand_aliasing={{0}: (3, {}), {1}: (4, {}), {2}: (5, {}), {3}: (6, {})} | custom-call | tf_op jit(solution)/shard_map/pallas_call | solution.py:176
  (11 shorter events, 0.2 us)
Async XLA Ops:
  0.6 1.6 %copy-start = (bf16[1,1,128,8192]{3,2,1,0:T(8,128)(2,1)S(1)}, bf16[1,1,128,8192]{3,2,1,0:T(8,128)(2,1)}, u32[]{:S(2)}) copy-start(bf16[1,1,128,8192]{3,2,1,0:T(8,128)(2,1)} %param.4) | copy-start | bytes 6291460
  2.5 4.8 %copy-start.1 = (bf16[1,1,128,8192]{3,2,1,0:T(8,128)(2,1)S(1)}, bf16[1,1,128,8192]{3,2,1,0:T(8,128)(2,1)}, u32[]{:S(2)}) copy-start(bf16[1,1,128,8192]{3,2,1,0:T(8,128)(2,1)} %param.4) | copy-start | bytes 6291460
  2.5 1.7 %collective-permute-start.2 = (bf16[2,2,2,16,1024]{4,3,2,1,0:T(8,128)(2,1)S(1)}, bf16[2,2,2,16,1024]{4,3,2,1,0:T(8,128)(2,1)S(1)}, u32[]{:S(2)}, u32[]{:S(2)}) collective-permute-start(bf16[2,2,2,16,1024]{4,3,2,1,0:T(8,128)(2,1)S(1)} %get-tuple-element.38), channel_id=1, source_target_pairs={{0,1},{1,0},{2,3},{3,2},{4,5},{5,4},{6,7},{7,6},{8,9},{9,8},{10,11... | collective-permute-start | bytes 786440 | tf_op jit(solution)/shard_map/ppermute | solution.py:28
  3.3 6.5 %copy-start.2 = (f32[16,2048]{1,0:T(8,128)S(1)}, f32[16,2048]{1,0:T(8,128)}, u32[]{:S(2)}) copy-start(f32[16,2048]{1,0:T(8,128)} %param.7) | copy-start | bytes 393220
  3.3 6.5 %copy-start.3 = (f32[16,2048]{1,0:T(8,128)S(1)}, f32[16,2048]{1,0:T(8,128)}, u32[]{:S(2)}) copy-start(f32[16,2048]{1,0:T(8,128)} %param.6) | copy-start | bytes 393220
  3.3 6.4 %copy-start.4 = (f32[16,2048]{1,0:T(8,128)S(1)}, f32[16,2048]{1,0:T(8,128)}, u32[]{:S(2)}) copy-start(f32[16,2048]{1,0:T(8,128)} %param.5) | copy-start | bytes 393220
  3.3 3.9 %collective-permute-start = (bf16[2,2,2,16,1024]{4,3,2,1,0:T(8,128)(2,1)S(1)}, bf16[2,2,2,16,1024]{4,3,2,1,0:T(8,128)(2,1)S(1)}, u32[]{:S(2)}, u32[]{:S(2)}) collective-permute-start(bf16[2,2,2,16,1024]{4,3,2,1,0:T(8,128)(2,1)S(1)} %get-tuple-element.33), channel_id=1, source_target_pairs={{0,1},{1,0},{2,3},{3,2},{4,5},{5,4},{6,7},{7,6},{8,9},{9,8},{10,11... | collective-permute-start | bytes 786440 | tf_op jit(solution)/shard_map/ppermute | solution.py:28
  4.3 7.4 %collective-permute-start.3 = (bf16[2,2,2,16,1024]{4,3,2,1,0:T(8,128)(2,1)S(1)}, bf16[2,2,2,16,1024]{4,3,2,1,0:T(8,128)(2,1)S(1)}, u32[]{:S(2)}, u32[]{:S(2)}) collective-permute-start(bf16[2,2,2,16,1024]{4,3,2,1,0:T(8,128)(2,1)S(1)} %add_convert_fusion), channel_id=1, source_target_pairs={{0,8},{1,5},{2,10},{3,7},{4,12},{5,1},{6,14},{7,3},{8,0},{9,13},{1... | collective-permute-start | bytes 786440 | tf_op jit(solution)/shard_map/ppermute | solution.py:28
  7.9 3.7 %collective-permute-start.1 = (bf16[2,2,2,16,1024]{4,3,2,1,0:T(8,128)(2,1)S(1)}, bf16[2,2,2,16,1024]{4,3,2,1,0:T(8,128)(2,1)S(1)}, u32[]{:S(2)}, u32[]{:S(2)}) collective-permute-start(bf16[2,2,2,16,1024]{4,3,2,1,0:T(8,128)(2,1)S(1)} %get-tuple-element.36), channel_id=1, source_target_pairs={{0,1},{1,0},{2,3},{3,2},{4,5},{5,4},{6,7},{7,6},{8,9},{9,8},{10,11... | collective-permute-start | bytes 786440 | tf_op jit(solution)/shard_map/ppermute | solution.py:28
  8.0 6.8 %collective-permute-start.8 = (bf16[2,2,2,16,1024]{4,3,2,1,0:T(8,128)(2,1)S(1)}, bf16[2,2,2,16,1024]{4,3,2,1,0:T(8,128)(2,1)S(1)}, u32[]{:S(2)}, u32[]{:S(2)}) collective-permute-start(bf16[2,2,2,16,1024]{4,3,2,1,0:T(8,128)(2,1)S(1)} %add_convert_fusion.1), channel_id=1, source_target_pairs={{0,8},{1,5},{2,10},{3,7},{4,12},{5,1},{6,14},{7,3},{8,0},{9,13},{1... | collective-permute-start | bytes 786440 | tf_op jit(solution)/shard_map/ppermute | solution.py:28
  9.4 5.5 %collective-permute-start.7 = (bf16[2,2,2,16,1024]{4,3,2,1,0:T(8,128)(2,1)S(1)}, bf16[2,2,2,16,1024]{4,3,2,1,0:T(8,128)(2,1)S(1)}, u32[]{:S(2)}, u32[]{:S(2)}) collective-permute-start(bf16[2,2,2,16,1024]{4,3,2,1,0:T(8,128)(2,1)S(1)} %get-tuple-element.40), channel_id=1, source_target_pairs={{0,1},{1,0},{2,3},{3,2},{4,5},{5,4},{6,7},{7,6},{8,9},{9,8},{10,11... | collective-permute-start | bytes 786440 | tf_op jit(solution)/shard_map/ppermute | solution.py:28
  9.8 17.8 %collective-permute-start.13 = (f32[3,16,2048]{2,1,0:T(8,128)S(1)}, f32[3,16,2048]{2,1,0:T(8,128)S(1)}, u32[]{:S(2)}, u32[]{:S(2)}) collective-permute-start(f32[3,16,2048]{2,1,0:T(8,128)S(1)} %pad_maximum_fusion.refs_3_), channel_id=1, source_target_pairs={{0,2},{1,3},{2,0},{3,1},{4,6},{5,7},{6,4},{7,5},{8,10},{9,11},{10,... | collective-permute-start | bytes 1179656 | tf_op jit(solution)/shard_map/ppermute | solution.py:28
  11.8 5.5 %collective-permute-start.4 = (bf16[2,2,16,1024]{3,2,1,0:T(8,128)(2,1)S(1)}, bf16[2,2,16,1024]{3,2,1,0:T(8,128)(2,1)S(1)}, u32[]{:S(2)}, u32[]{:S(2)}) collective-permute-start(bf16[2,2,16,1024]{3,2,1,0:T(8,128)(2,1)S(1)} %fusion), channel_id=1, source_target_pairs={{0,4},{1,9},{2,6},{3,11},{4,0},{5,13},{6,2},{7,15},{8,12},{9,1},{1... | collective-permute-start | bytes 393224 | tf_op jit(solution)/shard_map/ppermute | solution.py:28
  15.0 5.2 %collective-permute-start.9 = (bf16[2,2,16,1024]{3,2,1,0:T(8,128)(2,1)S(1)}, bf16[2,2,16,1024]{3,2,1,0:T(8,128)(2,1)S(1)}, u32[]{:S(2)}, u32[]{:S(2)}) collective-permute-start(bf16[2,2,16,1024]{3,2,1,0:T(8,128)(2,1)S(1)} %fusion.1), channel_id=1, source_target_pairs={{0,4},{1,9},{2,6},{3,11},{4,0},{5,13},{6,2},{7,15},{8,12},{9,1},{1... | collective-permute-start | bytes 393224 | tf_op jit(solution)/shard_map/ppermute | solution.py:28
  17.3 6.1 %collective-permute-start.5 = (bf16[2,16,1024]{2,1,0:T(8,128)(2,1)S(1)}, bf16[2,16,1024]{2,1,0:T(8,128)(2,1)S(1)}, u32[]{:S(2)}, u32[]{:S(2)}) collective-permute-start(bf16[2,16,1024]{2,1,0:T(8,128)(2,1)S(1)} %fusion.4), channel_id=1, source_target_pairs={{0,16},{1,17},{2,18},{3,19},{4,20},{5,21},{6,22},{7,23},{8,24},{9,... | collective-permute-start | bytes 196616 | tf_op jit(solution)/shard_map/ppermute | solution.py:28
  20.3 5.4 %collective-permute-start.10 = (bf16[2,16,1024]{2,1,0:T(8,128)(2,1)S(1)}, bf16[2,16,1024]{2,1,0:T(8,128)(2,1)S(1)}, u32[]{:S(2)}, u32[]{:S(2)}) collective-permute-start(bf16[2,16,1024]{2,1,0:T(8,128)(2,1)S(1)} %fusion.5), channel_id=1, source_target_pairs={{0,16},{1,17},{2,18},{3,19},{4,20},{5,21},{6,22},{7,23},{8,24},{9,... | collective-permute-start | bytes 196616 | tf_op jit(solution)/shard_map/ppermute | solution.py:28
  23.4 4.9 %collective-permute-start.6 = (bf16[2,16,1024]{2,1,0:T(8,128)(2,1)S(1)}, bf16[2,16,1024]{2,1,0:T(8,128)(2,1)S(1)}, u32[]{:S(2)}, u32[]{:S(2)}) collective-permute-start(bf16[2,16,1024]{2,1,0:T(8,128)(2,1)S(1)} %fusion.3), channel_id=1, source_target_pairs={{0,2},{1,3},{2,0},{3,1},{4,6},{5,7},{6,4},{7,5},{8,10},{9,11},{10,... | collective-permute-start | bytes 196616 | tf_op jit(solution)/shard_map/ppermute | solution.py:28
  25.7 4.3 %collective-permute-start.11 = (bf16[2,16,1024]{2,1,0:T(8,128)(2,1)S(1)}, bf16[2,16,1024]{2,1,0:T(8,128)(2,1)S(1)}, u32[]{:S(2)}, u32[]{:S(2)}) collective-permute-start(bf16[2,16,1024]{2,1,0:T(8,128)(2,1)S(1)} %fusion.2), channel_id=1, source_target_pairs={{0,2},{1,3},{2,0},{3,1},{4,6},{5,7},{6,4},{7,5},{8,10},{9,11},{10,... | collective-permute-start | bytes 196616 | tf_op jit(solution)/shard_map/ppermute | solution.py:28
  27.6 2.6 %collective-permute-start.14 = (f32[3,16,2048]{2,1,0:T(8,128)S(1)}, f32[3,16,2048]{2,1,0:T(8,128)S(1)}, u32[]{:S(2)}, u32[]{:S(2)}) collective-permute-start(f32[3,16,2048]{2,1,0:T(8,128)S(1)} %pad_maximum_fusion.refs_3_), channel_id=1, source_target_pairs={{0,1},{1,0},{2,3},{3,2},{4,5},{5,4},{6,7},{7,6},{8,9},{9,8},{10,11... | collective-permute-start | bytes 1179656 | tf_op jit(solution)/shard_map/ppermute | solution.py:28
  27.6 2.6 %collective-permute-start.15 = (f32[3,16,2048]{2,1,0:T(8,128)S(1)}, f32[3,16,2048]{2,1,0:T(8,128)S(1)}, u32[]{:S(2)}, u32[]{:S(2)}) collective-permute-start(f32[3,16,2048]{2,1,0:T(8,128)S(1)} %collective-permute-done.13.refs_4_), channel_id=1, source_target_pairs={{0,1},{1,0},{2,3},{3,2},{4,5},{5,4},{6,7},{7,6},{8,9},{9,8},{10,11... | collective-permute-start | bytes 1179656 | tf_op jit(solution)/shard_map/ppermute | solution.py:28
  28.4 1.7 %collective-permute-start.12 = (f32[2,16,1024]{2,1,0:T(8,128)S(1)}, f32[2,16,1024]{2,1,0:T(8,128)S(1)}, u32[]{:S(2)}, u32[]{:S(2)}) collective-permute-start(f32[2,16,1024]{2,1,0:T(8,128)S(1)} %add_multiply_fusion.1.refs_0_), channel_id=1, source_target_pairs={{0,1},{1,0},{2,3},{3,2},{4,5},{5,4},{6,7},{7,6},{8,9},{9,8},{10,11... | collective-permute-start | bytes 393224 | tf_op jit(solution)/shard_map/ppermute | solution.py:28
  30.0 1.4 %collective-permute-start.16 = (f32[2,16,1024]{2,1,0:T(8,128)S(1)}, f32[2,16,1024]{2,1,0:T(8,128)S(1)}, u32[]{:S(2)}, u32[]{:S(2)}) collective-permute-start(f32[2,16,1024]{2,1,0:T(8,128)S(1)} %add_multiply_fusion.refs_1_), channel_id=1, source_target_pairs={{0,1},{1,0},{2,3},{3,2},{4,5},{5,4},{6,7},{7,6},{8,9},{9,8},{10,11... | collective-permute-start | bytes 393224 | tf_op jit(solution)/shard_map/ppermute | solution.py:28

commit v8 on v7

--- a/solution.py
+++ b/solution.py
@@ -103,22 +103,18 @@
     ]
 
 
-def finish(own, other, states, near, cols):
-    parts, rows = len(own), own[0].shape[1]
+def finish(own, other, states, near, cols, outs):
+    rows = [*own.values(), *other.values()][0].shape[1]
     ng = 2 * len(states)
     edges = cut_up(cols)
 
-    def kernel(first, *refs):
+    def kernel(mine, theirs, first, *refs):
         refs = list(refs)
         take = lambda n: [refs.pop(0) for _ in range(n)]
-        own = take(parts) if first else []
-        other = dict(zip(range(parts - 1) if first else [parts - 1], take(parts - 1 if first else 1)))
-        states, near = take(ng // 2) if first else [], take(ng // 2)
-        if first:
-            outs = take(3)
-        else:
-            take(4)
-        weights, copies = take(1)[0], take(3)
+        own, other = take(len(mine)), take(len(theirs))
+        states, near = take(ng // 2 if mine else 0), take(ng // 2 if theirs else 0)
+        take(0 if first else 7)
+        outs, weights, copies = take(3), take(1)[0], take(3)
         wide, thin, sem = take(3)
         me = lax.axis_index("grp")
         last = lax.rem(me + ng - 1, ng)
@@ -128,61 +124,55 @@
             moves.append(pltpu.make_async_copy(source, target, sem.at[len(moves)]))
             moves[-1].start()
 
-        def block(n, part, state, x, edge, keep):
-            start, width = edge
-            new = updated(part[x], *[state[i, :, start : start + width] for i in range(3)])
+        def fresh(part, x, state, start, width):
+            return updated(part[x].astype(F32), *[state[i, :, start : start + width] for i in range(3)])
+
+        def weigh(n, new, start, width):
             thin[n, :, start : start + width] = new[0].astype(BF16)
-            if keep:
-                for i in range(3):
-                    wide[i, :, start : start + width] = new[i]
-
-        for k in range(len(states)):
-            for part, edge in zip(own, edges):
-                block(2 * k, part, states[k], (me >> 1) ^ k, edge, k == 0)
-            if k == 0:
-                for i in range(3):
-                    move(wide.at[i], outs[i])
-            move(thin.at[2 * k], weights.at[:, pl.ds(pl.multiple_of((me ^ (2 * k)) * cols, 128), cols)])
-        for index, part in other.items():
+            column = pl.multiple_of((me ^ n) * cols + start, 128)
+            move(thin.at[n, :, pl.ds(start, width)], weights.at[:, pl.ds(column, width)])
+
+        for index, part in zip(mine, own):
             start, width = edges[index]
-            here = pl.ds(start, width)
+            for k in range(ng // 2):
+                new = fresh(part, (me >> 1) ^ k, states[k], start, width)
+                if k == 0:
+                    for i in range(3):
+                        wide[i, :, start : start + width] = new[i]
+                        move(wide.at[i, :, pl.ds(start, width)], outs[i].at[:, pl.ds(start, width)])
+                weigh(2 * k, new, start, width)
+        for index, part in zip(theirs, other):
+            start, width = edges[index]
             for k in range(ng // 2):
                 @pl.when((me ^ last) >> 1 == k)
                 def _():
-                    new = updated(part[last >> 1], *[near[k][i, :, start : start + width] for i in range(3)])
+                    new = fresh(part, last >> 1, near[k], start, width)
                     for i in range(3):
                         wide[3 + i, :, start : start + width] = new[i]
             for i in range(3):
-                move(wide.at[3 + i, :, here], copies[i].at[:, here])
+                move(wide.at[3 + i, :, pl.ds(start, width)], copies[i].at[:, pl.ds(start, width)])
             for k in range(ng // 2):
-                block(2 * k + 1, part, near[k], (me >> 1) ^ k, edges[index], False)
-                column = pl.multiple_of((me ^ (2 * k + 1)) * cols + start, 128)
-                move(thin.at[2 * k + 1, :, here], weights.at[:, pl.ds(column, width)])
+                weigh(2 * k + 1, fresh(part, (me >> 1) ^ k, near[k], start, width), start, width)
         for m in moves:
             m.wait()
 
     shape = jax.ShapeDtypeStruct((rows, cols), F32)
-    shapes = [jax.ShapeDtypeStruct((rows, cols * ng), BF16)] + [shape] * 3
-    scratch = [pltpu.VMEM((6, rows, cols), F32), pltpu.VMEM((ng, rows, cols), BF16)]
-    early = pl.pallas_call(
-        functools.partial(kernel, True),
-        out_shape=[shape] * 3 + shapes,
-        in_specs=[VMEM] * (2 * parts - 1 + ng),
+    shapes = [shape] * 3 + [jax.ShapeDtypeStruct((rows, cols * ng), BF16)] + [shape] * 3
+    given = list(own.values()) + list(other.values()) + (states if own else []) + (near if other else [])
+    return pl.pallas_call(
+        functools.partial(kernel, list(own), list(other), not outs),
+        out_shape=shapes,
+        in_specs=[VMEM] * len(given) + [ANY] * len(outs),
         out_specs=[ANY] * 7,
-        scratch_shapes=scratch + [pltpu.SemaphoreType.DMA((3 + ng // 2 + (3 + ng // 2) * (parts - 1),))],
+        scratch_shapes=[
+            pltpu.VMEM((6, rows, cols), F32),
+            pltpu.VMEM((ng, rows, cols), BF16),
+            pltpu.SemaphoreType.DMA(((3 + ng // 2) * (len(own) + len(other)),)),
+        ],
+        input_output_aliases={len(given) + i: i for i in range(len(outs))},
         cost_estimate=pl.CostEstimate(flops=40 * rows * cols * ng, bytes_accessed=12 * rows * cols * ng, transcendentals=0),
         compiler_params=pltpu.CompilerParams(vmem_limit_bytes=LIMIT),
-    )(*own, *other[:-1], *states, *near)
-    late = pl.pallas_call(
-        functools.partial(kernel, False),
-        out_shape=shapes,
-        in_specs=[VMEM] * (1 + ng // 2) + [ANY] * 4,
-        out_specs=[ANY] * 4,
-        scratch_shapes=scratch + [pltpu.SemaphoreType.DMA((3 + ng // 2,))],
-        input_output_aliases={1 + ng // 2 + i: i for i in range(4)},
-        compiler_params=pltpu.CompilerParams(vmem_limit_bytes=LIMIT),
-    )(other[-1], *near, *early[3:])
-    return (*early[:3], *late)
+    )(*given, *outs)
 
 
 def finish_plain(own, other, states, near, cols):
@@ -234,6 +224,8 @@
         (out,), (mine,) = gather(g, [(1, 1), (0, 1)], [edge], rows, nf, ng)
         away_out.append(out)
         away_own.append(mine)
+    scaled = lambda t: t / (ng * nf)
+    outs = []
     split = lambda t: t.reshape((2,) * (f_bits - 1) + t.shape[2:])
     got_away = [split(swap(t, [1, 1])) for t in away_out]
     sent = [(split(t).astype(F32) + x.astype(F32)).astype(BF16) for t, x in zip(away_own, got_away)]
@@ -266,10 +258,21 @@
             states = lax.optimization_barrier((states, rounded[-1]))[0]
             near = [swap(s, [1, 1]) for s in states]
         got = [swap(t, [1 << b] * 2) for t in rounded]
+        if local and b == g_bits - 1 and len(cut) > 1:
+            head = rounded[0].astype(F32) + got[0].astype(F32)
+            outs = finish({0: scaled(head)}, {}, states, None, cols, [])
+            rounded[-1] = lax.optimization_barrier((rounded[-1], outs[0]))[0]
         ts = [t.astype(F32) + x.astype(F32) for t, x in zip(rounded, got)]
-    own = [t / (ng * nf) for t in ts]
+    own = [scaled(t) for t in ts]
     other = [swap(t, [1, 1]) for t in own]
-    return (finish if local else finish_plain)(own, other, states, near, cols)
+    if not local:
+        return finish_plain(own, other, states, near, cols)
+    own, other = dict(enumerate(own)), dict(enumerate(other))
+    tail = {max(other): other.pop(max(other))}
+    if len(cut) > 1:
+        own.pop(0)
+    outs = finish(own, other, states, near, cols, outs)
+    return tuple(finish({}, tail, states, near, cols, outs))
 
 
 def solution(mesh):

time: 32.4 us -> 32.3 us (level)
  waiting for transfers between devices: 5.03 us -> 4.05 us
  Pallas kernels: 3.04 us -> 3.75 us
    ppermute x17, waiting for transfers between devices: 5.03 us -> 4.05 us  [swap(): return lax.ppermute(x, BOTH, [(i, i ^ masks[i & 1]) for i in range(n)])]
    pallas_call x2 -> x3, Pallas kernels: 1.95 us -> 2.66 us  [finish(): pl.pallas_call(functools.partial(kernel, list(own), list(other), not outs...]
  transfers between devices with their start and end apart: 17 -> 17, of which waited for: 8 -> 8; matrix products, arithmetic and copies ran while one was open for 2% -> 2% of each run, Pallas kernels for 6% -> 8%
where the time goes in v8:
time: 32.3 us; the launch traced here: 32.1 us
  starting transfers between devices  21.3 us (66%)
  waiting for transfers between devices  4.05 us (13%)
  Pallas kernels  3.75 us (12%)
  local copies, waits for them, and re-layouts  1.69 us (5%)
  between operations  0.87 us (3%)
  other arithmetic  0.49 us (2%)
    ppermute x17, starting transfers between devices, swap(): return lax.ppermute(x, BOTH, [(i, i ^ masks[i & 1]) for i in range(n)])  21.3 us
    ppermute x17, waiting for transfers between devices, swap(): return lax.ppermute(x, BOTH, [(i, i ^ masks[i & 1]) for i in range(n)])  4.05 us
    pallas_call x3, Pallas kernels, finish(): pl.pallas_call(functools.partial(kernel, list(own), list(other), not outs...  2.66 us
    unnamed x10, local copies, waits for them, and re-layouts  1.61 us
    pallas_call x3, Pallas kernels, gathered(): pl.pallas_call(kernel, out_shape=[jax.ShapeDtypeStruct((2, nf // 4, ng //...  1.09 us
  transfers between devices with their start and end apart: 17, of which 8 were waited for; matrix products, arithmetic and copies ran while one was open for 2% of the time, Pallas kernels for 8%

profile of v8, /device:TPU:0, one launch (start us, length us, event | category | flops | bytes accessed | tf_op | source)
XLA Modules:
  0.0 32.1 jit_solution(15579921143225711053)
XLA Ops:
  0.6 0.0 copy-start
  0.6 1.6 %copy-done = bf16[1,1,128,8192]{3,2,1,0:T(8,128)(2,1)S(1)} copy-done((bf16[1,1,128,8192]{3,2,1,0:T(8,128)(2,1)S(1)}, bf16[1,1,128,8192]{3,2,1,0:T(8,128)(2,1)}, u32[]{:S(2)}) %copy-start) | copy-done | bytes 2097176
  2.2 0.3 shard_map.101
  2.5 0.0 copy-start.1
  2.5 0.5 %collective-permute-start.6 = (bf16[2,2,2,16,1024]{4,3,2,1,0:T(8,128)(2,1)S(1)}, bf16[2,2,2,16,1024]{4,3,2,1,0:T(8,128)(2,1)S(1)}, u32[]{:S(2)}, u32[]{:S(2)}) collective-permute-start(bf16[2,2,2,16,1024]{4,3,2,1,0:T(8,128)(2,1)S(1)} %get-tuple-element.44), channel_id=1, source_target_pairs={{0,1},{1,0},{2,3},{3,2},{4,5},{5,4},{6,7},{7,6},{8,9},{9,8},{10,11... | collective-permute-start | bytes 786440 | tf_op jit(solution)/shard_map/ppermute | solution.py:28
  3.0 0.3 shard_map.99
  3.3 0.0 copy-start.2
  3.3 0.0 copy-start.3
  3.3 0.0 copy-start.4
  3.3 0.1 collective-permute-start
  3.4 0.7 %collective-permute-done.6 = bf16[2,2,2,16,1024]{4,3,2,1,0:T(8,128)(2,1)S(1)} collective-permute-done((bf16[2,2,2,16,1024]{4,3,2,1,0:T(8,128)(2,1)S(1)}, bf16[2,2,2,16,1024]{4,3,2,1,0:T(8,128)(2,1)S(1)}, u32[]{:S(2)}, u32[]{:S(2)}) %collective-permute-start.6) | collective-permute-done | bytes 262176 | tf_op jit(solution)/shard_map/ppermute | solution.py:28
  4.2 0.1 add_convert_fusion
  4.3 3.0 %collective-permute-start.7 = (bf16[2,2,2,16,1024]{4,3,2,1,0:T(8,128)(2,1)S(1)}, bf16[2,2,2,16,1024]{4,3,2,1,0:T(8,128)(2,1)S(1)}, u32[]{:S(2)}, u32[]{:S(2)}) collective-permute-start(bf16[2,2,2,16,1024]{4,3,2,1,0:T(8,128)(2,1)S(1)} %add_convert_fusion), channel_id=1, source_target_pairs={{0,8},{1,5},{2,10},{3,7},{4,12},{5,1},{6,14},{7,3},{8,0},{9,13},{1... | collective-permute-start | bytes 786440 | tf_op jit(solution)/shard_map/ppermute | solution.py:28
  7.3 0.0 collective-permute-done
  7.3 0.1 add_convert_fusion.1
  7.3 0.0 copy-done.1
  7.3 0.6 %shard_map.100 = (bf16[2,2,2,16,1024]{4,3,2,1,0:T(8,128)(2,1)S(1)}, bf16[2,2,2,16,1024]{4,3,2,1,0:T(8,128)(2,1)S(1)}, bf16[2,2,2,16,1024]{4,3,2,1,0:T(8,128)(2,1)S(1)}, bf16[2,2,2,16,1024]{4,3,2,1,0:T(8,128)(2,1)S(1)}) custom-call(bf16[2,2,2,16,8192]{4,3,2,1,0:T(8,128)(2,1)S(1)} %bitcast.28), custom_call_target="tpu_custom_call" | custom-call | bytes 2097152 | tf_op jit(solution)/shard_map/pallas_call | solution.py:78
  7.9 0.1 collective-permute-start.5
  8.0 1.3 %collective-permute-start.2 = (bf16[2,2,2,16,1024]{4,3,2,1,0:T(8,128)(2,1)S(1)}, bf16[2,2,2,16,1024]{4,3,2,1,0:T(8,128)(2,1)S(1)}, u32[]{:S(2)}, u32[]{:S(2)}) collective-permute-start(bf16[2,2,2,16,1024]{4,3,2,1,0:T(8,128)(2,1)S(1)} %add_convert_fusion.1), channel_id=1, source_target_pairs={{0,8},{1,5},{2,10},{3,7},{4,12},{5,1},{6,14},{7,3},{8,0},{9,13},{1... | collective-permute-start | bytes 786440 | tf_op jit(solution)/shard_map/ppermute | solution.py:28
  9.4 0.0 copy-done.2
  9.4 0.0 copy-done.3
  9.4 0.0 copy-done.4
  9.4 1.6 %collective-permute-start.11 = (f32[3,16,2048]{2,1,0:T(8,128)S(1)}, f32[3,16,2048]{2,1,0:T(8,128)S(1)}, u32[]{:S(2)}, u32[]{:S(2)}) collective-permute-start(f32[3,16,2048]{2,1,0:T(8,128)S(1)} %pad_maximum_fusion.refs_1_.refs_2_), channel_id=1, source_target_pairs={{0,2},{1,3},{2,0},{3,1},{4,6},{5,7},{6,4},{7,5},{8,10},{9,11},{10,... | collective-permute-start | bytes 1179656 | tf_op jit(solution)/shard_map/ppermute | solution.py:28
  11.0 0.1 collective-permute-start.1
  11.1 0.6 %collective-permute-done.7 = bf16[2,2,2,16,1024]{4,3,2,1,0:T(8,128)(2,1)S(1)} collective-permute-done((bf16[2,2,2,16,1024]{4,3,2,1,0:T(8,128)(2,1)S(1)}, bf16[2,2,2,16,1024]{4,3,2,1,0:T(8,128)(2,1)S(1)}, u32[]{:S(2)}, u32[]{:S(2)}) %collective-permute-start.7) | collective-permute-done | bytes 262176 | tf_op jit(solution)/shard_map/ppermute | solution.py:28
  11.6 0.0 collective-permute-done.5
  11.6 0.1 convert_add_fusion
  11.8 2.0 %collective-permute-start.8 = (bf16[2,2,16,1024]{3,2,1,0:T(8,128)(2,1)S(1)}, bf16[2,2,16,1024]{3,2,1,0:T(8,128)(2,1)S(1)}, u32[]{:S(2)}, u32[]{:S(2)}) collective-permute-start(bf16[2,2,16,1024]{3,2,1,0:T(8,128)(2,1)S(1)} %fusion.1), channel_id=1, source_target_pairs={{0,4},{1,9},{2,6},{3,11},{4,0},{5,13},{6,2},{7,15},{8,12},{9,1},{1... | collective-permute-start | bytes 393224 | tf_op jit(solution)/shard_map/ppermute | solution.py:28
  13.8 0.8 %collective-permute-done.2 = bf16[2,2,2,16,1024]{4,3,2,1,0:T(8,128)(2,1)S(1)} collective-permute-done((bf16[2,2,2,16,1024]{4,3,2,1,0:T(8,128)(2,1)S(1)}, bf16[2,2,2,16,1024]{4,3,2,1,0:T(8,128)(2,1)S(1)}, u32[]{:S(2)}, u32[]{:S(2)}) %collective-permute-start.2) | collective-permute-done | bytes 262176 | tf_op jit(solution)/shard_map/ppermute | solution.py:28
  14.6 0.0 collective-permute-done.1
  14.6 0.1 convert_add_fusion.1
  14.8 2.5 %collective-permute-start.3 = (bf16[2,2,16,1024]{3,2,1,0:T(8,128)(2,1)S(1)}, bf16[2,2,16,1024]{3,2,1,0:T(8,128)(2,1)S(1)}, u32[]{:S(2)}, u32[]{:S(2)}) collective-permute-start(bf16[2,2,16,1024]{3,2,1,0:T(8,128)(2,1)S(1)} %fusion), channel_id=1, source_target_pairs={{0,4},{1,9},{2,6},{3,11},{4,0},{5,13},{6,2},{7,15},{8,12},{9,1},{1... | collective-permute-start | bytes 393224 | tf_op jit(solution)/shard_map/ppermute | solution.py:28
  17.3 0.0 collective-permute-done.8
  17.3 2.7 %collective-permute-start.9 = (bf16[2,16,1024]{2,1,0:T(8,128)(2,1)S(1)}, bf16[2,16,1024]{2,1,0:T(8,128)(2,1)S(1)}, u32[]{:S(2)}, u32[]{:S(2)}) collective-permute-start(bf16[2,16,1024]{2,1,0:T(8,128)(2,1)S(1)} %fusion.5), channel_id=1, source_target_pairs={{0,16},{1,17},{2,18},{3,19},{4,20},{5,21},{6,22},{7,23},{8,24},{9,... | collective-permute-start | bytes 196616 | tf_op jit(solution)/shard_map/ppermute | solution.py:28
  20.0 0.2 collective-permute-done.3
  20.3 3.0 %collective-permute-start.4 = (bf16[2,16,1024]{2,1,0:T(8,128)(2,1)S(1)}, bf16[2,16,1024]{2,1,0:T(8,128)(2,1)S(1)}, u32[]{:S(2)}, u32[]{:S(2)}) collective-permute-start(bf16[2,16,1024]{2,1,0:T(8,128)(2,1)S(1)} %fusion.4), channel_id=1, source_target_pairs={{0,16},{1,17},{2,18},{3,19},{4,20},{5,21},{6,22},{7,23},{8,24},{9,... | collective-permute-start | bytes 196616 | tf_op jit(solution)/shard_map/ppermute | solution.py:28
  23.3 0.0 collective-permute-done.9
  23.3 1.7 %collective-permute-start.10 = (bf16[2,16,1024]{2,1,0:T(8,128)(2,1)S(1)}, bf16[2,16,1024]{2,1,0:T(8,128)(2,1)S(1)}, u32[]{:S(2)}, u32[]{:S(2)}) collective-permute-start(bf16[2,16,1024]{2,1,0:T(8,128)(2,1)S(1)} %fusion.2), channel_id=1, source_target_pairs={{0,2},{1,3},{2,0},{3,1},{4,6},{5,7},{6,4},{7,5},{8,10},{9,11},{10,... | collective-permute-start | bytes 196616 | tf_op jit(solution)/shard_map/ppermute | solution.py:28
  25.0 0.5 %collective-permute-done.4 = bf16[2,16,1024]{2,1,0:T(8,128)(2,1)S(1)} collective-permute-done((bf16[2,16,1024]{2,1,0:T(8,128)(2,1)S(1)}, bf16[2,16,1024]{2,1,0:T(8,128)(2,1)S(1)}, u32[]{:S(2)}, u32[]{:S(2)}) %collective-permute-start.4) | collective-permute-done | bytes 65568 | tf_op jit(solution)/shard_map/ppermute | solution.py:28
  25.5 2.0 %collective-permute-start.12 = (bf16[2,16,1024]{2,1,0:T(8,128)(2,1)S(1)}, bf16[2,16,1024]{2,1,0:T(8,128)(2,1)S(1)}, u32[]{:S(2)}, u32[]{:S(2)}) collective-permute-start(bf16[2,16,1024]{2,1,0:T(8,128)(2,1)S(1)} %fusion.3), channel_id=1, source_target_pairs={{0,2},{1,3},{2,0},{3,1},{4,6},{5,7},{6,4},{7,5},{8,10},{9,11},{10,... | collective-permute-start | bytes 196616 | tf_op jit(solution)/shard_map/ppermute | solution.py:28
  27.6 0.0 collective-permute-done.11.refs_2_.refs_3_
  27.6 0.0 collective-permute-start.14
  27.6 0.5 %collective-permute-start.15 = (f32[3,16,2048]{2,1,0:T(8,128)S(1)}, f32[3,16,2048]{2,1,0:T(8,128)S(1)}, u32[]{:S(2)}, u32[]{:S(2)}) collective-permute-start(f32[3,16,2048]{2,1,0:T(8,128)S(1)} %collective-permute-done.11.refs_2_.refs_3_), channel_id=1, source_target_pairs={{0,1},{1,0},{2,3},{3,2},{4,5},{5,4},{6,7},{7,6},{8,9},{9,8},{10,11... | collective-permute-start | bytes 1179656 | tf_op jit(solution)/shard_map/ppermute | solution.py:28
  28.1 0.0 collective-permute-done.10
  28.1 0.1 collective-permute-start.16
  28.2 0.8 %shard_map.102 = (f32[16,2048]{1,0:T(8,128)}, f32[16,2048]{1,0:T(8,128)}, f32[16,2048]{1,0:T(8,128)}, bf16[16,8192]{1,0:T(8,128)(2,1)}, f32[16,2048]{1,0:T(8,128...) custom-call(f32[2,16,1024]{2,1,0:T(8,128)S(1)} %add_multiply_fusion.1.refs_0_, ...), custom_call_target="tpu_custom_call" | custom-call | flops 5242880 | bytes 1572864 | tf_op jit(solution)/shard_map/pallas_call | solution.py:162
  29.0 0.9 %collective-permute-done.12 = bf16[2,16,1024]{2,1,0:T(8,128)(2,1)S(1)} collective-permute-done((bf16[2,16,1024]{2,1,0:T(8,128)(2,1)S(1)}, bf16[2,16,1024]{2,1,0:T(8,128)(2,1)S(1)}, u32[]{:S(2)}, u32[]{:S(2)}) %collective-permute-start.12) | collective-permute-done | bytes 65568 | tf_op jit(solution)/shard_map/ppermute | solution.py:28
  29.9 0.1 collective-permute-start.13
  30.0 0.1 collective-permute-done.16.refs_1_
  30.0 0.0 collective-permute-done.14.refs_4_.refs_1_
  30.0 0.0 collective-permute-done.15.refs_5_.refs_2_
  30.0 1.0 %shard_map.103 = (f32[16,2048]{1,0:T(8,128)}, f32[16,2048]{1,0:T(8,128)}, f32[16,2048]{1,0:T(8,128)}, bf16[16,8192]{1,0:T(8,128)(2,1)}, f32[16,2048]{1,0:T(8,128...) custom-call(f32[2,16,1024]{2,1,0:T(8,128)S(1)} %add_multiply_fusion., ...), custom_call_target="tpu_custom_call", output_to_operand_aliasing={{0}: (6, {}), {1}: (7, {}), {2}: (8, {}), {3}: (9, {}), {4}... | custom-call | flops 5242880 | bytes 1572864 | tf_op jit(solution)/shard_map/pallas_call | solution.py:162
  31.1 0.2 collective-permute-done.13.refs_0_
  31.3 0.8 %shard_map.104 = (f32[16,2048]{1,0:T(8,128)}, f32[16,2048]{1,0:T(8,128)}, f32[16,2048]{1,0:T(8,128)}, bf16[16,8192]{1,0:T(8,128)(2,1)}, f32[16,2048]{1,0:T(8,128...) custom-call(f32[2,16,1024]{2,1,0:T(8,128)S(1)} %collective-permute-d, ...), custom_call_target="tpu_custom_call", output_to_operand_aliasing={{0}: (3, {}), {1}: (4, {}), {2}: (5, {}), {3}: (6, {}), {4}... | custom-call | flops 5242880 | bytes 1572864 | tf_op jit(solution)/shard_map/pallas_call | solution.py:162
  (11 shorter events, 0.2 us)
Async XLA Ops:
  0.6 1.6 %copy-start = (bf16[1,1,128,8192]{3,2,1,0:T(8,128)(2,1)S(1)}, bf16[1,1,128,8192]{3,2,1,0:T(8,128)(2,1)}, u32[]{:S(2)}) copy-start(bf16[1,1,128,8192]{3,2,1,0:T(8,128)(2,1)} %param.4) | copy-start | bytes 6291460
  2.5 4.8 %copy-start.1 = (bf16[1,1,128,8192]{3,2,1,0:T(8,128)(2,1)S(1)}, bf16[1,1,128,8192]{3,2,1,0:T(8,128)(2,1)}, u32[]{:S(2)}) copy-start(bf16[1,1,128,8192]{3,2,1,0:T(8,128)(2,1)} %param.4) | copy-start | bytes 6291460
  2.5 1.7 %collective-permute-start.6 = (bf16[2,2,2,16,1024]{4,3,2,1,0:T(8,128)(2,1)S(1)}, bf16[2,2,2,16,1024]{4,3,2,1,0:T(8,128)(2,1)S(1)}, u32[]{:S(2)}, u32[]{:S(2)}) collective-permute-start(bf16[2,2,2,16,1024]{4,3,2,1,0:T(8,128)(2,1)S(1)} %get-tuple-element.44), channel_id=1, source_target_pairs={{0,1},{1,0},{2,3},{3,2},{4,5},{5,4},{6,7},{7,6},{8,9},{9,8},{10,11... | collective-permute-start | bytes 786440 | tf_op jit(solution)/shard_map/ppermute | solution.py:28
  3.3 6.1 %copy-start.2 = (f32[16,2048]{1,0:T(8,128)S(1)}, f32[16,2048]{1,0:T(8,128)}, u32[]{:S(2)}) copy-start(f32[16,2048]{1,0:T(8,128)} %param.7) | copy-start | bytes 393220
  3.3 6.1 %copy-start.3 = (f32[16,2048]{1,0:T(8,128)S(1)}, f32[16,2048]{1,0:T(8,128)}, u32[]{:S(2)}) copy-start(f32[16,2048]{1,0:T(8,128)} %param.6) | copy-start | bytes 393220
  3.3 6.1 %copy-start.4 = (f32[16,2048]{1,0:T(8,128)S(1)}, f32[16,2048]{1,0:T(8,128)}, u32[]{:S(2)}) copy-start(f32[16,2048]{1,0:T(8,128)} %param.5) | copy-start | bytes 393220
  3.3 3.9 %collective-permute-start = (bf16[2,2,2,16,1024]{4,3,2,1,0:T(8,128)(2,1)S(1)}, bf16[2,2,2,16,1024]{4,3,2,1,0:T(8,128)(2,1)S(1)}, u32[]{:S(2)}, u32[]{:S(2)}) collective-permute-start(bf16[2,2,2,16,1024]{4,3,2,1,0:T(8,128)(2,1)S(1)} %get-tuple-element.37), channel_id=1, source_target_pairs={{0,1},{1,0},{2,3},{3,2},{4,5},{5,4},{6,7},{7,6},{8,9},{9,8},{10,11... | collective-permute-start | bytes 786440 | tf_op jit(solution)/shard_map/ppermute | solution.py:28
  4.3 7.4 %collective-permute-start.7 = (bf16[2,2,2,16,1024]{4,3,2,1,0:T(8,128)(2,1)S(1)}, bf16[2,2,2,16,1024]{4,3,2,1,0:T(8,128)(2,1)S(1)}, u32[]{:S(2)}, u32[]{:S(2)}) collective-permute-start(bf16[2,2,2,16,1024]{4,3,2,1,0:T(8,128)(2,1)S(1)} %add_convert_fusion), channel_id=1, source_target_pairs={{0,8},{1,5},{2,10},{3,7},{4,12},{5,1},{6,14},{7,3},{8,0},{9,13},{1... | collective-permute-start | bytes 786440 | tf_op jit(solution)/shard_map/ppermute | solution.py:28
  7.9 3.7 %collective-permute-start.5 = (bf16[2,2,2,16,1024]{4,3,2,1,0:T(8,128)(2,1)S(1)}, bf16[2,2,2,16,1024]{4,3,2,1,0:T(8,128)(2,1)S(1)}, u32[]{:S(2)}, u32[]{:S(2)}) collective-permute-start(bf16[2,2,2,16,1024]{4,3,2,1,0:T(8,128)(2,1)S(1)} %get-tuple-element.42), channel_id=1, source_target_pairs={{0,1},{1,0},{2,3},{3,2},{4,5},{5,4},{6,7},{7,6},{8,9},{9,8},{10,11... | collective-permute-start | bytes 786440 | tf_op jit(solution)/shard_map/ppermute | solution.py:28
  8.0 6.6 %collective-permute-start.2 = (bf16[2,2,2,16,1024]{4,3,2,1,0:T(8,128)(2,1)S(1)}, bf16[2,2,2,16,1024]{4,3,2,1,0:T(8,128)(2,1)S(1)}, u32[]{:S(2)}, u32[]{:S(2)}) collective-permute-start(bf16[2,2,2,16,1024]{4,3,2,1,0:T(8,128)(2,1)S(1)} %add_convert_fusion.1), channel_id=1, source_target_pairs={{0,8},{1,5},{2,10},{3,7},{4,12},{5,1},{6,14},{7,3},{8,0},{9,13},{1... | collective-permute-start | bytes 786440 | tf_op jit(solution)/shard_map/ppermute | solution.py:28
  9.4 18.2 %collective-permute-start.11 = (f32[3,16,2048]{2,1,0:T(8,128)S(1)}, f32[3,16,2048]{2,1,0:T(8,128)S(1)}, u32[]{:S(2)}, u32[]{:S(2)}) collective-permute-start(f32[3,16,2048]{2,1,0:T(8,128)S(1)} %pad_maximum_fusion.refs_1_.refs_2_), channel_id=1, source_target_pairs={{0,2},{1,3},{2,0},{3,1},{4,6},{5,7},{6,4},{7,5},{8,10},{9,11},{10,... | collective-permute-start | bytes 1179656 | tf_op jit(solution)/shard_map/ppermute | solution.py:28
  11.0 3.6 %collective-permute-start.1 = (bf16[2,2,2,16,1024]{4,3,2,1,0:T(8,128)(2,1)S(1)}, bf16[2,2,2,16,1024]{4,3,2,1,0:T(8,128)(2,1)S(1)}, u32[]{:S(2)}, u32[]{:S(2)}) collective-permute-start(bf16[2,2,2,16,1024]{4,3,2,1,0:T(8,128)(2,1)S(1)} %get-tuple-element.40), channel_id=1, source_target_pairs={{0,1},{1,0},{2,3},{3,2},{4,5},{5,4},{6,7},{7,6},{8,9},{9,8},{10,11... | collective-permute-start | bytes 786440 | tf_op jit(solution)/shard_map/ppermute | solution.py:28
  11.8 5.5 %collective-permute-start.8 = (bf16[2,2,16,1024]{3,2,1,0:T(8,128)(2,1)S(1)}, bf16[2,2,16,1024]{3,2,1,0:T(8,128)(2,1)S(1)}, u32[]{:S(2)}, u32[]{:S(2)}) collective-permute-start(bf16[2,2,16,1024]{3,2,1,0:T(8,128)(2,1)S(1)} %fusion.1), channel_id=1, source_target_pairs={{0,4},{1,9},{2,6},{3,11},{4,0},{5,13},{6,2},{7,15},{8,12},{9,1},{1... | collective-permute-start | bytes 393224 | tf_op jit(solution)/shard_map/ppermute | solution.py:28
  14.8 5.4 %collective-permute-start.3 = (bf16[2,2,16,1024]{3,2,1,0:T(8,128)(2,1)S(1)}, bf16[2,2,16,1024]{3,2,1,0:T(8,128)(2,1)S(1)}, u32[]{:S(2)}, u32[]{:S(2)}) collective-permute-start(bf16[2,2,16,1024]{3,2,1,0:T(8,128)(2,1)S(1)} %fusion), channel_id=1, source_target_pairs={{0,4},{1,9},{2,6},{3,11},{4,0},{5,13},{6,2},{7,15},{8,12},{9,1},{1... | collective-permute-start | bytes 393224 | tf_op jit(solution)/shard_map/ppermute | solution.py:28
  17.3 5.9 %collective-permute-start.9 = (bf16[2,16,1024]{2,1,0:T(8,128)(2,1)S(1)}, bf16[2,16,1024]{2,1,0:T(8,128)(2,1)S(1)}, u32[]{:S(2)}, u32[]{:S(2)}) collective-permute-start(bf16[2,16,1024]{2,1,0:T(8,128)(2,1)S(1)} %fusion.5), channel_id=1, source_target_pairs={{0,16},{1,17},{2,18},{3,19},{4,20},{5,21},{6,22},{7,23},{8,24},{9,... | collective-permute-start | bytes 196616 | tf_op jit(solution)/shard_map/ppermute | solution.py:28
  20.3 5.2 %collective-permute-start.4 = (bf16[2,16,1024]{2,1,0:T(8,128)(2,1)S(1)}, bf16[2,16,1024]{2,1,0:T(8,128)(2,1)S(1)}, u32[]{:S(2)}, u32[]{:S(2)}) collective-permute-start(bf16[2,16,1024]{2,1,0:T(8,128)(2,1)S(1)} %fusion.4), channel_id=1, source_target_pairs={{0,16},{1,17},{2,18},{3,19},{4,20},{5,21},{6,22},{7,23},{8,24},{9,... | collective-permute-start | bytes 196616 | tf_op jit(solution)/shard_map/ppermute | solution.py:28
  23.3 4.8 %collective-permute-start.10 = (bf16[2,16,1024]{2,1,0:T(8,128)(2,1)S(1)}, bf16[2,16,1024]{2,1,0:T(8,128)(2,1)S(1)}, u32[]{:S(2)}, u32[]{:S(2)}) collective-permute-start(bf16[2,16,1024]{2,1,0:T(8,128)(2,1)S(1)} %fusion.2), channel_id=1, source_target_pairs={{0,2},{1,3},{2,0},{3,1},{4,6},{5,7},{6,4},{7,5},{8,10},{9,11},{10,... | collective-permute-start | bytes 196616 | tf_op jit(solution)/shard_map/ppermute | solution.py:28
  25.5 4.3 %collective-permute-start.12 = (bf16[2,16,1024]{2,1,0:T(8,128)(2,1)S(1)}, bf16[2,16,1024]{2,1,0:T(8,128)(2,1)S(1)}, u32[]{:S(2)}, u32[]{:S(2)}) collective-permute-start(bf16[2,16,1024]{2,1,0:T(8,128)(2,1)S(1)} %fusion.3), channel_id=1, source_target_pairs={{0,2},{1,3},{2,0},{3,1},{4,6},{5,7},{6,4},{7,5},{8,10},{9,11},{10,... | collective-permute-start | bytes 196616 | tf_op jit(solution)/shard_map/ppermute | solution.py:28
  27.6 2.5 %collective-permute-start.14 = (f32[3,16,2048]{2,1,0:T(8,128)S(1)}, f32[3,16,2048]{2,1,0:T(8,128)S(1)}, u32[]{:S(2)}, u32[]{:S(2)}) collective-permute-start(f32[3,16,2048]{2,1,0:T(8,128)S(1)} %pad_maximum_fusion.refs_1_.refs_2_), channel_id=1, source_target_pairs={{0,1},{1,0},{2,3},{3,2},{4,5},{5,4},{6,7},{7,6},{8,9},{9,8},{10,11... | collective-permute-start | bytes 1179656 | tf_op jit(solution)/shard_map/ppermute | solution.py:28
  27.6 2.5 %collective-permute-start.15 = (f32[3,16,2048]{2,1,0:T(8,128)S(1)}, f32[3,16,2048]{2,1,0:T(8,128)S(1)}, u32[]{:S(2)}, u32[]{:S(2)}) collective-permute-start(f32[3,16,2048]{2,1,0:T(8,128)S(1)} %collective-permute-done.11.refs_2_.refs_3_), channel_id=1, source_target_pairs={{0,1},{1,0},{2,3},{3,2},{4,5},{5,4},{6,7},{7,6},{8,9},{9,8},{10,11... | collective-permute-start | bytes 1179656 | tf_op jit(solution)/shard_map/ppermute | solution.py:28
  28.1 1.9 %collective-permute-start.16 = (f32[2,16,1024]{2,1,0:T(8,128)S(1)}, f32[2,16,1024]{2,1,0:T(8,128)S(1)}, u32[]{:S(2)}, u32[]{:S(2)}) collective-permute-start(f32[2,16,1024]{2,1,0:T(8,128)S(1)} %add_multiply_fusion.1.refs_0_), channel_id=1, source_target_pairs={{0,1},{1,0},{2,3},{3,2},{4,5},{5,4},{6,7},{7,6},{8,9},{9,8},{10,11... | collective-permute-start | bytes 393224 | tf_op jit(solution)/shard_map/ppermute | solution.py:28
  29.9 1.4 %collective-permute-start.13 = (f32[2,16,1024]{2,1,0:T(8,128)S(1)}, f32[2,16,1024]{2,1,0:T(8,128)S(1)}, u32[]{:S(2)}, u32[]{:S(2)}) collective-permute-start(f32[2,16,1024]{2,1,0:T(8,128)S(1)} %add_multiply_fusion.refs_0_), channel_id=1, source_target_pairs={{0,1},{1,0},{2,3},{3,2},{4,5},{5,4},{6,7},{7,6},{8,9},{9,8},{10,11... | collective-permute-start | bytes 393224 | tf_op jit(solution)/shard_map/ppermute | solution.py:28

commit v9 on v7

--- a/solution.py
+++ b/solution.py
@@ -17,7 +17,7 @@
 BF16 = jnp.bfloat16
 BOTH = ("fsdp", "grp")
 SHARES = [1, 1]
-ORDERS = [[1, 0], [0, 1]]
+ORDERS = [[[1, 0], [0, 2]], [[1, 0], [0, 1]]]
 VMEM = pl.BlockSpec(memory_space=pltpu.VMEM)
 ANY = pl.BlockSpec(memory_space=pl.ANY)
 LIMIT = 4 * 2**20
@@ -244,20 +244,19 @@
 
     high = list(range(f_bits - 1, 1, -1))
     labels = [[[0] + high, [1] + high] for _ in cut]
-    orders = [o + list(range(len(o), f_bits)) for o in ORDERS]
+    orders = [[o + [b for b in range(f_bits) if b not in o] for o in ORDERS[k % 2]] for k in range(len(cut))]
     for step in range(f_bits):
-        masks = [ng << o[step] for o in orders]
+        masks = [[ng << o[step] for o in pair] for pair in orders]
         if step == 0:
             held = lax.optimization_barrier(((master, moment_one, moment_two), sent[-1]))[0]
             states = [jnp.stack(held)]
             for b in range(1, g_bits):
                 states = states + [swap(s, [1 << b] * 2) for s in states]
-        got = [swap(s, masks) for s in sent]
+        got = [swap(s, m) for s, m in zip(sent, masks)]
         ts = [k + x.astype(F32) for k, x in zip(kept, got)]
         if step == f_bits - 1:
             break
-        want = [o[step + 1] for o in orders]
-        moved = [onward(t, core, me_f, names, want) for t, names in zip(ts, labels)]
+        moved = [onward(t, core, me_f, names, [o[step + 1] for o in pair]) for t, names, pair in zip(ts, labels, orders)]
         sent, kept, labels = [list(m) for m in zip(*moved)]
 
     for b in range(1, g_bits):

time: 32.4 us -> 32.5 us (level)
  no operation moved by 1% of the time
where the time goes in v9:
time: 32.5 us; the launch traced here: 32.4 us
  starting transfers between devices  21.2 us (65%)
  waiting for transfers between devices  4.98 us (15%)
  Pallas kernels  3.04 us (9%)
  local copies, waits for them, and re-layouts  1.72 us (5%)
  between operations  0.96 us (3%)
  other arithmetic  0.51 us (2%)
    ppermute x17, starting transfers between devices, swap(): return lax.ppermute(x, BOTH, [(i, i ^ masks[i & 1]) for i in range(n)])  21.2 us
    ppermute x17, waiting for transfers between devices, swap(): return lax.ppermute(x, BOTH, [(i, i ^ masks[i & 1]) for i in range(n)])  4.98 us
    unnamed x10, local copies, waits for them, and re-layouts  1.61 us
    pallas_call x1, Pallas kernels, finish(): pl.pallas_call(functools.partial(kernel, True), out_shape=[shape] * 3 + s...  1.1 us
    pallas_call x3, Pallas kernels, gathered(): pl.pallas_call(kernel, out_shape=[jax.ShapeDtypeStruct((2, nf // 4, ng //...  1.09 us
    pallas_call x1, Pallas kernels, finish(): pl.pallas_call(functools.partial(kernel, False), out_shape=shapes, in_spe...  0.85 us
  transfers between devices with their start and end apart: 17, of which 8 were waited for; matrix products, arithmetic and copies ran while one was open for 2% of the time, Pallas kernels for 6%

profile of v9, /device:TPU:0, one launch (start us, length us, event | category | flops | bytes accessed | tf_op | source)
XLA Modules:
  0.0 32.4 jit_solution(10968443044756223980)
XLA Ops:
  0.6 0.0 copy-start
  0.6 1.6 %copy-done = bf16[1,1,128,8192]{3,2,1,0:T(8,128)(2,1)S(1)} copy-done((bf16[1,1,128,8192]{3,2,1,0:T(8,128)(2,1)S(1)}, bf16[1,1,128,8192]{3,2,1,0:T(8,128)(2,1)}, u32[]{:S(2)}) %copy-start) | copy-done | bytes 2097176
  2.2 0.3 shard_map.101
  2.5 0.0 copy-start.1
  2.5 0.5 %collective-permute-start.2 = (bf16[2,2,2,16,1024]{4,3,2,1,0:T(8,128)(2,1)S(1)}, bf16[2,2,2,16,1024]{4,3,2,1,0:T(8,128)(2,1)S(1)}, u32[]{:S(2)}, u32[]{:S(2)}) collective-permute-start(bf16[2,2,2,16,1024]{4,3,2,1,0:T(8,128)(2,1)S(1)} %get-tuple-element.38), channel_id=1, source_target_pairs={{0,1},{1,0},{2,3},{3,2},{4,5},{5,4},{6,7},{7,6},{8,9},{9,8},{10,11... | collective-permute-start | bytes 786440 | tf_op jit(solution)/shard_map/ppermute | solution.py:28
  3.0 0.3 shard_map.99
  3.3 0.0 copy-start.2
  3.3 0.0 copy-start.3
  3.3 0.0 copy-start.4
  3.3 0.1 collective-permute-start
  3.4 0.7 %collective-permute-done.2 = bf16[2,2,2,16,1024]{4,3,2,1,0:T(8,128)(2,1)S(1)} collective-permute-done((bf16[2,2,2,16,1024]{4,3,2,1,0:T(8,128)(2,1)S(1)}, bf16[2,2,2,16,1024]{4,3,2,1,0:T(8,128)(2,1)S(1)}, u32[]{:S(2)}, u32[]{:S(2)}) %collective-permute-start.2) | collective-permute-done | bytes 262176 | tf_op jit(solution)/shard_map/ppermute | solution.py:28
  4.2 0.1 add_convert_fusion
  4.3 3.0 %collective-permute-start.3 = (bf16[2,2,2,16,1024]{4,3,2,1,0:T(8,128)(2,1)S(1)}, bf16[2,2,2,16,1024]{4,3,2,1,0:T(8,128)(2,1)S(1)}, u32[]{:S(2)}, u32[]{:S(2)}) collective-permute-start(bf16[2,2,2,16,1024]{4,3,2,1,0:T(8,128)(2,1)S(1)} %add_convert_fusion), channel_id=1, source_target_pairs={{0,8},{1,5},{2,10},{3,7},{4,12},{5,1},{6,14},{7,3},{8,0},{9,13},{1... | collective-permute-start | bytes 786440 | tf_op jit(solution)/shard_map/ppermute | solution.py:28
  7.3 0.0 collective-permute-done
  7.3 0.1 add_convert_fusion.1
  7.3 0.0 copy-done.1
  7.3 0.6 %shard_map.100 = (bf16[2,2,2,16,1024]{4,3,2,1,0:T(8,128)(2,1)S(1)}, bf16[2,2,2,16,1024]{4,3,2,1,0:T(8,128)(2,1)S(1)}, bf16[2,2,2,16,1024]{4,3,2,1,0:T(8,128)(2,1)S(1)}, bf16[2,2,2,16,1024]{4,3,2,1,0:T(8,128)(2,1)S(1)}) custom-call(bf16[2,2,2,16,8192]{4,3,2,1,0:T(8,128)(2,1)S(1)} %bitcast.32), custom_call_target="tpu_custom_call" | custom-call | bytes 2097152 | tf_op jit(solution)/shard_map/pallas_call | solution.py:78
  7.9 0.1 collective-permute-start.1
  8.1 1.3 %collective-permute-start.8 = (bf16[2,2,2,16,1024]{4,3,2,1,0:T(8,128)(2,1)S(1)}, bf16[2,2,2,16,1024]{4,3,2,1,0:T(8,128)(2,1)S(1)}, u32[]{:S(2)}, u32[]{:S(2)}) collective-permute-start(bf16[2,2,2,16,1024]{4,3,2,1,0:T(8,128)(2,1)S(1)} %add_convert_fusion.1), channel_id=1, source_target_pairs={{0,8},{1,5},{2,10},{3,7},{4,12},{5,1},{6,14},{7,3},{8,0},{9,13},{1... | collective-permute-start | bytes 786440 | tf_op jit(solution)/shard_map/ppermute | solution.py:28
  9.4 0.4 %collective-permute-start.7 = (bf16[2,2,2,16,1024]{4,3,2,1,0:T(8,128)(2,1)S(1)}, bf16[2,2,2,16,1024]{4,3,2,1,0:T(8,128)(2,1)S(1)}, u32[]{:S(2)}, u32[]{:S(2)}) collective-permute-start(bf16[2,2,2,16,1024]{4,3,2,1,0:T(8,128)(2,1)S(1)} %get-tuple-element.40), channel_id=1, source_target_pairs={{0,1},{1,0},{2,3},{3,2},{4,5},{5,4},{6,7},{7,6},{8,9},{9,8},{10,11... | collective-permute-start | bytes 786440 | tf_op jit(solution)/shard_map/ppermute | solution.py:28
  9.7 0.0 copy-done.2
  9.8 0.0 copy-done.3
  9.8 0.0 copy-done.4
  9.8 1.6 %collective-permute-start.13 = (f32[3,16,2048]{2,1,0:T(8,128)S(1)}, f32[3,16,2048]{2,1,0:T(8,128)S(1)}, u32[]{:S(2)}, u32[]{:S(2)}) collective-permute-start(f32[3,16,2048]{2,1,0:T(8,128)S(1)} %pad_maximum_fusion.refs_3_), channel_id=1, source_target_pairs={{0,2},{1,3},{2,0},{3,1},{4,6},{5,7},{6,4},{7,5},{8,10},{9,11},{10,... | collective-permute-start | bytes 1179656 | tf_op jit(solution)/shard_map/ppermute | solution.py:28
  11.3 0.3 collective-permute-done.3
  11.6 0.0 collective-permute-done.1
  11.6 0.1 convert_add_fusion.1
  11.8 2.0 %collective-permute-start.4 = (bf16[2,2,16,1024]{3,2,1,0:T(8,128)(2,1)S(1)}, bf16[2,2,16,1024]{3,2,1,0:T(8,128)(2,1)S(1)}, u32[]{:S(2)}, u32[]{:S(2)}) collective-permute-start(bf16[2,2,16,1024]{3,2,1,0:T(8,128)(2,1)S(1)} %pad_maximum_fusion.1), channel_id=1, source_target_pairs={{0,4},{1,17},{2,6},{3,19},{4,0},{5,21},{6,2},{7,23},{8,12},{9,25},... | collective-permute-start | bytes 393224 | tf_op jit(solution)/shard_map/ppermute | solution.py:28
  13.8 0.7 %collective-permute-done.8 = bf16[2,2,2,16,1024]{4,3,2,1,0:T(8,128)(2,1)S(1)} collective-permute-done((bf16[2,2,2,16,1024]{4,3,2,1,0:T(8,128)(2,1)S(1)}, bf16[2,2,2,16,1024]{4,3,2,1,0:T(8,128)(2,1)S(1)}, u32[]{:S(2)}, u32[]{:S(2)}) %collective-permute-start.8) | collective-permute-done | bytes 262176 | tf_op jit(solution)/shard_map/ppermute | solution.py:28
  14.5 0.0 collective-permute-done.7
  14.5 0.1 convert_add_fusion
  14.7 1.9 %collective-permute-start.9 = (bf16[2,2,16,1024]{3,2,1,0:T(8,128)(2,1)S(1)}, bf16[2,2,16,1024]{3,2,1,0:T(8,128)(2,1)S(1)}, u32[]{:S(2)}, u32[]{:S(2)}) collective-permute-start(bf16[2,2,16,1024]{3,2,1,0:T(8,128)(2,1)S(1)} %fusion), channel_id=1, source_target_pairs={{0,4},{1,9},{2,6},{3,11},{4,0},{5,13},{6,2},{7,15},{8,12},{9,1},{1... | collective-permute-start | bytes 393224 | tf_op jit(solution)/shard_map/ppermute | solution.py:28
  16.6 0.2 collective-permute-done.4
  16.9 3.2 %collective-permute-start.5 = (bf16[2,16,1024]{2,1,0:T(8,128)(2,1)S(1)}, bf16[2,16,1024]{2,1,0:T(8,128)(2,1)S(1)}, u32[]{:S(2)}, u32[]{:S(2)}) collective-permute-start(bf16[2,16,1024]{2,1,0:T(8,128)(2,1)S(1)} %fusion.5), channel_id=1, source_target_pairs={{0,16},{1,9},{2,18},{3,11},{4,20},{5,13},{6,22},{7,15},{8,24},{9,1... | collective-permute-start | bytes 196616 | tf_op jit(solution)/shard_map/ppermute | solution.py:28
  20.1 0.0 collective-permute-done.9
  20.1 3.4 %collective-permute-start.10 = (bf16[2,16,1024]{2,1,0:T(8,128)(2,1)S(1)}, bf16[2,16,1024]{2,1,0:T(8,128)(2,1)S(1)}, u32[]{:S(2)}, u32[]{:S(2)}) collective-permute-start(bf16[2,16,1024]{2,1,0:T(8,128)(2,1)S(1)} %fusion.6), channel_id=1, source_target_pairs={{0,16},{1,17},{2,18},{3,19},{4,20},{5,21},{6,22},{7,23},{8,24},{9,... | collective-permute-start | bytes 196616 | tf_op jit(solution)/shard_map/ppermute | solution.py:28
  23.5 0.0 collective-permute-done.5
  23.5 1.6 %collective-permute-start.6 = (bf16[2,16,1024]{2,1,0:T(8,128)(2,1)S(1)}, bf16[2,16,1024]{2,1,0:T(8,128)(2,1)S(1)}, u32[]{:S(2)}, u32[]{:S(2)}) collective-permute-start(bf16[2,16,1024]{2,1,0:T(8,128)(2,1)S(1)} %fusion.2), channel_id=1, source_target_pairs={{0,2},{1,3},{2,0},{3,1},{4,6},{5,7},{6,4},{7,5},{8,10},{9,11},{10,... | collective-permute-start | bytes 196616 | tf_op jit(solution)/shard_map/ppermute | solution.py:28
  25.1 0.7 %collective-permute-done.10 = bf16[2,16,1024]{2,1,0:T(8,128)(2,1)S(1)} collective-permute-done((bf16[2,16,1024]{2,1,0:T(8,128)(2,1)S(1)}, bf16[2,16,1024]{2,1,0:T(8,128)(2,1)S(1)}, u32[]{:S(2)}, u32[]{:S(2)}) %collective-permute-start.10) | collective-permute-done | bytes 65568 | tf_op jit(solution)/shard_map/ppermute | solution.py:28
  25.8 1.6 %collective-permute-start.11 = (bf16[2,16,1024]{2,1,0:T(8,128)(2,1)S(1)}, bf16[2,16,1024]{2,1,0:T(8,128)(2,1)S(1)}, u32[]{:S(2)}, u32[]{:S(2)}) collective-permute-start(bf16[2,16,1024]{2,1,0:T(8,128)(2,1)S(1)} %fusion.1), channel_id=1, source_target_pairs={{0,2},{1,3},{2,0},{3,1},{4,6},{5,7},{6,4},{7,5},{8,10},{9,11},{10,... | collective-permute-start | bytes 196616 | tf_op jit(solution)/shard_map/ppermute | solution.py:28
  27.3 0.0 collective-permute-done.13.refs_4_
  27.3 0.0 collective-permute-start.14
  27.3 0.5 %collective-permute-start.15 = (f32[3,16,2048]{2,1,0:T(8,128)S(1)}, f32[3,16,2048]{2,1,0:T(8,128)S(1)}, u32[]{:S(2)}, u32[]{:S(2)}) collective-permute-start(f32[3,16,2048]{2,1,0:T(8,128)S(1)} %collective-permute-done.13.refs_4_), channel_id=1, source_target_pairs={{0,1},{1,0},{2,3},{3,2},{4,5},{5,4},{6,7},{7,6},{8,9},{9,8},{10,11... | collective-permute-start | bytes 1179656 | tf_op jit(solution)/shard_map/ppermute | solution.py:28
  27.8 0.6 %collective-permute-done.6 = bf16[2,16,1024]{2,1,0:T(8,128)(2,1)S(1)} collective-permute-done((bf16[2,16,1024]{2,1,0:T(8,128)(2,1)S(1)}, bf16[2,16,1024]{2,1,0:T(8,128)(2,1)S(1)}, u32[]{:S(2)}, u32[]{:S(2)}) %collective-permute-start.6) | collective-permute-done | bytes 65568 | tf_op jit(solution)/shard_map/ppermute | solution.py:28
  28.5 0.1 collective-permute-start.12
  28.5 1.6 %collective-permute-done.11 = bf16[2,16,1024]{2,1,0:T(8,128)(2,1)S(1)} collective-permute-done((bf16[2,16,1024]{2,1,0:T(8,128)(2,1)S(1)}, bf16[2,16,1024]{2,1,0:T(8,128)(2,1)S(1)}, u32[]{:S(2)}, u32[]{:S(2)}) %collective-permute-start.11) | collective-permute-done | bytes 65568 | tf_op jit(solution)/shard_map/ppermute | solution.py:28
  30.1 0.1 collective-permute-start.16
  30.2 0.0 collective-permute-done.12.refs_2_
  30.2 0.0 collective-permute-done.14.refs_5_.refs_1_
  30.2 0.0 collective-permute-done.15.refs_6_.refs_2_
  30.2 1.1 %shard_map.102 = (f32[16,2048]{1,0:T(8,128)}, f32[16,2048]{1,0:T(8,128)}, f32[16,2048]{1,0:T(8,128)}, bf16[16,8192]{1,0:T(8,128)(2,1)}, f32[16,2048]{1,0:T(8,128...) custom-call(f32[2,16,1024]{2,1,0:T(8,128)S(1)} %add_multiply_fusion.1.refs_0_, f32[2,16,1024]{2,1,0:T(8,128)S(1)} %add_multiply_fusion.refs_1_, ...), custom_call_target="tpu_custom_call" | custom-call | flops 5242880 | bytes 1572864 | tf_op jit(solution)/shard_map/pallas_call | solution.py:167
  31.4 0.2 collective-permute-done.16.refs_0_
  31.5 0.8 %shard_map.103 = (bf16[16,8192]{1,0:T(8,128)(2,1)}, f32[16,2048]{1,0:T(8,128)}, f32[16,2048]{1,0:T(8,128)}, f32[16,2048]{1,0:T(8,128)}) custom-call(f32[2,16,1024]{2,1,0:T(8,128)S(1)} %collective-permute-done.16.refs_0_, ...), custom_call_target="tpu_custom_call", output_to_operand_aliasing={{0}: (3, {}), {1}: (4, {}), {2}: (5, {}), {3}: (6, {})} | custom-call | tf_op jit(solution)/shard_map/pallas_call | solution.py:176
  (13 shorter events, 0.3 us)
Async XLA Ops:
  0.6 1.6 %copy-start = (bf16[1,1,128,8192]{3,2,1,0:T(8,128)(2,1)S(1)}, bf16[1,1,128,8192]{3,2,1,0:T(8,128)(2,1)}, u32[]{:S(2)}) copy-start(bf16[1,1,128,8192]{3,2,1,0:T(8,128)(2,1)} %param.4) | copy-start | bytes 6291460
  2.5 4.8 %copy-start.1 = (bf16[1,1,128,8192]{3,2,1,0:T(8,128)(2,1)S(1)}, bf16[1,1,128,8192]{3,2,1,0:T(8,128)(2,1)}, u32[]{:S(2)}) copy-start(bf16[1,1,128,8192]{3,2,1,0:T(8,128)(2,1)} %param.4) | copy-start | bytes 6291460
  2.5 1.7 %collective-permute-start.2 = (bf16[2,2,2,16,1024]{4,3,2,1,0:T(8,128)(2,1)S(1)}, bf16[2,2,2,16,1024]{4,3,2,1,0:T(8,128)(2,1)S(1)}, u32[]{:S(2)}, u32[]{:S(2)}) collective-permute-start(bf16[2,2,2,16,1024]{4,3,2,1,0:T(8,128)(2,1)S(1)} %get-tuple-element.38), channel_id=1, source_target_pairs={{0,1},{1,0},{2,3},{3,2},{4,5},{5,4},{6,7},{7,6},{8,9},{9,8},{10,11... | collective-permute-start | bytes 786440 | tf_op jit(solution)/shard_map/ppermute | solution.py:28
  3.3 6.5 %copy-start.2 = (f32[16,2048]{1,0:T(8,128)S(1)}, f32[16,2048]{1,0:T(8,128)}, u32[]{:S(2)}) copy-start(f32[16,2048]{1,0:T(8,128)} %param.7) | copy-start | bytes 393220
  3.3 6.5 %copy-start.3 = (f32[16,2048]{1,0:T(8,128)S(1)}, f32[16,2048]{1,0:T(8,128)}, u32[]{:S(2)}) copy-start(f32[16,2048]{1,0:T(8,128)} %param.6) | copy-start | bytes 393220
  3.3 6.4 %copy-start.4 = (f32[16,2048]{1,0:T(8,128)S(1)}, f32[16,2048]{1,0:T(8,128)}, u32[]{:S(2)}) copy-start(f32[16,2048]{1,0:T(8,128)} %param.5) | copy-start | bytes 393220
  3.3 3.9 %collective-permute-start = (bf16[2,2,2,16,1024]{4,3,2,1,0:T(8,128)(2,1)S(1)}, bf16[2,2,2,16,1024]{4,3,2,1,0:T(8,128)(2,1)S(1)}, u32[]{:S(2)}, u32[]{:S(2)}) collective-permute-start(bf16[2,2,2,16,1024]{4,3,2,1,0:T(8,128)(2,1)S(1)} %get-tuple-element.33), channel_id=1, source_target_pairs={{0,1},{1,0},{2,3},{3,2},{4,5},{5,4},{6,7},{7,6},{8,9},{9,8},{10,11... | collective-permute-start | bytes 786440 | tf_op jit(solution)/shard_map/ppermute | solution.py:28
  4.3 7.4 %collective-permute-start.3 = (bf16[2,2,2,16,1024]{4,3,2,1,0:T(8,128)(2,1)S(1)}, bf16[2,2,2,16,1024]{4,3,2,1,0:T(8,128)(2,1)S(1)}, u32[]{:S(2)}, u32[]{:S(2)}) collective-permute-start(bf16[2,2,2,16,1024]{4,3,2,1,0:T(8,128)(2,1)S(1)} %add_convert_fusion), channel_id=1, source_target_pairs={{0,8},{1,5},{2,10},{3,7},{4,12},{5,1},{6,14},{7,3},{8,0},{9,13},{1... | collective-permute-start | bytes 786440 | tf_op jit(solution)/shard_map/ppermute | solution.py:28
  7.9 3.7 %collective-permute-start.1 = (bf16[2,2,2,16,1024]{4,3,2,1,0:T(8,128)(2,1)S(1)}, bf16[2,2,2,16,1024]{4,3,2,1,0:T(8,128)(2,1)S(1)}, u32[]{:S(2)}, u32[]{:S(2)}) collective-permute-start(bf16[2,2,2,16,1024]{4,3,2,1,0:T(8,128)(2,1)S(1)} %get-tuple-element.36), channel_id=1, source_target_pairs={{0,1},{1,0},{2,3},{3,2},{4,5},{5,4},{6,7},{7,6},{8,9},{9,8},{10,11... | collective-permute-start | bytes 786440 | tf_op jit(solution)/shard_map/ppermute | solution.py:28
  8.1 6.4 %collective-permute-start.8 = (bf16[2,2,2,16,1024]{4,3,2,1,0:T(8,128)(2,1)S(1)}, bf16[2,2,2,16,1024]{4,3,2,1,0:T(8,128)(2,1)S(1)}, u32[]{:S(2)}, u32[]{:S(2)}) collective-permute-start(bf16[2,2,2,16,1024]{4,3,2,1,0:T(8,128)(2,1)S(1)} %add_convert_fusion.1), channel_id=1, source_target_pairs={{0,8},{1,5},{2,10},{3,7},{4,12},{5,1},{6,14},{7,3},{8,0},{9,13},{1... | collective-permute-start | bytes 786440 | tf_op jit(solution)/shard_map/ppermute | solution.py:28
  9.4 5.2 %collective-permute-start.7 = (bf16[2,2,2,16,1024]{4,3,2,1,0:T(8,128)(2,1)S(1)}, bf16[2,2,2,16,1024]{4,3,2,1,0:T(8,128)(2,1)S(1)}, u32[]{:S(2)}, u32[]{:S(2)}) collective-permute-start(bf16[2,2,2,16,1024]{4,3,2,1,0:T(8,128)(2,1)S(1)} %get-tuple-element.40), channel_id=1, source_target_pairs={{0,1},{1,0},{2,3},{3,2},{4,5},{5,4},{6,7},{7,6},{8,9},{9,8},{10,11... | collective-permute-start | bytes 786440 | tf_op jit(solution)/shard_map/ppermute | solution.py:28
  9.8 17.5 %collective-permute-start.13 = (f32[3,16,2048]{2,1,0:T(8,128)S(1)}, f32[3,16,2048]{2,1,0:T(8,128)S(1)}, u32[]{:S(2)}, u32[]{:S(2)}) collective-permute-start(f32[3,16,2048]{2,1,0:T(8,128)S(1)} %pad_maximum_fusion.refs_3_), channel_id=1, source_target_pairs={{0,2},{1,3},{2,0},{3,1},{4,6},{5,7},{6,4},{7,5},{8,10},{9,11},{10,... | collective-permute-start | bytes 1179656 | tf_op jit(solution)/shard_map/ppermute | solution.py:28
  11.8 5.0 %collective-permute-start.4 = (bf16[2,2,16,1024]{3,2,1,0:T(8,128)(2,1)S(1)}, bf16[2,2,16,1024]{3,2,1,0:T(8,128)(2,1)S(1)}, u32[]{:S(2)}, u32[]{:S(2)}) collective-permute-start(bf16[2,2,16,1024]{3,2,1,0:T(8,128)(2,1)S(1)} %pad_maximum_fusion.1), channel_id=1, source_target_pairs={{0,4},{1,17},{2,6},{3,19},{4,0},{5,21},{6,2},{7,23},{8,12},{9,25},... | collective-permute-start | bytes 393224 | tf_op jit(solution)/shard_map/ppermute | solution.py:28
  14.7 5.4 %collective-permute-start.9 = (bf16[2,2,16,1024]{3,2,1,0:T(8,128)(2,1)S(1)}, bf16[2,2,16,1024]{3,2,1,0:T(8,128)(2,1)S(1)}, u32[]{:S(2)}, u32[]{:S(2)}) collective-permute-start(bf16[2,2,16,1024]{3,2,1,0:T(8,128)(2,1)S(1)} %fusion), channel_id=1, source_target_pairs={{0,4},{1,9},{2,6},{3,11},{4,0},{5,13},{6,2},{7,15},{8,12},{9,1},{1... | collective-permute-start | bytes 393224 | tf_op jit(solution)/shard_map/ppermute | solution.py:28
  16.9 6.6 %collective-permute-start.5 = (bf16[2,16,1024]{2,1,0:T(8,128)(2,1)S(1)}, bf16[2,16,1024]{2,1,0:T(8,128)(2,1)S(1)}, u32[]{:S(2)}, u32[]{:S(2)}) collective-permute-start(bf16[2,16,1024]{2,1,0:T(8,128)(2,1)S(1)} %fusion.5), channel_id=1, source_target_pairs={{0,16},{1,9},{2,18},{3,11},{4,20},{5,13},{6,22},{7,15},{8,24},{9,1... | collective-permute-start | bytes 196616 | tf_op jit(solution)/shard_map/ppermute | solution.py:28
  20.1 5.6 %collective-permute-start.10 = (bf16[2,16,1024]{2,1,0:T(8,128)(2,1)S(1)}, bf16[2,16,1024]{2,1,0:T(8,128)(2,1)S(1)}, u32[]{:S(2)}, u32[]{:S(2)}) collective-permute-start(bf16[2,16,1024]{2,1,0:T(8,128)(2,1)S(1)} %fusion.6), channel_id=1, source_target_pairs={{0,16},{1,17},{2,18},{3,19},{4,20},{5,21},{6,22},{7,23},{8,24},{9,... | collective-permute-start | bytes 196616 | tf_op jit(solution)/shard_map/ppermute | solution.py:28
  23.5 4.9 %collective-permute-start.6 = (bf16[2,16,1024]{2,1,0:T(8,128)(2,1)S(1)}, bf16[2,16,1024]{2,1,0:T(8,128)(2,1)S(1)}, u32[]{:S(2)}, u32[]{:S(2)}) collective-permute-start(bf16[2,16,1024]{2,1,0:T(8,128)(2,1)S(1)} %fusion.2), channel_id=1, source_target_pairs={{0,2},{1,3},{2,0},{3,1},{4,6},{5,7},{6,4},{7,5},{8,10},{9,11},{10,... | collective-permute-start | bytes 196616 | tf_op jit(solution)/shard_map/ppermute | solution.py:28
  25.8 4.3 %collective-permute-start.11 = (bf16[2,16,1024]{2,1,0:T(8,128)(2,1)S(1)}, bf16[2,16,1024]{2,1,0:T(8,128)(2,1)S(1)}, u32[]{:S(2)}, u32[]{:S(2)}) collective-permute-start(bf16[2,16,1024]{2,1,0:T(8,128)(2,1)S(1)} %fusion.1), channel_id=1, source_target_pairs={{0,2},{1,3},{2,0},{3,1},{4,6},{5,7},{6,4},{7,5},{8,10},{9,11},{10,... | collective-permute-start | bytes 196616 | tf_op jit(solution)/shard_map/ppermute | solution.py:28
  27.3 2.9 %collective-permute-start.14 = (f32[3,16,2048]{2,1,0:T(8,128)S(1)}, f32[3,16,2048]{2,1,0:T(8,128)S(1)}, u32[]{:S(2)}, u32[]{:S(2)}) collective-permute-start(f32[3,16,2048]{2,1,0:T(8,128)S(1)} %pad_maximum_fusion.refs_3_), channel_id=1, source_target_pairs={{0,1},{1,0},{2,3},{3,2},{4,5},{5,4},{6,7},{7,6},{8,9},{9,8},{10,11... | collective-permute-start | bytes 1179656 | tf_op jit(solution)/shard_map/ppermute | solution.py:28
  27.3 2.9 %collective-permute-start.15 = (f32[3,16,2048]{2,1,0:T(8,128)S(1)}, f32[3,16,2048]{2,1,0:T(8,128)S(1)}, u32[]{:S(2)}, u32[]{:S(2)}) collective-permute-start(f32[3,16,2048]{2,1,0:T(8,128)S(1)} %collective-permute-done.13.refs_4_), channel_id=1, source_target_pairs={{0,1},{1,0},{2,3},{3,2},{4,5},{5,4},{6,7},{7,6},{8,9},{9,8},{10,11... | collective-permute-start | bytes 1179656 | tf_op jit(solution)/shard_map/ppermute | solution.py:28
  28.5 1.8 %collective-permute-start.12 = (f32[2,16,1024]{2,1,0:T(8,128)S(1)}, f32[2,16,1024]{2,1,0:T(8,128)S(1)}, u32[]{:S(2)}, u32[]{:S(2)}) collective-permute-start(f32[2,16,1024]{2,1,0:T(8,128)S(1)} %add_multiply_fusion.1.refs_0_), channel_id=1, source_target_pairs={{0,1},{1,0},{2,3},{3,2},{4,5},{5,4},{6,7},{7,6},{8,9},{9,8},{10,11... | collective-permute-start | bytes 393224 | tf_op jit(solution)/shard_map/ppermute | solution.py:28
  30.1 1.4 %collective-permute-start.16 = (f32[2,16,1024]{2,1,0:T(8,128)S(1)}, f32[2,16,1024]{2,1,0:T(8,128)S(1)}, u32[]{:S(2)}, u32[]{:S(2)}) collective-permute-start(f32[2,16,1024]{2,1,0:T(8,128)S(1)} %add_multiply_fusion.refs_1_), channel_id=1, source_target_pairs={{0,1},{1,0},{2,3},{3,2},{4,5},{5,4},{6,7},{7,6},{8,9},{9,8},{10,11... | collective-permute-start | bytes 393224 | tf_op jit(solution)/shard_map/ppermute | solution.py:28

commit v10 on v7

--- a/solution.py
+++ b/solution.py
@@ -130,7 +130,7 @@
 
         def block(n, part, state, x, edge, keep):
             start, width = edge
-            new = updated(part[x], *[state[i, :, start : start + width] for i in range(3)])
+            new = updated(part[x].astype(F32), *[state[i, :, start : start + width] for i in range(3)])
             thin[n, :, start : start + width] = new[0].astype(BF16)
             if keep:
                 for i in range(3):
@@ -149,7 +149,7 @@
             for k in range(ng // 2):
                 @pl.when((me ^ last) >> 1 == k)
                 def _():
-                    new = updated(part[last >> 1], *[near[k][i, :, start : start + width] for i in range(3)])
+                    new = updated(part[last >> 1].astype(F32), *[near[k][i, :, start : start + width] for i in range(3)])
                     for i in range(3):
                         wide[3 + i, :, start : start + width] = new[i]
             for i in range(3):
@@ -191,7 +191,7 @@
     ng = 2 * len(states)
     gradient = jnp.stack([pick((own, other)[r & 1], (me >> 1) ^ (r >> 1), 0) for r in range(ng)])
     state = jnp.stack([(states, near)[r & 1][r >> 1] for r in range(ng)])
-    new = updated(gradient, state[:, 0], state[:, 1], state[:, 2])
+    new = updated(gradient.astype(F32), state[:, 0], state[:, 1], state[:, 2])
     blocks = new[0].astype(BF16)
     weights = jnp.zeros((own.shape[1], cols * ng), BF16)
     for r in range(ng):
@@ -267,7 +267,7 @@
             near = [swap(s, [1, 1]) for s in states]
         got = [swap(t, [1 << b] * 2) for t in rounded]
         ts = [t.astype(F32) + x.astype(F32) for t, x in zip(rounded, got)]
-    own = [t / (ng * nf) for t in ts]
+    own = [(t / (ng * nf)).astype(BF16) for t in ts]
     other = [swap(t, [1, 1]) for t in own]
     return (finish if local else finish_plain)(own, other, states, near, cols)
 

time: 32.4 us -> 32.4 us (level)
  no operation moved by 1% of the time
where the time goes in v10:
time: 32.4 us; the launch traced here: 32.2 us
  starting transfers between devices  21.2 us (65%)
  waiting for transfers between devices  4.92 us (15%)
  Pallas kernels  3.05 us (9%)
  local copies, waits for them, and re-layouts  1.69 us (5%)
  between operations  0.88 us (3%)
  other arithmetic  0.49 us (2%)
    ppermute x17, starting transfers between devices, swap(): return lax.ppermute(x, BOTH, [(i, i ^ masks[i & 1]) for i in range(n)])  21.2 us
    ppermute x17, waiting for transfers between devices, swap(): return lax.ppermute(x, BOTH, [(i, i ^ masks[i & 1]) for i in range(n)])  4.92 us
    unnamed x10, local copies, waits for them, and re-layouts  1.61 us
    pallas_call x1, Pallas kernels, finish(): pl.pallas_call(functools.partial(kernel, True), out_shape=[shape] * 3 + s...  1.12 us
    pallas_call x3, Pallas kernels, gathered(): pl.pallas_call(kernel, out_shape=[jax.ShapeDtypeStruct((2, nf // 4, ng //...  1.09 us
    pallas_call x1, Pallas kernels, finish(): pl.pallas_call(functools.partial(kernel, False), out_shape=shapes, in_spe...  0.84 us
  transfers between devices with their start and end apart: 17, of which 8 were waited for; matrix products, arithmetic and copies ran while one was open for 2% of the time, Pallas kernels for 6%

profile of v10, /device:TPU:0, one launch (start us, length us, event | category | flops | bytes accessed | tf_op | source)
XLA Modules:
  0.0 32.2 jit_solution(16774790272103366696)
XLA Ops:
  0.6 0.0 copy-start
  0.6 1.6 %copy-done = bf16[1,1,128,8192]{3,2,1,0:T(8,128)(2,1)S(1)} copy-done((bf16[1,1,128,8192]{3,2,1,0:T(8,128)(2,1)S(1)}, bf16[1,1,128,8192]{3,2,1,0:T(8,128)(2,1)}, u32[]{:S(2)}) %copy-start) | copy-done | bytes 2097176
  2.2 0.3 shard_map.101
  2.5 0.0 copy-start.1
  2.5 0.5 %collective-permute-start.2 = (bf16[2,2,2,16,1024]{4,3,2,1,0:T(8,128)(2,1)S(1)}, bf16[2,2,2,16,1024]{4,3,2,1,0:T(8,128)(2,1)S(1)}, u32[]{:S(2)}, u32[]{:S(2)}) collective-permute-start(bf16[2,2,2,16,1024]{4,3,2,1,0:T(8,128)(2,1)S(1)} %get-tuple-element.38), channel_id=1, source_target_pairs={{0,1},{1,0},{2,3},{3,2},{4,5},{5,4},{6,7},{7,6},{8,9},{9,8},{10,11... | collective-permute-start | bytes 786440 | tf_op jit(solution)/shard_map/ppermute | solution.py:28
  3.0 0.3 shard_map.99
  3.3 0.0 copy-start.2
  3.3 0.0 copy-start.3
  3.3 0.0 copy-start.4
  3.3 0.1 collective-permute-start
  3.4 0.7 %collective-permute-done.2 = bf16[2,2,2,16,1024]{4,3,2,1,0:T(8,128)(2,1)S(1)} collective-permute-done((bf16[2,2,2,16,1024]{4,3,2,1,0:T(8,128)(2,1)S(1)}, bf16[2,2,2,16,1024]{4,3,2,1,0:T(8,128)(2,1)S(1)}, u32[]{:S(2)}, u32[]{:S(2)}) %collective-permute-start.2) | collective-permute-done | bytes 262176 | tf_op jit(solution)/shard_map/ppermute | solution.py:28
  4.2 0.1 add_convert_fusion
  4.3 3.0 %collective-permute-start.3 = (bf16[2,2,2,16,1024]{4,3,2,1,0:T(8,128)(2,1)S(1)}, bf16[2,2,2,16,1024]{4,3,2,1,0:T(8,128)(2,1)S(1)}, u32[]{:S(2)}, u32[]{:S(2)}) collective-permute-start(bf16[2,2,2,16,1024]{4,3,2,1,0:T(8,128)(2,1)S(1)} %add_convert_fusion), channel_id=1, source_target_pairs={{0,8},{1,5},{2,10},{3,7},{4,12},{5,1},{6,14},{7,3},{8,0},{9,13},{1... | collective-permute-start | bytes 786440 | tf_op jit(solution)/shard_map/ppermute | solution.py:28
  7.3 0.0 collective-permute-done
  7.3 0.1 add_convert_fusion.1
  7.3 0.0 copy-done.1
  7.3 0.6 %shard_map.100 = (bf16[2,2,2,16,1024]{4,3,2,1,0:T(8,128)(2,1)S(1)}, bf16[2,2,2,16,1024]{4,3,2,1,0:T(8,128)(2,1)S(1)}, bf16[2,2,2,16,1024]{4,3,2,1,0:T(8,128)(2,1)S(1)}, bf16[2,2,2,16,1024]{4,3,2,1,0:T(8,128)(2,1)S(1)}) custom-call(bf16[2,2,2,16,8192]{4,3,2,1,0:T(8,128)(2,1)S(1)} %bitcast.28), custom_call_target="tpu_custom_call" | custom-call | bytes 2097152 | tf_op jit(solution)/shard_map/pallas_call | solution.py:78
  7.9 0.1 collective-permute-start.1
  8.0 1.3 %collective-permute-start.8 = (bf16[2,2,2,16,1024]{4,3,2,1,0:T(8,128)(2,1)S(1)}, bf16[2,2,2,16,1024]{4,3,2,1,0:T(8,128)(2,1)S(1)}, u32[]{:S(2)}, u32[]{:S(2)}) collective-permute-start(bf16[2,2,2,16,1024]{4,3,2,1,0:T(8,128)(2,1)S(1)} %add_convert_fusion.1), channel_id=1, source_target_pairs={{0,8},{1,5},{2,10},{3,7},{4,12},{5,1},{6,14},{7,3},{8,0},{9,13},{1... | collective-permute-start | bytes 786440 | tf_op jit(solution)/shard_map/ppermute | solution.py:28
  9.4 0.4 %collective-permute-start.7 = (bf16[2,2,2,16,1024]{4,3,2,1,0:T(8,128)(2,1)S(1)}, bf16[2,2,2,16,1024]{4,3,2,1,0:T(8,128)(2,1)S(1)}, u32[]{:S(2)}, u32[]{:S(2)}) collective-permute-start(bf16[2,2,2,16,1024]{4,3,2,1,0:T(8,128)(2,1)S(1)} %get-tuple-element.40), channel_id=1, source_target_pairs={{0,1},{1,0},{2,3},{3,2},{4,5},{5,4},{6,7},{7,6},{8,9},{9,8},{10,11... | collective-permute-start | bytes 786440 | tf_op jit(solution)/shard_map/ppermute | solution.py:28
  9.7 0.0 copy-done.2
  9.8 0.0 copy-done.3
  9.8 0.0 copy-done.4
  9.8 1.6 %collective-permute-start.13 = (f32[3,16,2048]{2,1,0:T(8,128)S(1)}, f32[3,16,2048]{2,1,0:T(8,128)S(1)}, u32[]{:S(2)}, u32[]{:S(2)}) collective-permute-start(f32[3,16,2048]{2,1,0:T(8,128)S(1)} %pad_maximum_fusion.refs_3_), channel_id=1, source_target_pairs={{0,2},{1,3},{2,0},{3,1},{4,6},{5,7},{6,4},{7,5},{8,10},{9,11},{10,... | collective-permute-start | bytes 1179656 | tf_op jit(solution)/shard_map/ppermute | solution.py:28
  11.3 0.3 collective-permute-done.3
  11.6 0.0 collective-permute-done.1
  11.6 0.1 convert_add_fusion.1
  11.8 2.0 %collective-permute-start.4 = (bf16[2,2,16,1024]{3,2,1,0:T(8,128)(2,1)S(1)}, bf16[2,2,16,1024]{3,2,1,0:T(8,128)(2,1)S(1)}, u32[]{:S(2)}, u32[]{:S(2)}) collective-permute-start(bf16[2,2,16,1024]{3,2,1,0:T(8,128)(2,1)S(1)} %fusion), channel_id=1, source_target_pairs={{0,4},{1,9},{2,6},{3,11},{4,0},{5,13},{6,2},{7,15},{8,12},{9,1},{1... | collective-permute-start | bytes 393224 | tf_op jit(solution)/shard_map/ppermute | solution.py:28
  13.8 1.1 %collective-permute-done.8 = bf16[2,2,2,16,1024]{4,3,2,1,0:T(8,128)(2,1)S(1)} collective-permute-done((bf16[2,2,2,16,1024]{4,3,2,1,0:T(8,128)(2,1)S(1)}, bf16[2,2,2,16,1024]{4,3,2,1,0:T(8,128)(2,1)S(1)}, u32[]{:S(2)}, u32[]{:S(2)}) %collective-permute-start.8) | collective-permute-done | bytes 262176 | tf_op jit(solution)/shard_map/ppermute | solution.py:28
  14.9 0.0 collective-permute-done.7
  14.9 0.1 convert_add_fusion
  15.0 2.2 %collective-permute-start.9 = (bf16[2,2,16,1024]{3,2,1,0:T(8,128)(2,1)S(1)}, bf16[2,2,16,1024]{3,2,1,0:T(8,128)(2,1)S(1)}, u32[]{:S(2)}, u32[]{:S(2)}) collective-permute-start(bf16[2,2,16,1024]{3,2,1,0:T(8,128)(2,1)S(1)} %fusion.1), channel_id=1, source_target_pairs={{0,4},{1,9},{2,6},{3,11},{4,0},{5,13},{6,2},{7,15},{8,12},{9,1},{1... | collective-permute-start | bytes 393224 | tf_op jit(solution)/shard_map/ppermute | solution.py:28
  17.3 0.0 collective-permute-done.4
  17.3 2.7 %collective-permute-start.5 = (bf16[2,16,1024]{2,1,0:T(8,128)(2,1)S(1)}, bf16[2,16,1024]{2,1,0:T(8,128)(2,1)S(1)}, u32[]{:S(2)}, u32[]{:S(2)}) collective-permute-start(bf16[2,16,1024]{2,1,0:T(8,128)(2,1)S(1)} %fusion.4), channel_id=1, source_target_pairs={{0,16},{1,17},{2,18},{3,19},{4,20},{5,21},{6,22},{7,23},{8,24},{9,... | collective-permute-start | bytes 196616 | tf_op jit(solution)/shard_map/ppermute | solution.py:28
  20.0 0.2 collective-permute-done.9
  20.3 3.2 %collective-permute-start.10 = (bf16[2,16,1024]{2,1,0:T(8,128)(2,1)S(1)}, bf16[2,16,1024]{2,1,0:T(8,128)(2,1)S(1)}, u32[]{:S(2)}, u32[]{:S(2)}) collective-permute-start(bf16[2,16,1024]{2,1,0:T(8,128)(2,1)S(1)} %fusion.5), channel_id=1, source_target_pairs={{0,16},{1,17},{2,18},{3,19},{4,20},{5,21},{6,22},{7,23},{8,24},{9,... | collective-permute-start | bytes 196616 | tf_op jit(solution)/shard_map/ppermute | solution.py:28
  23.4 0.0 collective-permute-done.5
  23.4 1.6 %collective-permute-start.6 = (bf16[2,16,1024]{2,1,0:T(8,128)(2,1)S(1)}, bf16[2,16,1024]{2,1,0:T(8,128)(2,1)S(1)}, u32[]{:S(2)}, u32[]{:S(2)}) collective-permute-start(bf16[2,16,1024]{2,1,0:T(8,128)(2,1)S(1)} %fusion.3), channel_id=1, source_target_pairs={{0,2},{1,3},{2,0},{3,1},{4,6},{5,7},{6,4},{7,5},{8,10},{9,11},{10,... | collective-permute-start | bytes 196616 | tf_op jit(solution)/shard_map/ppermute | solution.py:28
  25.0 0.7 %collective-permute-done.10 = bf16[2,16,1024]{2,1,0:T(8,128)(2,1)S(1)} collective-permute-done((bf16[2,16,1024]{2,1,0:T(8,128)(2,1)S(1)}, bf16[2,16,1024]{2,1,0:T(8,128)(2,1)S(1)}, u32[]{:S(2)}, u32[]{:S(2)}) %collective-permute-start.10) | collective-permute-done | bytes 65568 | tf_op jit(solution)/shard_map/ppermute | solution.py:28
  25.7 1.9 %collective-permute-start.11 = (bf16[2,16,1024]{2,1,0:T(8,128)(2,1)S(1)}, bf16[2,16,1024]{2,1,0:T(8,128)(2,1)S(1)}, u32[]{:S(2)}, u32[]{:S(2)}) collective-permute-start(bf16[2,16,1024]{2,1,0:T(8,128)(2,1)S(1)} %fusion.2), channel_id=1, source_target_pairs={{0,2},{1,3},{2,0},{3,1},{4,6},{5,7},{6,4},{7,5},{8,10},{9,11},{10,... | collective-permute-start | bytes 196616 | tf_op jit(solution)/shard_map/ppermute | solution.py:28
  27.6 0.0 collective-permute-done.13.refs_4_
  27.6 0.0 collective-permute-start.14
  27.6 0.5 %collective-permute-start.15 = (f32[3,16,2048]{2,1,0:T(8,128)S(1)}, f32[3,16,2048]{2,1,0:T(8,128)S(1)}, u32[]{:S(2)}, u32[]{:S(2)}) collective-permute-start(f32[3,16,2048]{2,1,0:T(8,128)S(1)} %collective-permute-done.13.refs_4_), channel_id=1, source_target_pairs={{0,1},{1,0},{2,3},{3,2},{4,5},{5,4},{6,7},{7,6},{8,9},{9,8},{10,11... | collective-permute-start | bytes 1179656 | tf_op jit(solution)/shard_map/ppermute | solution.py:28
  28.1 0.3 collective-permute-done.6
  28.4 0.1 collective-permute-start.12
  28.5 1.5 %collective-permute-done.11 = bf16[2,16,1024]{2,1,0:T(8,128)(2,1)S(1)} collective-permute-done((bf16[2,16,1024]{2,1,0:T(8,128)(2,1)S(1)}, bf16[2,16,1024]{2,1,0:T(8,128)(2,1)S(1)}, u32[]{:S(2)}, u32[]{:S(2)}) %collective-permute-start.11) | collective-permute-done | bytes 65568 | tf_op jit(solution)/shard_map/ppermute | solution.py:28
  30.0 0.1 collective-permute-start.16
  30.1 0.0 collective-permute-done.12.refs_2_
  30.1 0.0 collective-permute-done.14.refs_5_.refs_1_
  30.1 0.0 collective-permute-done.15.refs_6_.refs_2_
  30.1 1.1 %shard_map.102 = (f32[16,2048]{1,0:T(8,128)}, f32[16,2048]{1,0:T(8,128)}, f32[16,2048]{1,0:T(8,128)}, bf16[16,8192]{1,0:T(8,128)(2,1)}, f32[16,2048]{1,0:T(8,128...) custom-call(bf16[2,16,1024]{2,1,0:T(8,128)(2,1)S(1)} %multiply_convert_fusion.1.refs_0_, ...), custom_call_target="tpu_custom_call" | custom-call | flops 5242880 | bytes 1572864 | tf_op jit(solution)/shard_map/pallas_call | solution.py:167
  31.3 0.1 collective-permute-done.16.refs_0_
  31.4 0.8 %shard_map.103 = (bf16[16,8192]{1,0:T(8,128)(2,1)}, f32[16,2048]{1,0:T(8,128)}, f32[16,2048]{1,0:T(8,128)}, f32[16,2048]{1,0:T(8,128)}) custom-call(bf16[2,16,1024]{2,1,0:T(8,128)(2,1)S(1)} %collective-permute-done.16.refs_0_, ...), custom_call_target="tpu_custom_call", output_to_operand_aliasing={{0}: (3, {}), {1}: (4, {}), {2}: (5, {}), {3}: (6, {})} | custom-call | tf_op jit(solution)/shard_map/pallas_call | solution.py:176
  (11 shorter events, 0.2 us)
Async XLA Ops:
  0.6 1.6 %copy-start = (bf16[1,1,128,8192]{3,2,1,0:T(8,128)(2,1)S(1)}, bf16[1,1,128,8192]{3,2,1,0:T(8,128)(2,1)}, u32[]{:S(2)}) copy-start(bf16[1,1,128,8192]{3,2,1,0:T(8,128)(2,1)} %param.4) | copy-start | bytes 6291460
  2.5 4.8 %copy-start.1 = (bf16[1,1,128,8192]{3,2,1,0:T(8,128)(2,1)S(1)}, bf16[1,1,128,8192]{3,2,1,0:T(8,128)(2,1)}, u32[]{:S(2)}) copy-start(bf16[1,1,128,8192]{3,2,1,0:T(8,128)(2,1)} %param.4) | copy-start | bytes 6291460
  2.5 1.7 %collective-permute-start.2 = (bf16[2,2,2,16,1024]{4,3,2,1,0:T(8,128)(2,1)S(1)}, bf16[2,2,2,16,1024]{4,3,2,1,0:T(8,128)(2,1)S(1)}, u32[]{:S(2)}, u32[]{:S(2)}) collective-permute-start(bf16[2,2,2,16,1024]{4,3,2,1,0:T(8,128)(2,1)S(1)} %get-tuple-element.38), channel_id=1, source_target_pairs={{0,1},{1,0},{2,3},{3,2},{4,5},{5,4},{6,7},{7,6},{8,9},{9,8},{10,11... | collective-permute-start | bytes 786440 | tf_op jit(solution)/shard_map/ppermute | solution.py:28
  3.3 6.5 %copy-start.2 = (f32[16,2048]{1,0:T(8,128)S(1)}, f32[16,2048]{1,0:T(8,128)}, u32[]{:S(2)}) copy-start(f32[16,2048]{1,0:T(8,128)} %param.7) | copy-start | bytes 393220
  3.3 6.5 %copy-start.3 = (f32[16,2048]{1,0:T(8,128)S(1)}, f32[16,2048]{1,0:T(8,128)}, u32[]{:S(2)}) copy-start(f32[16,2048]{1,0:T(8,128)} %param.6) | copy-start | bytes 393220
  3.3 6.4 %copy-start.4 = (f32[16,2048]{1,0:T(8,128)S(1)}, f32[16,2048]{1,0:T(8,128)}, u32[]{:S(2)}) copy-start(f32[16,2048]{1,0:T(8,128)} %param.5) | copy-start | bytes 393220
  3.3 3.9 %collective-permute-start = (bf16[2,2,2,16,1024]{4,3,2,1,0:T(8,128)(2,1)S(1)}, bf16[2,2,2,16,1024]{4,3,2,1,0:T(8,128)(2,1)S(1)}, u32[]{:S(2)}, u32[]{:S(2)}) collective-permute-start(bf16[2,2,2,16,1024]{4,3,2,1,0:T(8,128)(2,1)S(1)} %get-tuple-element.33), channel_id=1, source_target_pairs={{0,1},{1,0},{2,3},{3,2},{4,5},{5,4},{6,7},{7,6},{8,9},{9,8},{10,11... | collective-permute-start | bytes 786440 | tf_op jit(solution)/shard_map/ppermute | solution.py:28
  4.3 7.4 %collective-permute-start.3 = (bf16[2,2,2,16,1024]{4,3,2,1,0:T(8,128)(2,1)S(1)}, bf16[2,2,2,16,1024]{4,3,2,1,0:T(8,128)(2,1)S(1)}, u32[]{:S(2)}, u32[]{:S(2)}) collective-permute-start(bf16[2,2,2,16,1024]{4,3,2,1,0:T(8,128)(2,1)S(1)} %add_convert_fusion), channel_id=1, source_target_pairs={{0,8},{1,5},{2,10},{3,7},{4,12},{5,1},{6,14},{7,3},{8,0},{9,13},{1... | collective-permute-start | bytes 786440 | tf_op jit(solution)/shard_map/ppermute | solution.py:28
  7.9 3.7 %collective-permute-start.1 = (bf16[2,2,2,16,1024]{4,3,2,1,0:T(8,128)(2,1)S(1)}, bf16[2,2,2,16,1024]{4,3,2,1,0:T(8,128)(2,1)S(1)}, u32[]{:S(2)}, u32[]{:S(2)}) collective-permute-start(bf16[2,2,2,16,1024]{4,3,2,1,0:T(8,128)(2,1)S(1)} %get-tuple-element.36), channel_id=1, source_target_pairs={{0,1},{1,0},{2,3},{3,2},{4,5},{5,4},{6,7},{7,6},{8,9},{9,8},{10,11... | collective-permute-start | bytes 786440 | tf_op jit(solution)/shard_map/ppermute | solution.py:28
  8.0 6.8 %collective-permute-start.8 = (bf16[2,2,2,16,1024]{4,3,2,1,0:T(8,128)(2,1)S(1)}, bf16[2,2,2,16,1024]{4,3,2,1,0:T(8,128)(2,1)S(1)}, u32[]{:S(2)}, u32[]{:S(2)}) collective-permute-start(bf16[2,2,2,16,1024]{4,3,2,1,0:T(8,128)(2,1)S(1)} %add_convert_fusion.1), channel_id=1, source_target_pairs={{0,8},{1,5},{2,10},{3,7},{4,12},{5,1},{6,14},{7,3},{8,0},{9,13},{1... | collective-permute-start | bytes 786440 | tf_op jit(solution)/shard_map/ppermute | solution.py:28
  9.4 5.5 %collective-permute-start.7 = (bf16[2,2,2,16,1024]{4,3,2,1,0:T(8,128)(2,1)S(1)}, bf16[2,2,2,16,1024]{4,3,2,1,0:T(8,128)(2,1)S(1)}, u32[]{:S(2)}, u32[]{:S(2)}) collective-permute-start(bf16[2,2,2,16,1024]{4,3,2,1,0:T(8,128)(2,1)S(1)} %get-tuple-element.40), channel_id=1, source_target_pairs={{0,1},{1,0},{2,3},{3,2},{4,5},{5,4},{6,7},{7,6},{8,9},{9,8},{10,11... | collective-permute-start | bytes 786440 | tf_op jit(solution)/shard_map/ppermute | solution.py:28
  9.8 17.8 %collective-permute-start.13 = (f32[3,16,2048]{2,1,0:T(8,128)S(1)}, f32[3,16,2048]{2,1,0:T(8,128)S(1)}, u32[]{:S(2)}, u32[]{:S(2)}) collective-permute-start(f32[3,16,2048]{2,1,0:T(8,128)S(1)} %pad_maximum_fusion.refs_3_), channel_id=1, source_target_pairs={{0,2},{1,3},{2,0},{3,1},{4,6},{5,7},{6,4},{7,5},{8,10},{9,11},{10,... | collective-permute-start | bytes 1179656 | tf_op jit(solution)/shard_map/ppermute | solution.py:28
  11.8 5.5 %collective-permute-start.4 = (bf16[2,2,16,1024]{3,2,1,0:T(8,128)(2,1)S(1)}, bf16[2,2,16,1024]{3,2,1,0:T(8,128)(2,1)S(1)}, u32[]{:S(2)}, u32[]{:S(2)}) collective-permute-start(bf16[2,2,16,1024]{3,2,1,0:T(8,128)(2,1)S(1)} %fusion), channel_id=1, source_target_pairs={{0,4},{1,9},{2,6},{3,11},{4,0},{5,13},{6,2},{7,15},{8,12},{9,1},{1... | collective-permute-start | bytes 393224 | tf_op jit(solution)/shard_map/ppermute | solution.py:28
  15.0 5.2 %collective-permute-start.9 = (bf16[2,2,16,1024]{3,2,1,0:T(8,128)(2,1)S(1)}, bf16[2,2,16,1024]{3,2,1,0:T(8,128)(2,1)S(1)}, u32[]{:S(2)}, u32[]{:S(2)}) collective-permute-start(bf16[2,2,16,1024]{3,2,1,0:T(8,128)(2,1)S(1)} %fusion.1), channel_id=1, source_target_pairs={{0,4},{1,9},{2,6},{3,11},{4,0},{5,13},{6,2},{7,15},{8,12},{9,1},{1... | collective-permute-start | bytes 393224 | tf_op jit(solution)/shard_map/ppermute | solution.py:28
  17.3 6.1 %collective-permute-start.5 = (bf16[2,16,1024]{2,1,0:T(8,128)(2,1)S(1)}, bf16[2,16,1024]{2,1,0:T(8,128)(2,1)S(1)}, u32[]{:S(2)}, u32[]{:S(2)}) collective-permute-start(bf16[2,16,1024]{2,1,0:T(8,128)(2,1)S(1)} %fusion.4), channel_id=1, source_target_pairs={{0,16},{1,17},{2,18},{3,19},{4,20},{5,21},{6,22},{7,23},{8,24},{9,... | collective-permute-start | bytes 196616 | tf_op jit(solution)/shard_map/ppermute | solution.py:28
  20.3 5.4 %collective-permute-start.10 = (bf16[2,16,1024]{2,1,0:T(8,128)(2,1)S(1)}, bf16[2,16,1024]{2,1,0:T(8,128)(2,1)S(1)}, u32[]{:S(2)}, u32[]{:S(2)}) collective-permute-start(bf16[2,16,1024]{2,1,0:T(8,128)(2,1)S(1)} %fusion.5), channel_id=1, source_target_pairs={{0,16},{1,17},{2,18},{3,19},{4,20},{5,21},{6,22},{7,23},{8,24},{9,... | collective-permute-start | bytes 196616 | tf_op jit(solution)/shard_map/ppermute | solution.py:28
  23.4 4.9 %collective-permute-start.6 = (bf16[2,16,1024]{2,1,0:T(8,128)(2,1)S(1)}, bf16[2,16,1024]{2,1,0:T(8,128)(2,1)S(1)}, u32[]{:S(2)}, u32[]{:S(2)}) collective-permute-start(bf16[2,16,1024]{2,1,0:T(8,128)(2,1)S(1)} %fusion.3), channel_id=1, source_target_pairs={{0,2},{1,3},{2,0},{3,1},{4,6},{5,7},{6,4},{7,5},{8,10},{9,11},{10,... | collective-permute-start | bytes 196616 | tf_op jit(solution)/shard_map/ppermute | solution.py:28
  25.7 4.3 %collective-permute-start.11 = (bf16[2,16,1024]{2,1,0:T(8,128)(2,1)S(1)}, bf16[2,16,1024]{2,1,0:T(8,128)(2,1)S(1)}, u32[]{:S(2)}, u32[]{:S(2)}) collective-permute-start(bf16[2,16,1024]{2,1,0:T(8,128)(2,1)S(1)} %fusion.2), channel_id=1, source_target_pairs={{0,2},{1,3},{2,0},{3,1},{4,6},{5,7},{6,4},{7,5},{8,10},{9,11},{10,... | collective-permute-start | bytes 196616 | tf_op jit(solution)/shard_map/ppermute | solution.py:28
  27.6 2.6 %collective-permute-start.14 = (f32[3,16,2048]{2,1,0:T(8,128)S(1)}, f32[3,16,2048]{2,1,0:T(8,128)S(1)}, u32[]{:S(2)}, u32[]{:S(2)}) collective-permute-start(f32[3,16,2048]{2,1,0:T(8,128)S(1)} %pad_maximum_fusion.refs_3_), channel_id=1, source_target_pairs={{0,1},{1,0},{2,3},{3,2},{4,5},{5,4},{6,7},{7,6},{8,9},{9,8},{10,11... | collective-permute-start | bytes 1179656 | tf_op jit(solution)/shard_map/ppermute | solution.py:28
  27.6 2.6 %collective-permute-start.15 = (f32[3,16,2048]{2,1,0:T(8,128)S(1)}, f32[3,16,2048]{2,1,0:T(8,128)S(1)}, u32[]{:S(2)}, u32[]{:S(2)}) collective-permute-start(f32[3,16,2048]{2,1,0:T(8,128)S(1)} %collective-permute-done.13.refs_4_), channel_id=1, source_target_pairs={{0,1},{1,0},{2,3},{3,2},{4,5},{5,4},{6,7},{7,6},{8,9},{9,8},{10,11... | collective-permute-start | bytes 1179656 | tf_op jit(solution)/shard_map/ppermute | solution.py:28
  28.4 1.7 %collective-permute-start.12 = (bf16[2,16,1024]{2,1,0:T(8,128)(2,1)S(1)}, bf16[2,16,1024]{2,1,0:T(8,128)(2,1)S(1)}, u32[]{:S(2)}, u32[]{:S(2)}) collective-permute-start(bf16[2,16,1024]{2,1,0:T(8,128)(2,1)S(1)} %multiply_convert_fusion.1.refs_0_), channel_id=1, source_target_pairs={{0,1},{1,0},{2,3},{3,2},{4,5},{5,4},{6,7},{7,6},{8,9},{9,8},{10,11... | collective-permute-start | bytes 196616 | tf_op jit(solution)/shard_map/ppermute | solution.py:28
  30.0 1.3 %collective-permute-start.16 = (bf16[2,16,1024]{2,1,0:T(8,128)(2,1)S(1)}, bf16[2,16,1024]{2,1,0:T(8,128)(2,1)S(1)}, u32[]{:S(2)}, u32[]{:S(2)}) collective-permute-start(bf16[2,16,1024]{2,1,0:T(8,128)(2,1)S(1)} %multiply_convert_fusion.refs_1_), channel_id=1, source_target_pairs={{0,1},{1,0},{2,3},{3,2},{4,5},{5,4},{6,7},{7,6},{8,9},{9,8},{10,11... | collective-permute-start | bytes 196616 | tf_op jit(solution)/shard_map/ppermute | solution.py:28
